TPU v7x, 32 devices: a whole 2x2x4 slice. The times are simulated.
32 devices in a mesh: loop: 16 (over z, y, core), grp: 2 (over x).
Axes of the slice: x: 2, y: 2, z: 4, core: 2. Of those that a mesh axis runs over, the one named last changes fastest.
Arguments:
- jacobian: float32 [768, 16384], P('grp', 'loop'), may hold values from -0.21875 to 0.21875
Outputs:
- normal_matrix: float32 [16384, 16384], P(('loop', 'grp'))
All inputs are finite; a program needn't handle non-finite values.
Results may differ from a plain program's by a relative error of at most 0.00007.
Values sent between devices are 32-bit elements; how exact they have to be, the bound alone decides.
No kernel may reach another device: no remote copies, remote signals or barrier semaphores. Data moves between devices by JAX's collectives and lax.ppermute only.
A program may use at most 192 MiB of HBM per device.

v0:
```python
import jax
import jax.numpy as jnp
from jax import lax
from jax.sharding import PartitionSpec as P

damping = 0.1


def gram_block(left_block, right_block):
    return lax.dot_general(
        left_block,
        right_block,
        (((0,), (0,)), ((), ())),
        precision=lax.Precision.HIGHEST,
        preferred_element_type=jnp.float32,
    )


def per_device(jacobian):
    partial_value = gram_block(jacobian, lax.all_gather(jacobian, "loop", axis=1, tiled=True))
    gram_rows = lax.psum_scatter(partial_value, "grp", scatter_dimension=0, tiled=True)
    row_count = gram_rows.shape[0]
    row_start = (lax.axis_index("loop") * lax.axis_size("grp") + lax.axis_index("grp")) * row_count
    row_ids = row_start + jnp.arange(row_count, dtype=jnp.int32)[:, None]
    col_ids = jnp.arange(gram_rows.shape[1], dtype=jnp.int32)[None, :]
    factor = jnp.where(row_ids == col_ids, jnp.float32(1.0 + damping), jnp.float32(1.0))
    return gram_rows * factor


def solution(mesh):
    in_specs = (P("grp", "loop"),)
    out_specs = P(("loop", "grp"), None)
    return jax.shard_map(
        per_device, mesh=mesh, in_specs=in_specs, out_specs=out_specs, check_vma=False
    )
```

profile of v0, /device:TPU:0, one launch (start us, length us, event | category | flops | bytes accessed | tf_op | source)
XLA Modules:
  0.0 1010.9 jit_solution(5433368069422095771)
XLA Ops:
  6.5 0.0 all-gather.2.cloned.1.call-start
  6.5 0.7 all-gather.2.cloned.1.call-update
  7.3 0.0 reduce-scatter.2.cloned.1.call-start
  7.3 132.9 %all-gather.2.cloned.1.call-done = f32[384,16384]{1,0:T(8,128)} async-done(((f32[384,1024]{1,0:T(8,128)}), f32[384,16384]{1,0:T(8,128)}) %all-gather.2.cloned.1.call-update) | async-done | bytes 25165840 | tf_op jit(solution)/shard_map/all_gather | solution.py:20
  140.2 112.0 %fusion = f32[1024,16384]{1,0:T(8,128)} fusion(f32[384,1024]{1,0:T(8,128)} %param.1, f32[384,16384]{1,0:T(8,128)} %all-gather.2.cloned.1.call-done), kind=kOutput, calls=%fused_computation.3 | convolution fusion | flops 77309411328 | bytes 93847552 | tf_op jit(solution)/shard_map/dot_general | solution.py:10
  252.2 0.0 reduce-scatter.2.cloned.1.call-update
  252.2 728.5 %reduce-scatter.2.cloned.1.call-done = f32[512,16384]{1,0:T(8,128)} async-done(((f32[1024,16384]{1,0:T(8,128)}), f32[512,16384]{1,0:T(8,128)}) %reduce-scatter.2.cloned.1.call-update) | async-done | bytes 33554448 | tf_op jit(solution)/shard_map/reduce_scatter | solution.py:21
  980.8 23.3 %select_multiply_fusion = f32[512,16384]{1,0:T(8,128)} fusion(f32[512,16384]{1,0:T(8,128)} %reduce-scatter.2.cloned.1.call-done, s32[512]{0:T(512)S(1)} %iota_add_fusion), kind=kLoop, calls=%fused_computation | loop fusion | flops 25165824 | bytes 67110912 | tf_op jit(solution)/shard_map/mul | solution.py:27
  (1 shorter events, 0.0 us)
Async XLA Ops:
  6.5 133.7 %all-gather.2.cloned.1.call-start = ((), (), s32[]{:S(2)}) async-start(), calls=%async_computation.1 | async-start | bytes 26738688 | tf_op jit(solution)/shard_map/all_gather | solution.py:20
  7.3 973.5 %reduce-scatter.2.cloned.1.call-start = ((), (), s32[]{:S(2)}) async-start(), calls=%async_computation.2 | async-start | bytes 100663296 | tf_op jit(solution)/shard_map/reduce_scatter | solution.py:21
Sparse Core Ops, SparseCore 0:
  8.9 131.2 all-gather.1
  252.3 728.3 reduce-scatter.1
where the time goes:
time: 1010 us
  waiting for transfers between devices  862 us (85%)
  matrix products  112 us (11%)
  other arithmetic  23.3 us (2%)
  between operations  13.4 us (1%)
    reduce_scatter x1, waiting for transfers between devices, per_device(): lax.psum_scatter(partial_value, 'grp', scatter_dimension=0, tiled=True)  729 us
    all_gather x1, waiting for transfers between devices, per_device(): lax.all_gather(jacobian, 'loop', axis=1, tiled=True)  133 us
    dot_general x1, matrix products, gram_block(): lax.dot_general(left_block, right_block, (((0,), (0,)), ((), ())), precis...  112 us
    mul x1, other arithmetic, per_device(): return gram_rows * factor  23.3 us
  transfers between devices with their start and end apart: 2, of which 2 were waited for; matrix products, arithmetic and copies ran while one was open for 0% of the time, Pallas kernels for 0%

commit v1 on v0

v1 whole, which is shorter than its diff:
```python
import functools

import jax
import jax.numpy as jnp
from jax import lax
from jax.experimental import pallas as pl
from jax.experimental.pallas import tpu as pltpu
from jax.sharding import PartitionSpec as P

damping = 0.1
PASSES = 3
VMEM_BYTES = 40 * 1024 * 1024


def split_high_low(value):
    high = value.astype(jnp.bfloat16)
    low = (value - high.astype(jnp.float32)).astype(jnp.bfloat16)
    return high, low


def left_kernel(first_ref, second_ref, left_ref):
    depth = first_ref.shape[0]
    for place, ref in enumerate((first_ref, second_ref)):
        high, low = split_high_low(ref[...].T)
        for part, piece in enumerate((high, high, low)):
            left_ref[:, pl.ds(2 * depth * part + depth * place, depth)] = piece


def left_operand(first, second):
    depth, rows = first.shape
    return pl.pallas_call(
        left_kernel,
        out_shape=jax.ShapeDtypeStruct((rows, 2 * PASSES * depth), jnp.bfloat16),
        compiler_params=pltpu.CompilerParams(vmem_limit_bytes=VMEM_BYTES),
        name="left_operand",
    )(first, second)


def panel_kernel(sizes, tiles, diagonal, ids_ref, *refs):
    left_ref, out_ref, right_ref = refs[0], refs[-2], refs[-1]
    blocks = refs[1 : 1 + sum(map(sum, sizes))]
    step = pl.program_id(0)
    at = 0
    for index, counts in enumerate(sizes):
        groups = []
        for count in counts:
            groups.append(blocks[at : at + count])
            at += count

        @pl.when(step // tiles == index)
        def fill(groups=groups):
            depth = groups[0][0].shape[0]
            for place, group in enumerate(groups):
                value = functools.reduce(jnp.add, [ref[...] for ref in group])
                high, low = split_high_low(value)
                for part, piece in enumerate((high, low, high)):
                    right_ref[pl.ds(2 * depth * part + depth * place, depth), :] = piece

    product = jnp.dot(left_ref[...], right_ref[...], preferred_element_type=jnp.float32)
    if diagonal:
        width = product.shape[1]
        row_ids = lax.broadcasted_iota(jnp.int32, product.shape, 0) + ids_ref[len(sizes)]
        col_ids = lax.broadcasted_iota(jnp.int32, product.shape, 1) + (step % tiles) * width
        hit = (row_ids == col_ids) & (ids_ref[len(sizes) + 1 + step // tiles] == 1)
        product = jnp.where(hit, product * jnp.float32(1.0 + damping), product)
    out_ref[...] = product


def panels(out, left, columns, pairs, ids, diagonal=False):
    rows = left.shape[0]
    depth, width = pairs[0][0][0].shape
    tile = min(width, 512)
    tiles = width // tile
    sizes = tuple(tuple(len(half) for half in pair) for pair in pairs)
    operands, specs = [], []
    for index, pair in enumerate(pairs):
        for half in pair:
            for array in half:
                operands.append(array)
                specs.append(
                    pl.BlockSpec(
                        (depth, tile),
                        lambda t, ids, index=index: (0, jnp.clip(t - index * tiles, 0, tiles - 1)),
                    )
                )
    steps = len(pairs) * tiles
    in_specs = [pl.BlockSpec(left.shape, lambda t, ids: (0, 0))] + specs
    args = [ids, left] + operands
    aliases = {}
    if out is not None:
        aliases = {len(args): 0}
        args.append(out)
        in_specs.append(pl.BlockSpec(memory_space=pl.ANY))
    body = functools.partial(panel_kernel, sizes, tiles, diagonal)
    return pl.pallas_call(
        body,
        out_shape=jax.ShapeDtypeStruct((rows, columns), jnp.float32),
        grid_spec=pltpu.PrefetchScalarGridSpec(
            num_scalar_prefetch=1,
            grid=(steps,),
            in_specs=in_specs,
            out_specs=pl.BlockSpec((rows, tile), lambda t, ids: (0, ids[t // tiles] * tiles + t % tiles)),
            scratch_shapes=[pltpu.VMEM((left.shape[1], tile), jnp.bfloat16)],
        ),
        input_output_aliases=aliases,
        compiler_params=pltpu.CompilerParams(
            vmem_limit_bytes=VMEM_BYTES, dimension_semantics=("arbitrary",)
        ),
        cost_estimate=pl.CostEstimate(
            flops=2 * rows * left.shape[1] * width * len(pairs),
            bytes_accessed=4 * width * len(pairs) * (rows + 2 * depth),
            transcendentals=0,
        ),
        name="panels",
    )(*args)


def gathered(loop, grp, jacobian):
    rows_here = jacobian.shape[1] // grp
    me, side = lax.axis_index("loop"), lax.axis_index("grp")
    both = lax.all_gather(jacobian, "grp")
    everything = lax.all_gather(both, "loop")
    mine = lax.dynamic_slice_in_dim(both, side * rows_here, rows_here, axis=2)
    left = left_operand(mine[0], mine[1])
    out = None
    for panel in range(loop):
        ids = jnp.stack(
            [jnp.int32(panel), side * rows_here, (me == panel).astype(jnp.int32)]
        ).astype(jnp.int32)
        pair = ((everything[panel, 0],), (everything[panel, 1],))
        out = panels(out, left, jacobian.shape[1] * loop, [pair], ids, diagonal=True)
    return out


def rounds(loop, grp, jacobian):
    rows_here = jacobian.shape[1] // grp
    columns = jacobian.shape[1] * loop
    me, side = lax.axis_index("loop"), lax.axis_index("grp")
    z, y, core = me // 4, (me // 2) % 2, me % 2

    along_x = lambda v: lax.ppermute(v, "grp", [(0, 1), (1, 0)])
    along_y = lambda v: lax.ppermute(v, "loop", [(i, i ^ 2) for i in range(16)])
    pair_z = lambda v: lax.ppermute(v, "loop", [(i, i ^ 4) for i in range(16)])
    mid_z = lambda v: lax.ppermute(
        v, "loop", [(i, i + 4) for i in range(4, 8)] + [(i + 4, i) for i in range(4, 8)]
    )
    swap = lambda v: lax.ppermute(v, "loop", [(i, i ^ 1) for i in range(16)])

    c_self = jacobian
    x_self, y_self, c_mate, mid0 = along_x(c_self), along_y(c_self), pair_z(c_self), mid_z(c_self)

    d_self, y_mate, pair1, mid1 = along_x(y_self), along_y(c_mate), pair_z(mid0), mid_z(c_mate)
    c_near = pair1 + mid0

    x_near, y_near, d_mate = along_x(c_near), along_y(c_near), pair_z(d_self)

    x_mate, d_near, pair3, mid3 = along_x(c_mate), along_y(x_near), pair_z(mid1), mid_z(d_mate)
    c_far = pair3 + mid1

    x_far, y_far, pair4 = along_x(c_far), along_y(c_far), pair_z(mid3)

    mate_z = z ^ 1
    near_z = jnp.where(z < 2, 2, 1)
    far_z = jnp.where(z < 2, 3, 0)

    def ids_of(zz, yy, *more):
        base = zz * 4 + yy * 2
        return jnp.stack([base + core, base + 1 - core, *more]).astype(jnp.int32)

    def both(first, second):
        other = lambda half: tuple(swap(v) for v in half)
        return [(first, second), (other(first), other(second))]

    mine = lambda v: lax.dynamic_slice_in_dim(v, side * rows_here, rows_here, axis=1)
    left = left_operand(mine(c_self), mine(x_self))
    one, zero = jnp.int32(1), jnp.int32(0)
    ids = ids_of(z, y, side * rows_here, one, zero)
    out = panels(None, left, columns, both((c_self,), (x_self,)), ids, diagonal=True)
    out = panels(out, left, columns, both((y_self,), (d_self,)), ids_of(z, 1 - y))
    out = panels(out, left, columns, both((c_near,), (x_near,)), ids_of(near_z, y))
    out = panels(out, left, columns, both((y_mate,), (d_mate,)), ids_of(mate_z, 1 - y))
    out = panels(out, left, columns, both((c_mate,), (x_mate,)), ids_of(mate_z, y))
    out = panels(out, left, columns, both((y_near,), (d_near,)), ids_of(near_z, 1 - y))
    out = panels(out, left, columns, both((c_far,), (x_far,)), ids_of(far_z, y))
    out = panels(out, left, columns, both((y_far,), (pair4, mid3)), ids_of(far_z, 1 - y))
    return out


def solution(mesh):
    loop, grp = mesh.shape["loop"], mesh.shape["grp"]
    plan = rounds if (loop, grp) == (16, 2) else gathered
    return jax.shard_map(
        functools.partial(plan, loop, grp),
        mesh=mesh,
        in_specs=(P("grp", "loop"),),
        out_specs=P(("loop", "grp"), None),
        check_vma=False,
    )
```

time: 1010 us -> 309 us (0.31)
  waiting for transfers between devices: 862 us -> 171 us
  matrix products: 112 us -> 0 us
  Pallas kernels: 0 us -> 77 us
  starting transfers between devices: 0.04 us -> 39.3 us
  other arithmetic: 23.3 us -> 3.13 us
  local copies, waits for them, and re-layouts: 0 us -> 18.1 us
  between operations: 13.4 us -> 0.24 us
    reduce_scatter x1 -> x0, waiting for transfers between devices: 729 us -> none  [per_device(): lax.psum_scatter(partial_value, 'grp', scatter_dimension=0, tiled=True)]
    ppermute x0 -> x35, waiting for transfers between devices: none -> 171 us  [the longest x5 82 us: rounds(): along_x = lambda v: lax.ppermute(v, 'grp', [(0, 1), (1, 0)])]
    all_gather x1 -> x0, waiting for transfers between devices: 133 us -> none  [per_device(): lax.all_gather(jacobian, 'loop', axis=1, tiled=True)]
    dot_general x1 -> x0, matrix products: 112 us -> none  [gram_block(): lax.dot_general(left_block, right_block, (((0,), (0,)), ((), ())), precis...]
    pallas_call x0 -> x9, Pallas kernels: none -> 77 us  [the longest x8 76.5 us: panels(): pl.pallas_call(body, out_shape=jax.ShapeDtypeStruct((rows, columns), jnp....]
    ppermute x0 -> x35, starting transfers between devices: none -> 39.3 us  [the longest x5 19.7 us: rounds(): pair_z = lambda v: lax.ppermute(v, 'loop', [(i, i ^ 4) for i in range(16)])]
    mul x1 -> x0, other arithmetic: 23.3 us -> none  [per_device(): return gram_rows * factor]
    unnamed x0 -> x58, local copies, waits for them, and re-layouts: none -> 17.9 us
  transfers between devices with their start and end apart: 2 -> 35, of which waited for: 2 -> 9; matrix products, arithmetic and copies ran while one was open for 0% -> 1% of each run, Pallas kernels for 0% -> 21%
where the time goes in v1:
time: 309 us
  waiting for transfers between devices  171 us (55%)
  Pallas kernels  77 us (25%)
  starting transfers between devices  39.3 us (13%)
  local copies, waits for them, and re-layouts  18.1 us (6%)
  other arithmetic  3.13 us (1%)
    ppermute x5, waiting for transfers between devices, rounds(): along_x = lambda v: lax.ppermute(v, 'grp', [(0, 1), (1, 0)])  82 us
    pallas_call x8, Pallas kernels, panels(): pl.pallas_call(body, out_shape=jax.ShapeDtypeStruct((rows, columns), jnp....  76.5 us
    ppermute x5, waiting for transfers between devices, rounds(): pair_z = lambda v: lax.ppermute(v, 'loop', [(i, i ^ 4) for i in range(16)])  64.1 us
    ppermute x5, waiting for transfers between devices, rounds(): along_y = lambda v: lax.ppermute(v, 'loop', [(i, i ^ 2) for i in range(16)])  25 us
    ppermute x5, starting transfers between devices, rounds(): pair_z = lambda v: lax.ppermute(v, 'loop', [(i, i ^ 4) for i in range(16)])  19.7 us
    unnamed x58, local copies, waits for them, and re-layouts  17.9 us
    ppermute x5, starting transfers between devices, rounds(): along_y = lambda v: lax.ppermute(v, 'loop', [(i, i ^ 2) for i in range(16)])  7.73 us
    ppermute x5, starting transfers between devices, rounds(): along_x = lambda v: lax.ppermute(v, 'grp', [(0, 1), (1, 0)])  6.28 us
  transfers between devices with their start and end apart: 35, of which 9 were waited for; matrix products, arithmetic and copies ran while one was open for 1% of the time, Pallas kernels for 21%

profile of v1, /device:TPU:0, one launch (start us, length us, event | category | flops | bytes accessed | tf_op | source)
XLA Modules:
  0.0 308.9 jit_solution(10557118632637528043)
XLA Ops:
  0.0 2.9 collective-permute-start
  2.9 0.7 collective-permute-start.16
  3.7 1.6 collective-permute-start.5
  5.3 4.3 %collective-permute-start.1 = (f32[384,1024]{1,0:T(8,128)}, f32[384,1024]{1,0:T(8,128)S(1)}, u32[]{:S(2)}, u32[]{:S(2)}) collective-permute-start(f32[384,1024]{1,0:T(8,128)} %refs_1_.1), channel_id=1, source_target_pairs={{0,8},{2,10},{4,12},{6,14},{8,0},{10,2},{12,4},{14,6},{16,24},{18,... | collective-permute-start | bytes 4718600 | tf_op jit(solution)/shard_map/ppermute | solution.py:143
  9.6 28.0 %collective-permute-done.refs_2_ = f32[384,1024]{1,0:T(8,128)S(1)} collective-permute-done((f32[384,1024]{1,0:T(8,128)}, f32[384,1024]{1,0:T(8,128)S(1)}, u32[]{:S(2)}, u32[]{:S(2)}) %collective-permute-start) | collective-permute-done | bytes 1572896 | tf_op jit(solution)/shard_map/ppermute | solution.py:141
  37.5 4.9 %collective-permute-start.17 = (f32[384,1024]{1,0:T(8,128)S(1)}, f32[384,1024]{1,0:T(8,128)S(1)}, u32[]{:S(2)}, u32[]{:S(2)}) collective-permute-start(f32[384,1024]{1,0:T(8,128)S(1)} %collective-permute-done.16), channel_id=1, source_target_pairs={{0,8},{2,10},{4,12},{6,14},{8,0},{10,2},{12,4},{14,6},{16,24},{18,... | collective-permute-start | bytes 4718600 | tf_op jit(solution)/shard_map/ppermute | solution.py:143
  43.0 1.1 copy-done.1
  44.2 1.2 copy-done.13
  45.3 1.5 collective-permute-start.26
  46.8 1.1 copy-done.3
  48.0 1.5 collective-permute-start.23
  49.5 29.1 %collective-permute-done.17 = f32[384,1024]{1,0:T(8,128)S(1)} collective-permute-done((f32[384,1024]{1,0:T(8,128)S(1)}, f32[384,1024]{1,0:T(8,128)S(1)}, u32[]{:S(2)}, u32[]{:S(2)}) %collective-permute-start.17) | collective-permute-done | bytes 1572896 | tf_op jit(solution)/shard_map/ppermute | solution.py:143
  78.8 1.0 collective-permute-done.6.refs_2_
  79.8 0.8 collective-permute-start.2
  80.6 1.2 copy-done.5
  81.7 1.1 copy-done.17
  83.6 29.9 %collective-permute-done.23.refs_2_ = f32[384,1024]{1,0:T(8,128)S(1)} collective-permute-done((f32[384,1024]{1,0:T(8,128)S(1)}, f32[384,1024]{1,0:T(8,128)S(1)}, u32[]{:S(2)}, u32[]{:S(2)}) %collective-permute-start.23) | collective-permute-done | bytes 1572896 | tf_op jit(solution)/shard_map/ppermute | solution.py:141
  113.5 1.1 copy-done.11
  114.7 1.4 collective-permute-start.7
  116.0 1.2 copy-done.15
  117.4 1.3 copy-done.9
  118.8 1.1 copy-done.25
  120.3 1.2 copy-done.7
  121.5 23.2 %collective-permute-done.19.refs_2_ = f32[384,1024]{1,0:T(8,128)} collective-permute-done((f32[384,1024]{1,0:T(8,128)S(1)}, f32[384,1024]{1,0:T(8,128)}, u32[]{:S(2)}, u32[]{:S(2)}) %collective-permute-start.19) | collective-permute-done | bytes 1572896 | tf_op jit(solution)/shard_map/ppermute | solution.py:141
  144.7 1.4 collective-permute-start.3
  146.0 1.1 copy-done.23
  147.2 1.5 collective-permute-start.18
  148.7 3.3 %collective-permute-done.7.refs_2_ = f32[384,1024]{1,0:T(8,128)} collective-permute-done((f32[384,1024]{1,0:T(8,128)S(1)}, f32[384,1024]{1,0:T(8,128)}, u32[]{:S(2)}, u32[]{:S(2)}) %collective-permute-start.7) | collective-permute-done | bytes 1572896 | tf_op jit(solution)/shard_map/ppermute | solution.py:143
  152.0 1.2 copy-done.21
  153.7 1.2 copy-done.19
  154.9 1.5 collective-permute-start.20
  156.4 28.8 %collective-permute-done.3 = f32[384,1024]{1,0:T(8,128)S(1)} collective-permute-done((f32[384,1024]{1,0:T(8,128)S(1)}, f32[384,1024]{1,0:T(8,128)S(1)}, u32[]{:S(2)}, u32[]{:S(2)}) %collective-permute-start.3) | collective-permute-done | bytes 1572896 | tf_op jit(solution)/shard_map/ppermute | solution.py:143
  185.2 1.1 copy-done.28
  186.3 1.8 collective-permute-start.8
  188.5 2.4 add.97.refs_1_
  191.8 1.6 collective-permute-start.4
  193.3 25.0 %collective-permute-done.20.refs_2_ = f32[384,1024]{1,0:T(8,128)} collective-permute-done((f32[384,1024]{1,0:T(8,128)}, f32[384,1024]{1,0:T(8,128)}, u32[]{:S(2)}, u32[]{:S(2)}) %collective-permute-start.20) | collective-permute-done | bytes 1572896 | tf_op jit(solution)/shard_map/ppermute | solution.py:142
  218.3 7.7 %collective-permute-start.9 = (f32[384,1024]{1,0:T(8,128)}, f32[384,1024]{1,0:T(8,128)}, u32[]{:S(2)}, u32[]{:S(2)}) collective-permute-start(f32[384,1024]{1,0:T(8,128)} %collective-permute-done.8.refs_3_), channel_id=1, source_target_pairs={{0,8},{2,10},{4,12},{6,14},{8,0},{10,2},{12,4},{14,6},{16,24},{18,... | collective-permute-start | bytes 4718600 | tf_op jit(solution)/shard_map/ppermute | solution.py:143
  226.7 0.9 copy-done.2
  228.1 9.0 %panels.8.refs_5_ = f32[512,16384]{1,0:T(8,128)} custom-call(s32[5]{0:T(128)S(1)} %stack.99.ids_ref, bf16[512,2304]{1,0:T(8,128)(2,1)S(1)} %left_operand.1.refs_0_, f32[384,1024]{1,0:T(8,128)S(1)} %copy-done, f32[384,1024]{1,0:T(8,128)S(1)} %collective-permute-done.refs_2_, f32[384,1024]{1,0:T(8,128)S(1)} %copy-done.2, f32[384,1024]{1,0:T(8,128)S(1)} %copy-done.4), custom_call_target="tpu_custom_call" | custom-call | flops 4831838208 | bytes 10485760 | tf_op jit(solution)/shard_map/panels/pallas_call | solution.py:95
  237.1 8.8 %panels.9.refs_5_ = f32[512,16384]{1,0:T(8,128)} custom-call(s32[2]{0:T(128)S(1)} %pad_add_fusion.6.ids_ref, bf16[512,2304]{1,0:T(8,128)(2,1)S(1)} %left_operand.1.refs_0_, f32[384,1024]{1,0:T(8,128)S(1)} %copy-done.14, f32[384,1024]{1,0:T(8,128)S(1)} %copy-done.16, f32[384,1024]{1,0:T(8,128)S(1)} %copy-done.18, ...), custom_call_target="tpu_custom_call", output_to_operand_aliasing={{}: (6, {})} | custom-call | flops 4831838208 | bytes 10485760 | tf_op jit(solution)/shard_map/panels/pallas_call | solution.py:95
  246.4 9.8 %panels.10.refs_5_ = f32[512,16384]{1,0:T(8,128)} custom-call(s32[2]{0:T(128)S(1)} %pad_add_fusion.5.ids_ref, bf16[512,2304]{1,0:T(8,128)(2,1)S(1)} %left_operand.1.refs_0_, f32[384,1024]{1,0:T(8,128)S(1)} %add.104.refs_1_, f32[384,1024]{1,0:T(8,128)} %collective-permute-done.19.refs_2_, f32[384,1024]{1,0:T(8,128)S(1)} %copy-done.24, ...), custom_call_target="tpu_custom_call", output_to_operand_aliasing={{}: (6, {})} | custom-call | flops 4831838208 | bytes 10485760 | tf_op jit(solution)/shard_map/panels/pallas_call | solution.py:95
  256.8 3.0 collective-permute-done.9.refs_2_
  259.9 9.8 %panels.11.refs_5_ = f32[512,16384]{1,0:T(8,128)} custom-call(s32[2]{0:T(128)S(1)} %pad_add_fusion.4.ids_ref, bf16[512,2304]{1,0:T(8,128)(2,1)S(1)} %left_operand.1.refs_0_, f32[384,1024]{1,0:T(8,128)S(1)} %copy-done.10, f32[384,1024]{1,0:T(8,128)} %collective-permute-done.7.refs_2_, f32[384,1024]{1,0:T(8,128)S(1)} %copy-done.22, ...), custom_call_target="tpu_custom_call", output_to_operand_aliasing={{}: (6, {})} | custom-call | flops 4831838208 | bytes 10485760 | tf_op jit(solution)/shard_map/panels/pallas_call | solution.py:95
  269.7 8.8 %panels.12.refs_5_ = f32[512,16384]{1,0:T(8,128)} custom-call(s32[2]{0:T(128)S(1)} %pad_add_fusion.3.ids_ref, bf16[512,2304]{1,0:T(8,128)(2,1)S(1)} %left_operand.1.refs_0_, f32[384,1024]{1,0:T(8,128)S(1)} %copy-done.6, f32[384,1024]{1,0:T(8,128)S(1)} %copy-done.8, f32[384,1024]{1,0:T(8,128)S(1)} %copy-done.12, ...), custom_call_target="tpu_custom_call", output_to_operand_aliasing={{}: (6, {})} | custom-call | flops 4831838208 | bytes 10485760 | tf_op jit(solution)/shard_map/panels/pallas_call | solution.py:95
  278.4 10.0 %panels.13.refs_5_ = f32[512,16384]{1,0:T(8,128)} custom-call(s32[2]{0:T(128)S(1)} %pad_add_fusion.2.ids_ref, bf16[512,2304]{1,0:T(8,128)(2,1)S(1)} %left_operand.1.refs_0_, f32[384,1024]{1,0:T(8,128)} %collective-permute-done.18.refs_1_, f32[384,1024]{1,0:T(8,128)} %collective-permute-done.20.refs_2_, ...), custom_call_target="tpu_custom_call", output_to_operand_aliasing={{}: (6, {})} | custom-call | flops 4831838208 | bytes 10485760 | tf_op jit(solution)/shard_map/panels/pallas_call | solution.py:95
  288.4 9.6 %panels.14.refs_7_ = f32[512,16384]{1,0:T(8,128)} custom-call(s32[2]{0:T(128)S(1)} %pad_add_fusion.1.ids_ref, bf16[512,2304]{1,0:T(8,128)(2,1)S(1)} %left_operand.1.refs_0_, f32[384,1024]{1,0:T(8,128)S(1)} %add.97.refs_1_, f32[384,1024]{1,0:T(8,128)S(1)} %collective-permute-done.13.refs_2_, ...), custom_call_target="tpu_custom_call", output_to_operand_aliasing={{}: (6, {})} | custom-call | flops 4831838208 | bytes 10485760 | tf_op jit(solution)/shard_map/panels/pallas_call | solution.py:95
  298.1 10.8 %panels.15 = f32[512,16384]{1,0:T(8,128)} custom-call(s32[2]{0:T(128)S(1)} %pad_add_fusion.ids_ref, bf16[512,2304]{1,0:T(8,128)(2,1)S(1)} %left_operand.1.refs_0_, f32[384,1024]{1,0:T(8,128)S(1)} %collective-permute-done.4.refs_1_, f32[384,1024]{1,0:T(8,128)} %collective-permute-done.9.refs_2_, ...), custom_call_target="tpu_custom_call", output_to_operand_aliasing={{}: (8, {})} | custom-call | flops 4831838208 | bytes 10485760 | tf_op jit(solution)/shard_map/panels/pallas_call | solution.py:95
  (101 shorter events, 6.2 us)
Async XLA Ops:
  0.0 37.5 %collective-permute-start = (f32[384,1024]{1,0:T(8,128)}, f32[384,1024]{1,0:T(8,128)S(1)}, u32[]{:S(2)}, u32[]{:S(2)}) collective-permute-start(f32[384,1024]{1,0:T(8,128)} %refs_1_.1), channel_id=1, source_target_pairs={{0,1},{1,0},{2,3},{3,2},{4,5},{5,4},{6,7},{7,6},{8,9},{9,8},{10,11... | collective-permute-start | bytes 4718600 | tf_op jit(solution)/shard_map/ppermute | solution.py:141
  2.9 34.6 %collective-permute-start.16 = (f32[384,1024]{1,0:T(8,128)}, f32[384,1024]{1,0:T(8,128)S(1)}, u32[]{:S(2)}, u32[]{:S(2)}) collective-permute-start(f32[384,1024]{1,0:T(8,128)} %refs_1_.1), channel_id=1, source_target_pairs={{8,16},{10,18},{12,20},{14,22},{16,8},{18,10},{20,12},{22,14},{9,1... | collective-permute-start | bytes 4718600 | tf_op jit(solution)/shard_map/ppermute | solution.py:144
  3.7 38.8 %collective-permute-start.5 = (f32[384,1024]{1,0:T(8,128)}, f32[384,1024]{1,0:T(8,128)S(1)}, u32[]{:S(2)}, u32[]{:S(2)}) collective-permute-start(f32[384,1024]{1,0:T(8,128)} %refs_1_.1), channel_id=1, source_target_pairs={{0,4},{2,6},{4,0},{6,2},{8,12},{10,14},{12,8},{14,10},{16,20},{18,... | collective-permute-start | bytes 4718600 | tf_op jit(solution)/shard_map/ppermute | solution.py:142
  5.3 37.7 %collective-permute-start.33 = (f32[384,1024]{1,0:T(8,128)}, f32[384,1024]{1,0:T(8,128)S(1)}, u32[]{:S(2)}, u32[]{:S(2)}) collective-permute-start(f32[384,1024]{1,0:T(8,128)} %refs_1_.1), channel_id=1, source_target_pairs={{0,2},{2,0},{4,6},{6,4},{8,10},{10,8},{12,14},{14,12},{16,18},{18,... | collective-permute-start | bytes 4718600 | tf_op jit(solution)/shard_map/ppermute | solution.py:147
  5.3 40.0 %collective-permute-start.1 = (f32[384,1024]{1,0:T(8,128)}, f32[384,1024]{1,0:T(8,128)S(1)}, u32[]{:S(2)}, u32[]{:S(2)}) collective-permute-start(f32[384,1024]{1,0:T(8,128)} %refs_1_.1), channel_id=1, source_target_pairs={{0,8},{2,10},{4,12},{6,14},{8,0},{10,2},{12,4},{14,6},{16,24},{18,... | collective-permute-start | bytes 4718600 | tf_op jit(solution)/shard_map/ppermute | solution.py:143
  37.5 9.3 %collective-permute-start.34 = (f32[384,1024]{1,0:T(8,128)S(1)}, f32[384,1024]{1,0:T(8,128)S(1)}, u32[]{:S(2)}, u32[]{:S(2)}) collective-permute-start(f32[384,1024]{1,0:T(8,128)S(1)} %collective-permute-done.refs_2_), channel_id=1, source_target_pairs={{0,2},{2,0},{4,6},{6,4},{8,10},{10,8},{12,14},{14,12},{16,18},{18,... | collective-permute-start | bytes 4718600 | tf_op jit(solution)/shard_map/ppermute | solution.py:147
  37.5 41.0 %collective-permute-start.17 = (f32[384,1024]{1,0:T(8,128)S(1)}, f32[384,1024]{1,0:T(8,128)S(1)}, u32[]{:S(2)}, u32[]{:S(2)}) collective-permute-start(f32[384,1024]{1,0:T(8,128)S(1)} %collective-permute-done.16), channel_id=1, source_target_pairs={{0,8},{2,10},{4,12},{6,14},{8,0},{10,2},{12,4},{14,6},{16,24},{18,... | collective-permute-start | bytes 4718600 | tf_op jit(solution)/shard_map/ppermute | solution.py:143
  42.5 37.3 %collective-permute-start.6 = (f32[384,1024]{1,0:T(8,128)S(1)}, f32[384,1024]{1,0:T(8,128)S(1)}, u32[]{:S(2)}, u32[]{:S(2)}) collective-permute-start(f32[384,1024]{1,0:T(8,128)S(1)} %collective-permute-done.5.refs_1_), channel_id=1, source_target_pairs={{0,1},{1,0},{2,3},{3,2},{4,5},{5,4},{6,7},{7,6},{8,9},{9,8},{10,11... | collective-permute-start | bytes 4718600 | tf_op jit(solution)/shard_map/ppermute | solution.py:141
  44.1 37.6 %collective-permute-start.31 = (f32[384,1024]{1,0:T(8,128)S(1)}, f32[384,1024]{1,0:T(8,128)S(1)}, u32[]{:S(2)}, u32[]{:S(2)}) collective-permute-start(f32[384,1024]{1,0:T(8,128)S(1)} %collective-permute-done.5.refs_1_), channel_id=1, source_target_pairs={{0,2},{2,0},{4,6},{6,4},{8,10},{10,8},{12,14},{14,12},{16,18},{18,... | collective-permute-start | bytes 4718600 | tf_op jit(solution)/shard_map/ppermute | solution.py:147
  45.3 37.6 %collective-permute-start.26 = (f32[384,1024]{1,0:T(8,128)S(1)}, f32[384,1024]{1,0:T(8,128)S(1)}, u32[]{:S(2)}, u32[]{:S(2)}) collective-permute-start(f32[384,1024]{1,0:T(8,128)S(1)} %collective-permute-done.1.refs_1_), channel_id=1, source_target_pairs={{0,4},{2,6},{4,0},{6,2},{8,12},{10,14},{12,8},{14,10},{16,20},{18,... | collective-permute-start | bytes 4718600 | tf_op jit(solution)/shard_map/ppermute | solution.py:142
  48.0 65.5 %collective-permute-start.23 = (f32[384,1024]{1,0:T(8,128)S(1)}, f32[384,1024]{1,0:T(8,128)S(1)}, u32[]{:S(2)}, u32[]{:S(2)}) collective-permute-start(f32[384,1024]{1,0:T(8,128)S(1)} %collective-permute-done.1.refs_1_), channel_id=1, source_target_pairs={{0,1},{1,0},{2,3},{3,2},{4,5},{5,4},{6,7},{7,6},{8,9},{9,8},{10,11... | collective-permute-start | bytes 4718600 | tf_op jit(solution)/shard_map/ppermute | solution.py:141
  78.6 34.9 %collective-permute-start.24 = (f32[384,1024]{1,0:T(8,128)S(1)}, f32[384,1024]{1,0:T(8,128)S(1)}, u32[]{:S(2)}, u32[]{:S(2)}) collective-permute-start(f32[384,1024]{1,0:T(8,128)S(1)} %collective-permute-done.1.refs_1_), channel_id=1, source_target_pairs={{0,2},{2,0},{4,6},{6,4},{8,10},{10,8},{12,14},{14,12},{16,18},{18,... | collective-permute-start | bytes 4718600 | tf_op jit(solution)/shard_map/ppermute | solution.py:147
  79.8 37.4 %collective-permute-start.2 = (f32[384,1024]{1,0:T(8,128)S(1)}, f32[384,1024]{1,0:T(8,128)S(1)}, u32[]{:S(2)}, u32[]{:S(2)}) collective-permute-start(f32[384,1024]{1,0:T(8,128)S(1)} %collective-permute-done.1.refs_1_), channel_id=1, source_target_pairs={{8,16},{10,18},{12,20},{14,22},{16,8},{18,10},{20,12},{22,14},{9,1... | collective-permute-start | bytes 4718600 | tf_op jit(solution)/shard_map/ppermute | solution.py:144
  82.9 35.9 %collective-permute-start.32 = (f32[384,1024]{1,0:T(8,128)S(1)}, f32[384,1024]{1,0:T(8,128)S(1)}, u32[]{:S(2)}, u32[]{:S(2)}) collective-permute-start(f32[384,1024]{1,0:T(8,128)S(1)} %collective-permute-done.6.refs_2_), channel_id=1, source_target_pairs={{0,2},{2,0},{4,6},{6,4},{8,10},{10,8},{12,14},{14,12},{16,18},{18,... | collective-permute-start | bytes 4718600 | tf_op jit(solution)/shard_map/ppermute | solution.py:147
  82.9 61.8 %collective-permute-start.19 = (f32[384,1024]{1,0:T(8,128)S(1)}, f32[384,1024]{1,0:T(8,128)}, u32[]{:S(2)}, u32[]{:S(2)}) collective-permute-start(f32[384,1024]{1,0:T(8,128)S(1)} %add.104.refs_1_), channel_id=1, source_target_pairs={{0,1},{1,0},{2,3},{3,2},{4,5},{5,4},{6,7},{7,6},{8,9},{9,8},{10,11... | collective-permute-start | bytes 4718600 | tf_op jit(solution)/shard_map/ppermute | solution.py:141
  113.5 32.5 %collective-permute-start.29 = (f32[384,1024]{1,0:T(8,128)S(1)}, f32[384,1024]{1,0:T(8,128)S(1)}, u32[]{:S(2)}, u32[]{:S(2)}) collective-permute-start(f32[384,1024]{1,0:T(8,128)S(1)} %add.104.refs_1_), channel_id=1, source_target_pairs={{0,2},{2,0},{4,6},{6,4},{8,10},{10,8},{12,14},{14,12},{16,18},{18,... | collective-permute-start | bytes 4718600 | tf_op jit(solution)/shard_map/ppermute | solution.py:147
  114.7 37.3 %collective-permute-start.7 = (f32[384,1024]{1,0:T(8,128)S(1)}, f32[384,1024]{1,0:T(8,128)}, u32[]{:S(2)}, u32[]{:S(2)}) collective-permute-start(f32[384,1024]{1,0:T(8,128)S(1)} %collective-permute-done.6.refs_2_), channel_id=1, source_target_pairs={{0,8},{2,10},{4,12},{6,14},{8,0},{10,2},{12,4},{14,6},{16,24},{18,... | collective-permute-start | bytes 4718600 | tf_op jit(solution)/shard_map/ppermute | solution.py:143
  117.2 36.5 %copy-start.27 = (f32[384,1024]{1,0:T(8,128)}, f32[384,1024]{1,0:T(8,128)S(1)}, u32[]{:S(2)}) copy-start(f32[384,1024]{1,0:T(8,128)S(1)} %collective-permute-done.2) | copy-start | bytes 4718596
  117.2 34.7 %collective-permute-start.27 = (f32[384,1024]{1,0:T(8,128)S(1)}, f32[384,1024]{1,0:T(8,128)S(1)}, u32[]{:S(2)}, u32[]{:S(2)}) collective-permute-start(f32[384,1024]{1,0:T(8,128)S(1)} %collective-permute-done.26.refs_1_), channel_id=1, source_target_pairs={{0,2},{2,0},{4,6},{6,4},{8,10},{10,8},{12,14},{14,12},{16,18},{18,... | collective-permute-start | bytes 4718600 | tf_op jit(solution)/shard_map/ppermute | solution.py:147
  119.9 33.8 %collective-permute-start.25 = (f32[384,1024]{1,0:T(8,128)S(1)}, f32[384,1024]{1,0:T(8,128)S(1)}, u32[]{:S(2)}, u32[]{:S(2)}) collective-permute-start(f32[384,1024]{1,0:T(8,128)S(1)} %collective-permute-done.23.refs_2_), channel_id=1, source_target_pairs={{0,2},{2,0},{4,6},{6,4},{8,10},{10,8},{12,14},{14,12},{16,18},{18,... | collective-permute-start | bytes 4718600 | tf_op jit(solution)/shard_map/ppermute | solution.py:147
  144.7 40.5 %collective-permute-start.3 = (f32[384,1024]{1,0:T(8,128)S(1)}, f32[384,1024]{1,0:T(8,128)S(1)}, u32[]{:S(2)}, u32[]{:S(2)}) collective-permute-start(f32[384,1024]{1,0:T(8,128)S(1)} %collective-permute-done.2), channel_id=1, source_target_pairs={{0,8},{2,10},{4,12},{6,14},{8,0},{10,2},{12,4},{14,6},{16,24},{18,... | collective-permute-start | bytes 4718600 | tf_op jit(solution)/shard_map/ppermute | solution.py:143
  147.2 43.7 %collective-permute-start.18 = (f32[384,1024]{1,0:T(8,128)S(1)}, f32[384,1024]{1,0:T(8,128)}, u32[]{:S(2)}, u32[]{:S(2)}) collective-permute-start(f32[384,1024]{1,0:T(8,128)S(1)} %add.104.refs_1_), channel_id=1, source_target_pairs={{0,4},{2,6},{4,0},{6,2},{8,12},{10,14},{12,8},{14,10},{16,20},{18,... | collective-permute-start | bytes 4718600 | tf_op jit(solution)/shard_map/ppermute | solution.py:142
  151.9 39.5 %collective-permute-start.30 = (f32[384,1024]{1,0:T(8,128)}, f32[384,1024]{1,0:T(8,128)}, u32[]{:S(2)}, u32[]{:S(2)}) collective-permute-start(f32[384,1024]{1,0:T(8,128)} %collective-permute-done.19.refs_2_), channel_id=1, source_target_pairs={{0,2},{2,0},{4,6},{6,4},{8,10},{10,8},{12,14},{14,12},{16,18},{18,... | collective-permute-start | bytes 4718600 | tf_op jit(solution)/shard_map/ppermute | solution.py:147
  153.2 38.6 %collective-permute-start.28 = (f32[384,1024]{1,0:T(8,128)}, f32[384,1024]{1,0:T(8,128)}, u32[]{:S(2)}, u32[]{:S(2)}) collective-permute-start(f32[384,1024]{1,0:T(8,128)} %collective-permute-done.7.refs_2_), channel_id=1, source_target_pairs={{0,2},{2,0},{4,6},{6,4},{8,10},{10,8},{12,14},{14,12},{16,18},{18,... | collective-permute-start | bytes 4718600 | tf_op jit(solution)/shard_map/ppermute | solution.py:147
  154.9 63.4 %collective-permute-start.20 = (f32[384,1024]{1,0:T(8,128)}, f32[384,1024]{1,0:T(8,128)}, u32[]{:S(2)}, u32[]{:S(2)}) collective-permute-start(f32[384,1024]{1,0:T(8,128)} %collective-permute-done.19.refs_2_), channel_id=1, source_target_pairs={{0,4},{2,6},{4,0},{6,2},{8,12},{10,14},{12,8},{14,10},{16,20},{18,... | collective-permute-start | bytes 4718600 | tf_op jit(solution)/shard_map/ppermute | solution.py:142
  186.3 32.0 %collective-permute-start.8 = (f32[384,1024]{1,0:T(8,128)}, f32[384,1024]{1,0:T(8,128)}, u32[]{:S(2)}, u32[]{:S(2)}) collective-permute-start(f32[384,1024]{1,0:T(8,128)} %collective-permute-done.7.refs_2_), channel_id=1, source_target_pairs={{8,16},{10,18},{12,20},{14,22},{16,8},{18,10},{20,12},{22,14},{9,1... | collective-permute-start | bytes 4718600 | tf_op jit(solution)/shard_map/ppermute | solution.py:144
  188.5 3.2 %copy-start = (f32[384,1024]{1,0:T(8,128)S(1)}, f32[384,1024]{1,0:T(8,128)}, u32[]{:S(2)}) copy-start(f32[384,1024]{1,0:T(8,128)} %refs_1_.1) | copy-start | bytes 4718596
  190.8 55.1 %collective-permute-start.13 = (f32[384,1024]{1,0:T(8,128)S(1)}, f32[384,1024]{1,0:T(8,128)S(1)}, u32[]{:S(2)}, u32[]{:S(2)}) collective-permute-start(f32[384,1024]{1,0:T(8,128)S(1)} %add.97.refs_1_), channel_id=1, source_target_pairs={{0,1},{1,0},{2,3},{3,2},{4,5},{5,4},{6,7},{7,6},{8,9},{9,8},{10,11... | collective-permute-start | bytes 4718600 | tf_op jit(solution)/shard_map/ppermute | solution.py:141
  191.4 54.4 %collective-permute-start.21 = (f32[384,1024]{1,0:T(8,128)}, f32[384,1024]{1,0:T(8,128)S(1)}, u32[]{:S(2)}, u32[]{:S(2)}) collective-permute-start(f32[384,1024]{1,0:T(8,128)} %collective-permute-done.18.refs_1_), channel_id=1, source_target_pairs={{0,2},{2,0},{4,6},{6,4},{8,10},{10,8},{12,14},{14,12},{16,18},{18,... | collective-permute-start | bytes 4718600 | tf_op jit(solution)/shard_map/ppermute | solution.py:147
  191.8 64.5 %collective-permute-start.4 = (f32[384,1024]{1,0:T(8,128)S(1)}, f32[384,1024]{1,0:T(8,128)S(1)}, u32[]{:S(2)}, u32[]{:S(2)}) collective-permute-start(f32[384,1024]{1,0:T(8,128)S(1)} %add.97.refs_1_), channel_id=1, source_target_pairs={{0,4},{2,6},{4,0},{6,2},{8,12},{10,14},{12,8},{14,10},{16,20},{18,... | collective-permute-start | bytes 4718600 | tf_op jit(solution)/shard_map/ppermute | solution.py:142
  218.3 38.1 %collective-permute-start.22 = (f32[384,1024]{1,0:T(8,128)}, f32[384,1024]{1,0:T(8,128)}, u32[]{:S(2)}, u32[]{:S(2)}) collective-permute-start(f32[384,1024]{1,0:T(8,128)} %collective-permute-done.20.refs_2_), channel_id=1, source_target_pairs={{0,2},{2,0},{4,6},{6,4},{8,10},{10,8},{12,14},{14,12},{16,18},{18,... | collective-permute-start | bytes 4718600 | tf_op jit(solution)/shard_map/ppermute | solution.py:147
  218.3 41.5 %collective-permute-start.9 = (f32[384,1024]{1,0:T(8,128)}, f32[384,1024]{1,0:T(8,128)}, u32[]{:S(2)}, u32[]{:S(2)}) collective-permute-start(f32[384,1024]{1,0:T(8,128)} %collective-permute-done.8.refs_3_), channel_id=1, source_target_pairs={{0,8},{2,10},{4,12},{6,14},{8,0},{10,2},{12,4},{14,6},{16,24},{18,... | collective-permute-start | bytes 4718600 | tf_op jit(solution)/shard_map/ppermute | solution.py:143
  228.0 9.0 %copy-start.14 = (f32[384,1024]{1,0:T(8,128)S(1)}, f32[384,1024]{1,0:T(8,128)}, u32[]{:S(2)}) copy-start(f32[384,1024]{1,0:T(8,128)} %copy-done.13) | copy-start | bytes 4718596
  228.1 9.0 %copy-start.16 = (f32[384,1024]{1,0:T(8,128)S(1)}, f32[384,1024]{1,0:T(8,128)}, u32[]{:S(2)}) copy-start(f32[384,1024]{1,0:T(8,128)} %copy-done.15) | copy-start | bytes 4718596
  228.1 9.0 %copy-start.18 = (f32[384,1024]{1,0:T(8,128)S(1)}, f32[384,1024]{1,0:T(8,128)}, u32[]{:S(2)}) copy-start(f32[384,1024]{1,0:T(8,128)} %copy-done.17) | copy-start | bytes 4718596
  228.1 9.0 %copy-start.26 = (f32[384,1024]{1,0:T(8,128)S(1)}, f32[384,1024]{1,0:T(8,128)}, u32[]{:S(2)}) copy-start(f32[384,1024]{1,0:T(8,128)} %copy-done.25) | copy-start | bytes 4718596
  237.1 9.4 %copy-start.24 = (f32[384,1024]{1,0:T(8,128)S(1)}, f32[384,1024]{1,0:T(8,128)}, u32[]{:S(2)}) copy-start(f32[384,1024]{1,0:T(8,128)} %copy-done.23) | copy-start | bytes 4718596
  245.9 14.0 %copy-start.10 = (f32[384,1024]{1,0:T(8,128)S(1)}, f32[384,1024]{1,0:T(8,128)}, u32[]{:S(2)}) copy-start(f32[384,1024]{1,0:T(8,128)} %copy-done.9) | copy-start | bytes 4718596
  245.9 14.0 %copy-start.22 = (f32[384,1024]{1,0:T(8,128)S(1)}, f32[384,1024]{1,0:T(8,128)}, u32[]{:S(2)}) copy-start(f32[384,1024]{1,0:T(8,128)} %copy-done.21) | copy-start | bytes 4718596
  245.9 42.5 %collective-permute-start.14 = (f32[384,1024]{1,0:T(8,128)S(1)}, f32[384,1024]{1,0:T(8,128)S(1)}, u32[]{:S(2)}, u32[]{:S(2)}) collective-permute-start(f32[384,1024]{1,0:T(8,128)S(1)} %add.97.refs_1_), channel_id=1, source_target_pairs={{0,2},{2,0},{4,6},{6,4},{8,10},{10,8},{12,14},{14,12},{16,18},{18,... | collective-permute-start | bytes 4718600 | tf_op jit(solution)/shard_map/ppermute | solution.py:147
  246.0 42.5 %collective-permute-start.15 = (f32[384,1024]{1,0:T(8,128)S(1)}, f32[384,1024]{1,0:T(8,128)}, u32[]{:S(2)}, u32[]{:S(2)}) collective-permute-start(f32[384,1024]{1,0:T(8,128)S(1)} %collective-permute-done.13.refs_2_), channel_id=1, source_target_pairs={{0,2},{2,0},{4,6},{6,4},{8,10},{10,8},{12,14},{14,12},{16,18},{18,... | collective-permute-start | bytes 4718600 | tf_op jit(solution)/shard_map/ppermute | solution.py:147
  256.2 13.4 %copy-start.6 = (f32[384,1024]{1,0:T(8,128)S(1)}, f32[384,1024]{1,0:T(8,128)}, u32[]{:S(2)}) copy-start(f32[384,1024]{1,0:T(8,128)} %copy-done.5) | copy-start | bytes 4718596
  256.2 13.4 %copy-start.8 = (f32[384,1024]{1,0:T(8,128)S(1)}, f32[384,1024]{1,0:T(8,128)}, u32[]{:S(2)}) copy-start(f32[384,1024]{1,0:T(8,128)} %copy-done.7) | copy-start | bytes 4718596
  256.2 13.4 %copy-start.12 = (f32[384,1024]{1,0:T(8,128)S(1)}, f32[384,1024]{1,0:T(8,128)}, u32[]{:S(2)}) copy-start(f32[384,1024]{1,0:T(8,128)} %copy-done.11) | copy-start | bytes 4718596
  256.2 13.4 %copy-start.20 = (f32[384,1024]{1,0:T(8,128)S(1)}, f32[384,1024]{1,0:T(8,128)}, u32[]{:S(2)}) copy-start(f32[384,1024]{1,0:T(8,128)} %copy-done.19) | copy-start | bytes 4718596
  256.3 41.8 %collective-permute-start.12 = (f32[384,1024]{1,0:T(8,128)}, f32[384,1024]{1,0:T(8,128)}, u32[]{:S(2)}, u32[]{:S(2)}) collective-permute-start(f32[384,1024]{1,0:T(8,128)} %collective-permute-done.8.refs_3_), channel_id=1, source_target_pairs={{0,2},{2,0},{4,6},{6,4},{8,10},{10,8},{12,14},{14,12},{16,18},{18,... | collective-permute-start | bytes 4718600 | tf_op jit(solution)/shard_map/ppermute | solution.py:147
  256.4 41.6 %collective-permute-start.10 = (f32[384,1024]{1,0:T(8,128)S(1)}, f32[384,1024]{1,0:T(8,128)}, u32[]{:S(2)}, u32[]{:S(2)}) collective-permute-start(f32[384,1024]{1,0:T(8,128)S(1)} %collective-permute-done.4.refs_1_), channel_id=1, source_target_pairs={{0,2},{2,0},{4,6},{6,4},{8,10},{10,8},{12,14},{14,12},{16,18},{18,... | collective-permute-start | bytes 4718600 | tf_op jit(solution)/shard_map/ppermute | solution.py:147
  259.8 38.2 %collective-permute-start.11 = (f32[384,1024]{1,0:T(8,128)}, f32[384,1024]{1,0:T(8,128)}, u32[]{:S(2)}, u32[]{:S(2)}) collective-permute-start(f32[384,1024]{1,0:T(8,128)} %collective-permute-done.9.refs_2_), channel_id=1, source_target_pairs={{0,2},{2,0},{4,6},{6,4},{8,10},{10,8},{12,14},{14,12},{16,18},{18,... | collective-permute-start | bytes 4718600 | tf_op jit(solution)/shard_map/ppermute | solution.py:147
  (16 other events, 19.7 us)

commit v2 on v0

v2 whole, which is shorter than its diff:
```python
import functools

import jax
import jax.numpy as jnp
from jax import lax
from jax.experimental import pallas as pl
from jax.experimental.pallas import tpu as pltpu
from jax.sharding import PartitionSpec as P

damping = 0.1
PASSES = 3
VMEM_BYTES = 60 * 1024 * 1024
COST = 1024


def split_high_low(value):
    high = value.astype(jnp.bfloat16)
    low = (value - high.astype(jnp.float32)).astype(jnp.bfloat16)
    return high, low


def left_kernel(*refs):
    left_ref = refs[-1]
    depth, rows = refs[0].shape
    for block in range(len(refs) // 2):
        for place, ref in enumerate(refs[2 * block : 2 * block + 2]):
            high, low = split_high_low(ref[...].T)
            for part, piece in enumerate((high, high, low)):
                target = pl.ds(rows * block, rows), pl.ds(2 * depth * part + depth * place, depth)
                left_ref[target] = piece


def left_operand(*halves):
    depth, rows = halves[0].shape
    shape = rows * (len(halves) // 2), 2 * PASSES * depth
    return pl.pallas_call(
        left_kernel,
        out_shape=jax.ShapeDtypeStruct(shape, jnp.bfloat16),
        compiler_params=pltpu.CompilerParams(vmem_limit_bytes=VMEM_BYTES),
        cost_estimate=pl.CostEstimate(flops=COST, bytes_accessed=COST, transcendentals=0),
        name="left_operand",
    )(*halves)


def panel_kernel(sizes, diagonal, part, placed, tile, sends, ids_ref, *refs):
    count = sum(map(sum, sizes))
    left_hbm, blocks = refs[0], refs[1 : 1 + count]
    left_ref, held, done, stage_ref, left_sem, load_sem, store_sem, place_sem = refs[-8:]
    received_ref = refs[1 + count] if placed else None
    out_ref, send_ref = (refs[-10], refs[-9]) if sends else (refs[-9], None)
    width, rows = held.shape[-1], out_ref.shape[0]
    tiles, panel_count = width // tile, len(sizes)
    most = max(map(sum, sizes))
    left_copy = pltpu.make_async_copy(left_hbm.at[pl.ds(0, left_ref.shape[0])], left_ref, left_sem)
    loads, at = [], 0
    for index, counts in enumerate(sizes):
        loads.append([])
        for place in range(sum(counts)):
            here = index % 2, place
            loads[index].append(pltpu.make_async_copy(blocks[at], held.at[here], load_sem.at[here]))
            at += 1
    fetches, puts = [], []
    if placed:
        first, whole = placed
        for index in range(received_ref.shape[0]):
            column = pl.multiple_of(ids_ref[panel_count + index] * whole + first, 128)
            target = out_ref.at[:, pl.ds(column, received_ref.shape[-1])]
            stage = stage_ref.at[index]
            fetches.append(pltpu.make_async_copy(received_ref.at[index], stage, place_sem.at[index, 0]))
            puts.append(pltpu.make_async_copy(stage, target, place_sem.at[index, 1]))

    def stores(turn):
        first, whole = part
        index, column = turn // tiles, pl.multiple_of(lax.rem(turn, tiles) * tile, 128)
        slot = lax.rem(turn, 2)
        place = pl.multiple_of(ids_ref[index] * whole + first + column, 128)
        copies = [(done.at[slot, pl.ds(0, rows)], out_ref.at[:, pl.ds(place, tile)], store_sem.at[slot, 0])]
        if sends:
            target = send_ref.at[index, :, pl.ds(column, tile)]
            copies.append((done.at[slot, pl.ds(rows, rows)], target, store_sem.at[slot, 1]))
        return [pltpu.make_async_copy(*copy) for copy in copies]

    for copy in loads[0] + [left_copy] + (loads[1] if panel_count > 1 else []) + fetches:
        copy.start()
    left_copy.wait()
    turns = panel_count * tiles

    def turn_body(turn, carry):
        index, column = turn // tiles, pl.multiple_of(lax.rem(turn, tiles) * tile, 128)
        slot = lax.rem(index, 2)
        for here, copies in enumerate(loads):

            @pl.when(turn == here * tiles)
            def arrive(copies=copies):
                for copy in copies:
                    copy.wait()

        @pl.when(turn >= 2)
        def free():
            for copy in stores(turn - 2):
                copy.wait()

        @pl.when(turn == min(1, turns - 1))
        def put():
            for fetch, put in zip(fetches, puts):
                fetch.wait()
                put.start()

        block = [held[slot, k, :, pl.ds(column, tile)] for k in range(most)]
        if most > 2:
            extra = functools.reduce(jnp.logical_or, [index == i for i, n in enumerate(sizes) if sum(n) > 2])
            block[1] = block[1] + jnp.where(extra, block[2], 0.0)
        halves = [split_high_low(value) for value in block[:2]]
        high, low = (jnp.concatenate(pieces, axis=0) for pieces in zip(*halves))
        right = jnp.concatenate([high, low, high], axis=0)
        product = jnp.dot(left_ref[...], right, preferred_element_type=jnp.float32)
        if diagonal is not None:
            row_ids = lax.broadcasted_iota(jnp.int32, product.shape, 0) + ids_ref[ids_ref.shape[0] - 1]
            col_ids = lax.broadcasted_iota(jnp.int32, product.shape, 1) + column
            own = lax.broadcasted_iota(jnp.int32, product.shape, 0) < rows
            hit = (row_ids == col_ids) & own & (index == diagonal)
            product = jnp.where(hit, product * jnp.float32(1.0 + damping), product)
        done[lax.rem(turn, 2)] = product
        for copy in stores(turn):
            copy.start()
        for here in range(panel_count - 2):

            @pl.when(turn == here * tiles + tiles - 1)
            def fetch(copies=loads[here + 2]):
                for copy in copies:
                    copy.start()

        return carry

    lax.fori_loop(0, turns, turn_body, 0)
    for turn in range(max(0, turns - 2), turns):
        for copy in stores(turn):
            copy.wait()
    for copy in puts:
        copy.wait()


def panels(out, left, rows, columns, pairs, ids, received=None, placed=None, diagonal=None, part=None, sends=False, tile=None):
    depth, width = pairs[0][0][0].shape
    sizes = tuple(tuple(len(half) for half in pair) for pair in pairs)
    args = [ids, left] + [array for pair in pairs for half in pair for array in half]
    if received is not None:
        args.append(received)
    aliases = {}
    if out is not None:
        aliases = {len(args): 0}
        args.append(out)
    anywhere = pl.BlockSpec(memory_space=pl.ANY)
    most = max(map(sum, sizes))
    tile = tile or min(256, width)
    height = 2 * rows if sends else rows
    shapes = [jax.ShapeDtypeStruct((rows, columns), jnp.float32)]
    if sends:
        shapes.append(jax.ShapeDtypeStruct((len(pairs), rows, width), jnp.float32))
    outs = pl.pallas_call(
        functools.partial(panel_kernel, sizes, diagonal, part or (0, width), placed, tile, sends),
        out_shape=shapes,
        in_specs=[pl.BlockSpec(memory_space=pltpu.SMEM)] + [anywhere] * (len(args) - 1),
        out_specs=[anywhere] * len(shapes),
        scratch_shapes=[
            pltpu.VMEM((height, left.shape[1]), left.dtype),
            pltpu.VMEM((2, most, depth, width), jnp.float32),
            pltpu.VMEM((2, height, tile), jnp.float32),
            pltpu.VMEM(received.shape if placed else (8, 128), jnp.float32),
            pltpu.SemaphoreType.DMA,
            pltpu.SemaphoreType.DMA((2, most)),
            pltpu.SemaphoreType.DMA((2, 2)),
            pltpu.SemaphoreType.DMA((received.shape[0] if placed else 1, 2)),
        ],
        input_output_aliases=aliases,
        compiler_params=pltpu.CompilerParams(vmem_limit_bytes=VMEM_BYTES),
        cost_estimate=pl.CostEstimate(
            flops=20 * height * left.shape[1] * width * len(pairs),
            bytes_accessed=4 * width * len(pairs) * (height + 2 * depth),
            transcendentals=0,
        ),
        name="panels",
    )(*args)
    return outs if sends else outs[0]


def place_kernel(placed, ids_ref, received_ref, _, out_ref, stage_ref, place_sem):
    first, whole = placed
    fetches, puts = [], []
    for index in range(received_ref.shape[0]):
        column = pl.multiple_of(ids_ref[index] * whole + first, 128)
        target = out_ref.at[:, pl.ds(column, received_ref.shape[-1])]
        stage = stage_ref.at[index]
        fetches.append(pltpu.make_async_copy(received_ref.at[index], stage, place_sem.at[index, 0]))
        puts.append(pltpu.make_async_copy(stage, target, place_sem.at[index, 1]))
    for fetch in fetches:
        fetch.start()
    for fetch, put in zip(fetches, puts):
        fetch.wait()
        put.start()
    for put in puts:
        put.wait()


def place(out, received, ids, placed):
    anywhere = pl.BlockSpec(memory_space=pl.ANY)
    return pl.pallas_call(
        functools.partial(place_kernel, placed),
        out_shape=jax.ShapeDtypeStruct(out.shape, out.dtype),
        in_specs=[pl.BlockSpec(memory_space=pltpu.SMEM), anywhere, anywhere],
        out_specs=anywhere,
        scratch_shapes=[
            pltpu.VMEM(received.shape, received.dtype),
            pltpu.SemaphoreType.DMA((received.shape[0], 2)),
        ],
        input_output_aliases={2: 0},
        compiler_params=pltpu.CompilerParams(vmem_limit_bytes=VMEM_BYTES),
        cost_estimate=pl.CostEstimate(flops=0, bytes_accessed=8 * received.size, transcendentals=0),
        name="place",
    )(ids, received, out)


def gathered(loop, grp, jacobian):
    rows_here = jacobian.shape[1] // grp
    me, side = lax.axis_index("loop"), lax.axis_index("grp")
    both = lax.all_gather(jacobian, "grp")
    everything = lax.all_gather(both, "loop")
    mine = lax.dynamic_slice_in_dim(both, side * rows_here, rows_here, axis=2)
    left = left_operand(mine[0], mine[1])
    out = None
    for turn in range(loop):
        panel = (me + turn) % loop
        pair = tuple((lax.dynamic_index_in_dim(everything, panel, keepdims=False)[g],) for g in range(2))
        ids = jnp.stack([panel, side * rows_here]).astype(jnp.int32)
        out = panels(out, left, rows_here, jacobian.shape[1] * loop, [pair], ids, diagonal=None if turn else 0)
    return out


def rounds(loop, grp, jacobian):
    width = jacobian.shape[1]
    rows_here, columns = width // grp, width * loop
    me, side = lax.axis_index("loop"), lax.axis_index("grp")
    z, y, core = me // 4, (me // 2) % 2, me % 2

    along_x = lambda v: lax.ppermute(v, "grp", [(0, 1), (1, 0)])
    along_y = lambda v: lax.ppermute(v, "loop", [(i, i ^ 2) for i in range(16)])
    pair_z = lambda v: lax.ppermute(v, "loop", [(i, i ^ 4) for i in range(16)])
    mid_z = lambda v: lax.ppermute(
        v, "loop", [(i, i + 4) for i in range(4, 8)] + [(i + 4, i) for i in range(4, 8)]
    )
    swap = lambda v: lax.ppermute(v, "loop", [(i, i ^ 1) for i in range(16)])
    together = lax.optimization_barrier

    mate_z = z ^ 1
    near_z = jnp.where(z < 2, 2, 1)
    far_z = jnp.where(z < 2, 3, 0)
    shift = side * rows_here
    places = [(z, y), (z, 1 - y), (near_z, y), (mate_z, 1 - y), (mate_z, y), (near_z, 1 - y), (far_z, y), (far_z, 1 - y)]
    own = [zz * 4 + yy * 2 + core for zz, yy in places]
    other = [zz * 4 + yy * 2 + 1 - core for zz, yy in places]
    number = lambda *numbers: jnp.stack(numbers).astype(jnp.int32)
    ids = tuple(number(*n) for n in (own[:1] + [shift], own[1:2], own[2:4], own[4:6], own[6:], other[6:] + other[4:6]))
    put = tuple(number(*n) for n in (other[:1], other[1:2], other[2:4]))
    step = lambda out, left, turn, pairs, **kw: panels(out, left, rows_here, columns, pairs, ids[turn], **kw)
    whole = 0, width

    c = jacobian
    x_self, y_self, c_mate, mid0 = along_x(c), along_y(c), pair_z(c), mid_z(c)
    own_columns = lambda v: lax.dynamic_slice_in_dim(v, shift, rows_here, axis=1)
    own_c = own_columns(c)
    own_c_o = swap(own_c)
    x_self, y_self, c_mate, mid0, own_c, own_c_o, ids, put = together(
        (x_self, y_self, c_mate, mid0, own_c, own_c_o, ids, put)
    )

    d_self, y_mate, pair1, mid1 = along_x(y_self), along_y(c_mate), pair_z(mid0), mid_z(c_mate)
    own_x = own_columns(x_self)
    left = left_operand(own_c, own_x, own_c_o, swap(own_x))
    out, send1 = step(None, left, 0, [((c,), (x_self,))], diagonal=0, sends=True)
    d_self, y_mate, pair1, mid1, out = together((d_self, y_mate, pair1, mid1, out))

    d_mate = pair_z(d_self)
    c_near = pair1 + mid0
    x_near, y_near = along_x(c_near), along_y(c_near)
    out, send2 = step(out, left, 1, [((y_self,), (d_self,))], sends=True)
    out = place(out, swap(send1), put[0], whole)
    d_mate, x_near, y_near, c_near, c_mate, mid1, out = together(
        (d_mate, x_near, y_near, c_near, c_mate, mid1, out)
    )

    x_mate, d_near, pair3, mid3 = along_x(c_mate), along_y(x_near), pair_z(mid1), mid_z(d_mate)
    out, send3 = step(out, left, 2, [((c_near,), (x_near,)), ((y_mate,), (d_mate,))], sends=True)
    out = place(out, swap(send2), put[1], whole)
    x_mate, d_near, pair3, mid1, mid3, out = together((x_mate, d_near, pair3, mid1, mid3, out))

    d_far = pair_z(mid3)
    c_far = pair3 + mid1
    x_far, y_far = along_x(c_far), along_y(c_far)
    out, send4 = step(out, left, 3, [((c_mate,), (x_mate,)), ((y_near,), (d_near,))], sends=True)
    out = place(out, swap(send3), put[2], whole)
    c_far_o = swap(c_far)
    x_far, y_far, d_far, c_far, c_far_o, mid3, out = together((x_far, y_far, d_far, c_far, c_far_o, mid3, out))

    out = step(out, left, 4, [((c_far,), (x_far,)), ((y_far,), (d_far, mid3))])
    pairs = [((c_far_o,), (swap(x_far),)), ((swap(y_far),), (swap(d_far + mid3),))]
    return step(out, left, 5, pairs, received=swap(send4), placed=whole)


def solution(mesh):
    loop, grp = mesh.shape["loop"], mesh.shape["grp"]
    plan = rounds if (loop, grp) == (16, 2) else gathered
    return jax.shard_map(
        functools.partial(plan, loop, grp),
        mesh=mesh,
        in_specs=(P("grp", "loop"),),
        out_specs=P(("loop", "grp"), None),
        check_vma=False,
    )
```

time: 1010 us -> 233 us (0.23)
  waiting for transfers between devices: 862 us -> 92.4 us
  matrix products: 112 us -> 0 us
  Pallas kernels: 0 us -> 93.7 us
  starting transfers between devices: 0.04 us -> 32.1 us
  other arithmetic: 23.3 us -> 9.79 us
  between operations: 13.4 us -> 0.37 us
    reduce_scatter x1 -> x0, waiting for transfers between devices: 729 us -> none  [per_device(): lax.psum_scatter(partial_value, 'grp', scatter_dimension=0, tiled=True)]
    all_gather x1 -> x0, waiting for transfers between devices: 133 us -> none  [per_device(): lax.all_gather(jacobian, 'loop', axis=1, tiled=True)]
    dot_general x1 -> x0, matrix products: 112 us -> none  [gram_block(): lax.dot_general(left_block, right_block, (((0,), (0,)), ((), ())), precis...]
    pallas_call x0 -> x10, Pallas kernels: none -> 93.7 us  [the longest x6 78.6 us: panels(): pl.pallas_call(functools.partial(panel_kernel, sizes, diagonal, part or (...]
    ppermute x0 -> x28, waiting for transfers between devices: none -> 92.4 us  [the longest x5 73.2 us: rounds(): along_x = lambda v: lax.ppermute(v, 'grp', [(0, 1), (1, 0)])]
    ppermute x0 -> x28, starting transfers between devices: none -> 32.1 us  [the longest x5 15.1 us: rounds(): pair_z = lambda v: lax.ppermute(v, 'loop', [(i, i ^ 4) for i in range(16)])]
    mul x1 -> x0, other arithmetic: 23.3 us -> none  [per_device(): return gram_rows * factor]
  transfers between devices with their start and end apart: 2 -> 28, of which waited for: 2 -> 14; matrix products, arithmetic and copies ran while one was open for 0% -> 5% of each run, Pallas kernels for 0% -> 35%
where the time goes in v2:
time: 233 us
  Pallas kernels  93.7 us (40%)
  waiting for transfers between devices  92.4 us (40%)
  starting transfers between devices  32.1 us (14%)
  other arithmetic  9.79 us (4%)
  local copies, waits for them, and re-layouts  4.75 us (2%)
    pallas_call x6, Pallas kernels, panels(): pl.pallas_call(functools.partial(panel_kernel, sizes, diagonal, part or (...  78.6 us
    ppermute x5, waiting for transfers between devices, rounds(): along_x = lambda v: lax.ppermute(v, 'grp', [(0, 1), (1, 0)])  73.2 us
    ppermute x5, waiting for transfers between devices, rounds(): pair_z = lambda v: lax.ppermute(v, 'loop', [(i, i ^ 4) for i in range(16)])  15.3 us
    ppermute x5, starting transfers between devices, rounds(): pair_z = lambda v: lax.ppermute(v, 'loop', [(i, i ^ 4) for i in range(16)])  15.1 us
    pallas_call x3, Pallas kernels, place(): pl.pallas_call(functools.partial(place_kernel, placed), out_shape=jax.Sha...  10.1 us
    ppermute x5, starting transfers between devices, rounds(): along_x = lambda v: lax.ppermute(v, 'grp', [(0, 1), (1, 0)])  6.83 us
    ppermute x5, starting transfers between devices, rounds(): along_y = lambda v: lax.ppermute(v, 'loop', [(i, i ^ 2) for i in range(16)])  5.58 us
    pallas_call x1, Pallas kernels, left_operand(): pl.pallas_call(left_kernel, out_shape=jax.ShapeDtypeStruct(shape, jnp.bfl...  4.86 us
  transfers between devices with their start and end apart: 28, of which 14 were waited for; matrix products, arithmetic and copies ran while one was open for 5% of the time, Pallas kernels for 35%

profile of v2, /device:TPU:0, one launch (start us, length us, event | category | flops | bytes accessed | tf_op | source)
XLA Modules:
  0.0 233.0 jit_solution(4492426538247238605)
XLA Ops:
  0.0 2.9 %collective-permute-start = (f32[384,1024]{1,0:T(8,128)}, f32[384,1024]{1,0:T(8,128)}, u32[]{:S(2)}, u32[]{:S(2)}) collective-permute-start(f32[384,1024]{1,0:T(8,128)} %refs_1_.1), channel_id=1, source_target_pairs={{0,1},{1,0},{2,3},{3,2},{4,5},{5,4},{6,7},{7,6},{8,9},{9,8},{10,11... | collective-permute-start | bytes 4718600 | tf_op jit(solution)/shard_map/ppermute | solution.py:245
  2.9 1.5 collective-permute-start.1
  4.5 1.6 collective-permute-start.2
  6.0 0.7 collective-permute-start.3
  6.8 1.2 constant_dynamic-slice_fusion.1.refs_0_
  8.2 0.6 pad_add_fusion.5.ids_ref
  8.8 0.6 pad_add_fusion.4.ids_ref
  9.3 0.6 pad_add_fusion.2
  10.0 0.6 pad_add_fusion
  10.6 27.1 %collective-permute-done.refs_2_ = f32[384,1024]{1,0:T(8,128)} collective-permute-done((f32[384,1024]{1,0:T(8,128)}, f32[384,1024]{1,0:T(8,128)}, u32[]{:S(2)}, u32[]{:S(2)}) %collective-permute-start) | collective-permute-done | bytes 1572896 | tf_op jit(solution)/shard_map/ppermute | solution.py:245
  37.6 1.5 collective-permute-done.1.refs_1_
  39.1 1.2 collective-permute-done.2.refs_1_
  40.4 1.2 constant_dynamic-slice_fusion.refs_1_
  41.6 0.6 collective-permute-start.7
  42.2 1.8 collective-permute-start.9
  44.4 6.5 %collective-permute-start.8 = (f32[384,1024]{1,0:T(8,128)S(1)}, f32[384,1024]{1,0:T(8,128)}, u32[]{:S(2)}, u32[]{:S(2)}) collective-permute-start(f32[384,1024]{1,0:T(8,128)S(1)} %collective-permute-done.3), channel_id=1, source_target_pairs={{0,8},{2,10},{4,12},{6,14},{8,0},{10,2},{12,4},{14,6},{16,24},{18,... | collective-permute-start | bytes 4718600 | tf_op jit(solution)/shard_map/ppermute | solution.py:247
  50.9 4.9 %left_operand.1.refs_0_ = bf16[1024,2304]{1,0:T(8,128)(2,1)} custom-call(f32[384,512]{1,0:T(8,128)} %copy-done, f32[384,512]{1,0:T(8,128)} %copy-done.1, f32[384,512]{1,0:T(8,128)} %copy-done.5, f32[384,512]{1,0:T(8,128)} %collective-permute-done.5.refs_3_), custom_call_target="tpu_custom_call" | custom-call | flops 1024 | bytes 1024 | tf_op jit(solution)/shard_map/left_operand/pallas_call | solution.py:36
  55.8 10.7 %panels.6 = (f32[512,16384]{1,0:T(8,128)}, f32[1,512,1024]{2,1,0:T(8,128)}) custom-call(s32[2]{0:T(128)} %get-tuple-element.60.ids_ref, bf16[1024,2304]{1,0:T(8,128)(2,1)} %left_operand.1.refs_0_, f32[384,1024]{1,0:T(8,128)} %refs_1_.1, f32[384,1024]{1,0:T(8,128)} %collective-permute-done.refs_2_), custom_call_target="tpu_custom_call" | custom-call | flops 48318382080 | bytes 7340032 | tf_op jit(solution)/shard_map/panels/pallas_call | solution.py:160
  66.6 14.2 %collective-permute-done.6.refs_2_ = f32[384,1024]{1,0:T(8,128)} collective-permute-done((f32[384,1024]{1,0:T(8,128)}, f32[384,1024]{1,0:T(8,128)}, u32[]{:S(2)}, u32[]{:S(2)}) %collective-permute-start.6) | collective-permute-done | bytes 1572896 | tf_op jit(solution)/shard_map/ppermute | solution.py:245
  80.8 4.4 %collective-permute-done.8 = f32[384,1024]{1,0:T(8,128)} collective-permute-done((f32[384,1024]{1,0:T(8,128)S(1)}, f32[384,1024]{1,0:T(8,128)}, u32[]{:S(2)}, u32[]{:S(2)}) %collective-permute-start.8) | collective-permute-done | bytes 1572896 | tf_op jit(solution)/shard_map/ppermute | solution.py:247
  85.2 2.8 %add.129.refs_1_ = f32[384,1024]{1,0:T(8,128)} add(f32[384,1024]{1,0:T(8,128)} %collective-permute-done.8, f32[384,1024]{1,0:T(8,128)S(1)} %collective-permute-done.3) | non-fusion elementwise | flops 393216 | bytes 4718592 | tf_op jit(solution)/shard_map/add | solution.py:283
  88.0 1.5 collective-permute-start.11
  89.5 1.5 collective-permute-start.12
  91.0 1.7 collective-permute-start.10
  92.8 10.0 %panels.7 = (f32[512,16384]{1,0:T(8,128)}, f32[1,512,1024]{2,1,0:T(8,128)}) custom-call(s32[1]{0:T(128)} %bitcast.2.ids_ref, bf16[1024,2304]{1,0:T(8,128)(2,1)} %left_operand.1.refs_0_, f32[384,1024]{1,0:T(8,128)} %collective-permute-done.1.refs_1_, f32[384,1024]{1,0:T(8,128)} %collective-permute-done.6.refs_2_, ...), custom_call_target="tpu_custom_call", output_to_operand_aliasing={{0}: (4, {})} | custom-call | flops 48318382080 | bytes 7340032 | tf_op jit(solution)/shard_map/panels/pallas_call | solution.py:160
  102.9 2.9 %place.3.refs_5_ = f32[512,16384]{1,0:T(8,128)} custom-call(s32[1]{0:T(128)} %bitcast.13.ids_ref, f32[1,512,1024]{2,1,0:T(8,128)} %collective-permute-done.13.received_ref, f32[512,16384]{1,0:T(8,128)} %get-tuple-element.69._), custom_call_target="tpu_custom_call", output_to_operand_aliasing={{}: (2, {})} | custom-call | bytes 4194304 | tf_op jit(solution)/shard_map/place/pallas_call | solution.py:207
  105.8 17.8 %collective-permute-done.11.refs_2_ = f32[384,1024]{1,0:T(8,128)} collective-permute-done((f32[384,1024]{1,0:T(8,128)}, f32[384,1024]{1,0:T(8,128)}, u32[]{:S(2)}, u32[]{:S(2)}) %collective-permute-start.11) | collective-permute-done | bytes 1572896 | tf_op jit(solution)/shard_map/ppermute | solution.py:245
  123.7 1.1 collective-permute-done.12.refs_3_
  124.8 1.3 collective-permute-done.10.refs_4_
  127.1 1.7 collective-permute-start.16
  128.9 0.7 collective-permute-start.17
  129.6 16.9 %panels.8 = (f32[512,16384]{1,0:T(8,128)}, f32[2,512,1024]{2,1,0:T(8,128)}) custom-call(s32[2]{0:T(128)} %get-tuple-element.76.ids_ref, bf16[1024,2304]{1,0:T(8,128)(2,1)} %left_operand.1.refs_0_, f32[384,1024]{1,0:T(8,128)} %add.129.refs_1_, f32[384,1024]{1,0:T(8,128)} %collective-permute-done.11.refs_2_, ...), custom_call_target="tpu_custom_call", output_to_operand_aliasing={{0}: (6, {})} | custom-call | flops 96636764160 | bytes 14680064 | tf_op jit(solution)/shard_map/panels/pallas_call | solution.py:160
  146.6 1.2 copy-done.2
  147.8 2.9 %place.4.refs_5_ = f32[512,16384]{1,0:T(8,128)} custom-call(s32[1]{0:T(128)} %bitcast.14.ids_ref, f32[1,512,1024]{2,1,0:T(8,128)} %copy-done.2, f32[512,16384]{1,0:T(8,128)} %get-tuple-element.80._), custom_call_target="tpu_custom_call", output_to_operand_aliasing={{}: (2, {})} | custom-call | bytes 4194304 | tf_op jit(solution)/shard_map/place/pallas_call | solution.py:207
  150.7 9.5 %collective-permute-done.14.refs_2_ = f32[384,1024]{1,0:T(8,128)} collective-permute-done((f32[384,1024]{1,0:T(8,128)}, f32[384,1024]{1,0:T(8,128)}, u32[]{:S(2)}, u32[]{:S(2)}) %collective-permute-start.14) | collective-permute-done | bytes 1572896 | tf_op jit(solution)/shard_map/ppermute | solution.py:245
  160.9 2.8 %add.130.refs_1_ = f32[384,1024]{1,0:T(8,128)S(1)} add(f32[384,1024]{1,0:T(8,128)} %collective-permute-done.16, f32[384,1024]{1,0:T(8,128)} %collective-permute-done.9) | non-fusion elementwise | flops 393216 | bytes 4718592 | tf_op jit(solution)/shard_map/add | solution.py:297
  163.7 1.5 collective-permute-start.19
  165.2 1.5 collective-permute-start.20
  166.6 3.5 %collective-permute-start.21 = (f32[384,1024]{1,0:T(8,128)S(1)}, f32[384,1024]{1,0:T(8,128)}, u32[]{:S(2)}, u32[]{:S(2)}) collective-permute-start(f32[384,1024]{1,0:T(8,128)S(1)} %collective-permute-done.17.refs_5_), channel_id=1, source_target_pairs={{0,8},{2,10},{4,12},{6,14},{8,0},{10,2},{12,4},{14,6},{16,24},{18,... | collective-permute-start | bytes 4718600 | tf_op jit(solution)/shard_map/ppermute | solution.py:247
  170.2 16.9 %panels.9 = (f32[512,16384]{1,0:T(8,128)}, f32[2,512,1024]{2,1,0:T(8,128)}) custom-call(s32[2]{0:T(128)} %get-tuple-element.86.ids_ref, bf16[1024,2304]{1,0:T(8,128)(2,1)} %left_operand.1.refs_0_, f32[384,1024]{1,0:T(8,128)} %collective-permute-done.2.refs_1_, f32[384,1024]{1,0:T(8,128)} %collective-permute-done.14.refs_2_, ...), custom_call_target="tpu_custom_call", output_to_operand_aliasing={{0}: (6, {})} | custom-call | flops 96636764160 | bytes 14680064 | tf_op jit(solution)/shard_map/panels/pallas_call | solution.py:160
  187.4 4.3 %place.5.refs_6_ = f32[512,16384]{1,0:T(8,128)} custom-call(s32[2]{0:T(128)} %pad_add_fusion.5.ids_ref, f32[2,512,1024]{2,1,0:T(8,128)} %collective-permute-done.23.received_ref, f32[512,16384]{1,0:T(8,128)} %get-tuple-element.91._), custom_call_target="tpu_custom_call", output_to_operand_aliasing={{}: (2, {})} | custom-call | bytes 8388608 | tf_op jit(solution)/shard_map/place/pallas_call | solution.py:207
  191.7 4.7 %collective-permute-done.19.refs_2_ = f32[384,1024]{1,0:T(8,128)} collective-permute-done((f32[384,1024]{1,0:T(8,128)S(1)}, f32[384,1024]{1,0:T(8,128)}, u32[]{:S(2)}, u32[]{:S(2)}) %collective-permute-start.19) | collective-permute-done | bytes 1572896 | tf_op jit(solution)/shard_map/ppermute | solution.py:245
  196.4 1.0 collective-permute-done.20.refs_3_
  197.4 7.9 %collective-permute-done.21.refs_4_ = f32[384,1024]{1,0:T(8,128)} collective-permute-done((f32[384,1024]{1,0:T(8,128)S(1)}, f32[384,1024]{1,0:T(8,128)}, u32[]{:S(2)}, u32[]{:S(2)}) %collective-permute-start.21) | collective-permute-done | bytes 1572896 | tf_op jit(solution)/shard_map/ppermute | solution.py:247
  205.3 1.8 add.131
  207.8 11.6 %panels.10.refs_6_ = f32[512,16384]{1,0:T(8,128)} custom-call(s32[2]{0:T(128)} %get-tuple-element.98.ids_ref, bf16[1024,2304]{1,0:T(8,128)(2,1)} %left_operand.1.refs_0_, f32[384,1024]{1,0:T(8,128)} %copy-done.4, f32[384,1024]{1,0:T(8,128)} %collective-permute-done.19.refs_2_, ...), custom_call_target="tpu_custom_call", output_to_operand_aliasing={{}: (7, {})} | custom-call | flops 48318382080 | bytes 10485760 | tf_op jit(solution)/shard_map/panels/pallas_call | solution.py:160
  219.5 1.1 copy-done.7
  220.6 12.5 %panels.11 = f32[512,16384]{1,0:T(8,128)} custom-call(s32[4]{0:T(128)} %pad_add_fusion.4.ids_ref, bf16[1024,2304]{1,0:T(8,128)(2,1)} %left_operand.1.refs_0_, f32[384,1024]{1,0:T(8,128)} %collective-permute-done.22.refs_1_, f32[384,1024]{1,0:T(8,128)} %collective-permute-done.24.refs_2_, ...), custom_call_target="tpu_custom_call", output_to_operand_aliasing={{}: (7, {})} | custom-call | flops 48318382080 | bytes 10485760 | tf_op jit(solution)/shard_map/panels/pallas_call | solution.py:160
  (43 shorter events, 3.4 us)
Async XLA Ops:
  0.0 37.6 %collective-permute-start = (f32[384,1024]{1,0:T(8,128)}, f32[384,1024]{1,0:T(8,128)}, u32[]{:S(2)}, u32[]{:S(2)}) collective-permute-start(f32[384,1024]{1,0:T(8,128)} %refs_1_.1), channel_id=1, source_target_pairs={{0,1},{1,0},{2,3},{3,2},{4,5},{5,4},{6,7},{7,6},{8,9},{9,8},{10,11... | collective-permute-start | bytes 4718600 | tf_op jit(solution)/shard_map/ppermute | solution.py:245
  2.9 36.2 %collective-permute-start.1 = (f32[384,1024]{1,0:T(8,128)}, f32[384,1024]{1,0:T(8,128)}, u32[]{:S(2)}, u32[]{:S(2)}) collective-permute-start(f32[384,1024]{1,0:T(8,128)} %refs_1_.1), channel_id=1, source_target_pairs={{0,4},{2,6},{4,0},{6,2},{8,12},{10,14},{12,8},{14,10},{16,20},{18,... | collective-permute-start | bytes 4718600 | tf_op jit(solution)/shard_map/ppermute | solution.py:246
  4.5 35.9 %collective-permute-start.2 = (f32[384,1024]{1,0:T(8,128)}, f32[384,1024]{1,0:T(8,128)}, u32[]{:S(2)}, u32[]{:S(2)}) collective-permute-start(f32[384,1024]{1,0:T(8,128)} %refs_1_.1), channel_id=1, source_target_pairs={{0,8},{2,10},{4,12},{6,14},{8,0},{10,2},{12,4},{14,6},{16,24},{18,... | collective-permute-start | bytes 4718600 | tf_op jit(solution)/shard_map/ppermute | solution.py:247
  6.0 34.3 %collective-permute-start.3 = (f32[384,1024]{1,0:T(8,128)}, f32[384,1024]{1,0:T(8,128)S(1)}, u32[]{:S(2)}, u32[]{:S(2)}) collective-permute-start(f32[384,1024]{1,0:T(8,128)} %refs_1_.1), channel_id=1, source_target_pairs={{8,16},{10,18},{12,20},{14,22},{16,8},{18,10},{20,12},{22,14},{9,1... | collective-permute-start | bytes 4718600 | tf_op jit(solution)/shard_map/ppermute | solution.py:248
  8.0 43.0 %copy-start = (f32[384,512]{1,0:T(8,128)}, f32[384,512]{1,0:T(8,128)S(1)}, u32[]{:S(2)}) copy-start(f32[384,512]{1,0:T(8,128)S(1)} %constant_dynamic-slice_fusion.1.refs_0_) | copy-start | bytes 2359300
  8.0 2.6 %collective-permute-start.4 = (f32[384,512]{1,0:T(8,128)S(1)}, f32[384,512]{1,0:T(8,128)S(1)}, u32[]{:S(2)}, u32[]{:S(2)}) collective-permute-start(f32[384,512]{1,0:T(8,128)S(1)} %constant_dynamic-slice_fusion.1.refs_0_), channel_id=1, source_target_pairs={{0,2},{2,0},{4,6},{6,4},{8,10},{10,8},{12,14},{14,12},{16,18},{18,... | collective-permute-start | bytes 2359304 | tf_op jit(solution)/shard_map/ppermute | solution.py:251
  10.6 29.8 %copy-start.5 = (f32[384,512]{1,0:T(8,128)}, f32[384,512]{1,0:T(8,128)S(1)}, u32[]{:S(2)}) copy-start(f32[384,512]{1,0:T(8,128)S(1)} %collective-permute-done.4.refs_2_) | copy-start | bytes 2359300
  41.5 9.4 %copy-start.1 = (f32[384,512]{1,0:T(8,128)}, f32[384,512]{1,0:T(8,128)S(1)}, u32[]{:S(2)}) copy-start(f32[384,512]{1,0:T(8,128)S(1)} %constant_dynamic-slice_fusion.refs_1_) | copy-start | bytes 2359300
  41.6 9.4 %collective-permute-start.5 = (f32[384,512]{1,0:T(8,128)S(1)}, f32[384,512]{1,0:T(8,128)}, u32[]{:S(2)}, u32[]{:S(2)}) collective-permute-start(f32[384,512]{1,0:T(8,128)S(1)} %constant_dynamic-slice_fusion.refs_1_), channel_id=1, source_target_pairs={{0,2},{2,0},{4,6},{6,4},{8,10},{10,8},{12,14},{14,12},{16,18},{18,... | collective-permute-start | bytes 2359304 | tf_op jit(solution)/shard_map/ppermute | solution.py:251
  41.6 39.2 %collective-permute-start.7 = (f32[384,1024]{1,0:T(8,128)}, f32[384,1024]{1,0:T(8,128)}, u32[]{:S(2)}, u32[]{:S(2)}) collective-permute-start(f32[384,1024]{1,0:T(8,128)} %collective-permute-done.2.refs_1_), channel_id=1, source_target_pairs={{0,4},{2,6},{4,0},{6,2},{8,12},{10,14},{12,8},{14,10},{16,20},{18,... | collective-permute-start | bytes 4718600 | tf_op jit(solution)/shard_map/ppermute | solution.py:246
  42.2 43.0 %collective-permute-start.9 = (f32[384,1024]{1,0:T(8,128)}, f32[384,1024]{1,0:T(8,128)}, u32[]{:S(2)}, u32[]{:S(2)}) collective-permute-start(f32[384,1024]{1,0:T(8,128)} %collective-permute-done.2.refs_1_), channel_id=1, source_target_pairs={{8,16},{10,18},{12,20},{14,22},{16,8},{18,10},{20,12},{22,14},{9,1... | collective-permute-start | bytes 4718600 | tf_op jit(solution)/shard_map/ppermute | solution.py:248
  44.0 36.8 %collective-permute-start.6 = (f32[384,1024]{1,0:T(8,128)}, f32[384,1024]{1,0:T(8,128)}, u32[]{:S(2)}, u32[]{:S(2)}) collective-permute-start(f32[384,1024]{1,0:T(8,128)} %collective-permute-done.1.refs_1_), channel_id=1, source_target_pairs={{0,1},{1,0},{2,3},{3,2},{4,5},{5,4},{6,7},{7,6},{8,9},{9,8},{10,11... | collective-permute-start | bytes 4718600 | tf_op jit(solution)/shard_map/ppermute | solution.py:245
  44.4 40.8 %collective-permute-start.8 = (f32[384,1024]{1,0:T(8,128)S(1)}, f32[384,1024]{1,0:T(8,128)}, u32[]{:S(2)}, u32[]{:S(2)}) collective-permute-start(f32[384,1024]{1,0:T(8,128)S(1)} %collective-permute-done.3), channel_id=1, source_target_pairs={{0,8},{2,10},{4,12},{6,14},{8,0},{10,2},{12,4},{14,6},{16,24},{18,... | collective-permute-start | bytes 4718600 | tf_op jit(solution)/shard_map/ppermute | solution.py:247
  66.5 36.3 %collective-permute-start.13 = (f32[1,512,1024]{2,1,0:T(8,128)}, f32[1,512,1024]{2,1,0:T(8,128)}, u32[]{:S(2)}, u32[]{:S(2)}) collective-permute-start(f32[1,512,1024]{2,1,0:T(8,128)} %get-tuple-element.66), channel_id=1, source_target_pairs={{0,2},{2,0},{4,6},{6,4},{8,10},{10,8},{12,14},{14,12},{16,18},{18,... | collective-permute-start | bytes 6291464 | tf_op jit(solution)/shard_map/ppermute | solution.py:251
  88.0 35.6 %collective-permute-start.11 = (f32[384,1024]{1,0:T(8,128)}, f32[384,1024]{1,0:T(8,128)}, u32[]{:S(2)}, u32[]{:S(2)}) collective-permute-start(f32[384,1024]{1,0:T(8,128)} %add.129.refs_1_), channel_id=1, source_target_pairs={{0,1},{1,0},{2,3},{3,2},{4,5},{5,4},{6,7},{7,6},{8,9},{9,8},{10,11... | collective-permute-start | bytes 4718600 | tf_op jit(solution)/shard_map/ppermute | solution.py:245
  89.5 35.2 %collective-permute-start.12 = (f32[384,1024]{1,0:T(8,128)}, f32[384,1024]{1,0:T(8,128)S(1)}, u32[]{:S(2)}, u32[]{:S(2)}) collective-permute-start(f32[384,1024]{1,0:T(8,128)} %add.129.refs_1_), channel_id=1, source_target_pairs={{0,4},{2,6},{4,0},{6,2},{8,12},{10,14},{12,8},{14,10},{16,20},{18,... | collective-permute-start | bytes 4718600 | tf_op jit(solution)/shard_map/ppermute | solution.py:246
  91.0 35.1 %collective-permute-start.10 = (f32[384,1024]{1,0:T(8,128)}, f32[384,1024]{1,0:T(8,128)}, u32[]{:S(2)}, u32[]{:S(2)}) collective-permute-start(f32[384,1024]{1,0:T(8,128)} %collective-permute-done.6.refs_2_), channel_id=1, source_target_pairs={{0,8},{2,10},{4,12},{6,14},{8,0},{10,2},{12,4},{14,6},{16,24},{18,... | collective-permute-start | bytes 4718600 | tf_op jit(solution)/shard_map/ppermute | solution.py:247
  102.8 43.7 %collective-permute-start.18 = (f32[1,512,1024]{2,1,0:T(8,128)}, f32[1,512,1024]{2,1,0:T(8,128)S(1)}, u32[]{:S(2)}, u32[]{:S(2)}) collective-permute-start(f32[1,512,1024]{2,1,0:T(8,128)} %get-tuple-element.75), channel_id=1, source_target_pairs={{0,2},{2,0},{4,6},{6,4},{8,10},{10,8},{12,14},{14,12},{16,18},{18,... | collective-permute-start | bytes 6291464 | tf_op jit(solution)/shard_map/ppermute | solution.py:251
  124.8 2.4 %copy-start.6 = (f32[384,1024]{1,0:T(8,128)}, f32[384,1024]{1,0:T(8,128)S(1)}, u32[]{:S(2)}) copy-start(f32[384,1024]{1,0:T(8,128)S(1)} %collective-permute-done.12.refs_3_) | copy-start | bytes 4718596
  126.1 34.2 %collective-permute-start.14 = (f32[384,1024]{1,0:T(8,128)}, f32[384,1024]{1,0:T(8,128)}, u32[]{:S(2)}, u32[]{:S(2)}) collective-permute-start(f32[384,1024]{1,0:T(8,128)} %collective-permute-done.2.refs_1_), channel_id=1, source_target_pairs={{0,1},{1,0},{2,3},{3,2},{4,5},{5,4},{6,7},{7,6},{8,9},{9,8},{10,11... | collective-permute-start | bytes 4718600 | tf_op jit(solution)/shard_map/ppermute | solution.py:245
  126.6 33.9 %collective-permute-start.15 = (f32[384,1024]{1,0:T(8,128)}, f32[384,1024]{1,0:T(8,128)}, u32[]{:S(2)}, u32[]{:S(2)}) collective-permute-start(f32[384,1024]{1,0:T(8,128)} %collective-permute-done.11.refs_2_), channel_id=1, source_target_pairs={{0,4},{2,6},{4,0},{6,2},{8,12},{10,14},{12,8},{14,10},{16,20},{18,... | collective-permute-start | bytes 4718600 | tf_op jit(solution)/shard_map/ppermute | solution.py:246
  127.1 33.7 %collective-permute-start.16 = (f32[384,1024]{1,0:T(8,128)}, f32[384,1024]{1,0:T(8,128)}, u32[]{:S(2)}, u32[]{:S(2)}) collective-permute-start(f32[384,1024]{1,0:T(8,128)} %collective-permute-done.9), channel_id=1, source_target_pairs={{0,8},{2,10},{4,12},{6,14},{8,0},{10,2},{12,4},{14,6},{16,24},{18,... | collective-permute-start | bytes 4718600 | tf_op jit(solution)/shard_map/ppermute | solution.py:247
  128.9 32.0 %collective-permute-start.17 = (f32[384,1024]{1,0:T(8,128)}, f32[384,1024]{1,0:T(8,128)S(1)}, u32[]{:S(2)}, u32[]{:S(2)}) collective-permute-start(f32[384,1024]{1,0:T(8,128)} %collective-permute-done.10.refs_4_), channel_id=1, source_target_pairs={{8,16},{10,18},{12,20},{14,22},{16,8},{18,10},{20,12},{22,14},{9,1... | collective-permute-start | bytes 4718600 | tf_op jit(solution)/shard_map/ppermute | solution.py:248
  146.5 1.3 copy-start.2
  146.5 40.6 %collective-permute-start.23 = (f32[2,512,1024]{2,1,0:T(8,128)}, f32[2,512,1024]{2,1,0:T(8,128)}, u32[]{:S(2)}, u32[]{:S(2)}) collective-permute-start(f32[2,512,1024]{2,1,0:T(8,128)} %get-tuple-element.85), channel_id=1, source_target_pairs={{0,2},{2,0},{4,6},{6,4},{8,10},{10,8},{12,14},{14,12},{16,18},{18,... | collective-permute-start | bytes 12582920 | tf_op jit(solution)/shard_map/ppermute | solution.py:251
  160.9 44.4 %copy-start.3 = (f32[384,1024]{1,0:T(8,128)}, f32[384,1024]{1,0:T(8,128)S(1)}, u32[]{:S(2)}) copy-start(f32[384,1024]{1,0:T(8,128)S(1)} %collective-permute-done.17.refs_5_) | copy-start | bytes 4718596
  163.7 23.4 %copy-start.4 = (f32[384,1024]{1,0:T(8,128)}, f32[384,1024]{1,0:T(8,128)S(1)}, u32[]{:S(2)}) copy-start(f32[384,1024]{1,0:T(8,128)S(1)} %add.130.refs_1_) | copy-start | bytes 4718596
  163.7 32.7 %collective-permute-start.19 = (f32[384,1024]{1,0:T(8,128)S(1)}, f32[384,1024]{1,0:T(8,128)}, u32[]{:S(2)}, u32[]{:S(2)}) collective-permute-start(f32[384,1024]{1,0:T(8,128)S(1)} %add.130.refs_1_), channel_id=1, source_target_pairs={{0,1},{1,0},{2,3},{3,2},{4,5},{5,4},{6,7},{7,6},{8,9},{9,8},{10,11... | collective-permute-start | bytes 4718600 | tf_op jit(solution)/shard_map/ppermute | solution.py:245
  165.2 32.2 %collective-permute-start.20 = (f32[384,1024]{1,0:T(8,128)S(1)}, f32[384,1024]{1,0:T(8,128)}, u32[]{:S(2)}, u32[]{:S(2)}) collective-permute-start(f32[384,1024]{1,0:T(8,128)S(1)} %add.130.refs_1_), channel_id=1, source_target_pairs={{0,4},{2,6},{4,0},{6,2},{8,12},{10,14},{12,8},{14,10},{16,20},{18,... | collective-permute-start | bytes 4718600 | tf_op jit(solution)/shard_map/ppermute | solution.py:246
  166.6 30.8 %collective-permute-start.22 = (f32[384,1024]{1,0:T(8,128)S(1)}, f32[384,1024]{1,0:T(8,128)}, u32[]{:S(2)}, u32[]{:S(2)}) collective-permute-start(f32[384,1024]{1,0:T(8,128)S(1)} %add.130.refs_1_), channel_id=1, source_target_pairs={{0,2},{2,0},{4,6},{6,4},{8,10},{10,8},{12,14},{14,12},{16,18},{18,... | collective-permute-start | bytes 4718600 | tf_op jit(solution)/shard_map/ppermute | solution.py:251
  166.6 38.7 %collective-permute-start.21 = (f32[384,1024]{1,0:T(8,128)S(1)}, f32[384,1024]{1,0:T(8,128)}, u32[]{:S(2)}, u32[]{:S(2)}) collective-permute-start(f32[384,1024]{1,0:T(8,128)S(1)} %collective-permute-done.17.refs_5_), channel_id=1, source_target_pairs={{0,8},{2,10},{4,12},{6,14},{8,0},{10,2},{12,4},{14,6},{16,24},{18,... | collective-permute-start | bytes 4718600 | tf_op jit(solution)/shard_map/ppermute | solution.py:247
  187.1 32.3 %collective-permute-start.27 = (f32[2,512,1024]{2,1,0:T(8,128)}, f32[2,512,1024]{2,1,0:T(8,128)}, u32[]{:S(2)}, u32[]{:S(2)}) collective-permute-start(f32[2,512,1024]{2,1,0:T(8,128)} %get-tuple-element.97), channel_id=1, source_target_pairs={{0,2},{2,0},{4,6},{6,4},{8,10},{10,8},{12,14},{14,12},{16,18},{18,... | collective-permute-start | bytes 12582920 | tf_op jit(solution)/shard_map/ppermute | solution.py:251
  207.1 12.3 %collective-permute-start.26 = (f32[384,1024]{1,0:T(8,128)S(1)}, f32[384,1024]{1,0:T(8,128)S(1)}, u32[]{:S(2)}, u32[]{:S(2)}) collective-permute-start(f32[384,1024]{1,0:T(8,128)S(1)} %add.131), channel_id=1, source_target_pairs={{0,2},{2,0},{4,6},{6,4},{8,10},{10,8},{12,14},{14,12},{16,18},{18,... | collective-permute-start | bytes 4718600 | tf_op jit(solution)/shard_map/ppermute | solution.py:251
  207.2 12.2 %collective-permute-start.24 = (f32[384,1024]{1,0:T(8,128)}, f32[384,1024]{1,0:T(8,128)}, u32[]{:S(2)}, u32[]{:S(2)}) collective-permute-start(f32[384,1024]{1,0:T(8,128)} %collective-permute-done.19.refs_2_), channel_id=1, source_target_pairs={{0,2},{2,0},{4,6},{6,4},{8,10},{10,8},{12,14},{14,12},{16,18},{18,... | collective-permute-start | bytes 4718600 | tf_op jit(solution)/shard_map/ppermute | solution.py:251
  207.7 11.8 %collective-permute-start.25 = (f32[384,1024]{1,0:T(8,128)}, f32[384,1024]{1,0:T(8,128)}, u32[]{:S(2)}, u32[]{:S(2)}) collective-permute-start(f32[384,1024]{1,0:T(8,128)} %collective-permute-done.20.refs_3_), channel_id=1, source_target_pairs={{0,2},{2,0},{4,6},{6,4},{8,10},{10,8},{12,14},{14,12},{16,18},{18,... | collective-permute-start | bytes 4718600 | tf_op jit(solution)/shard_map/ppermute | solution.py:251
  219.4 1.2 copy-start.7

commit v3 on v2

--- a/solution.py
+++ b/solution.py
@@ -8,7 +8,6 @@
 from jax.sharding import PartitionSpec as P
 
 damping = 0.1
-PASSES = 3
 VMEM_BYTES = 60 * 1024 * 1024
 COST = 1024
 
@@ -25,14 +24,14 @@
     for block in range(len(refs) // 2):
         for place, ref in enumerate(refs[2 * block : 2 * block + 2]):
             high, low = split_high_low(ref[...].T)
-            for part, piece in enumerate((high, high, low)):
+            for part, piece in enumerate((high, low)):
                 target = pl.ds(rows * block, rows), pl.ds(2 * depth * part + depth * place, depth)
                 left_ref[target] = piece
 
 
 def left_operand(*halves):
     depth, rows = halves[0].shape
-    shape = rows * (len(halves) // 2), 2 * PASSES * depth
+    shape = rows * (len(halves) // 2), 4 * depth
     return pl.pallas_call(
         left_kernel,
         out_shape=jax.ShapeDtypeStruct(shape, jnp.bfloat16),
@@ -44,14 +43,15 @@
 
 def panel_kernel(sizes, diagonal, part, placed, tile, sends, ids_ref, *refs):
     count = sum(map(sum, sizes))
-    left_hbm, blocks = refs[0], refs[1 : 1 + count]
-    left_ref, held, done, stage_ref, left_sem, load_sem, store_sem, place_sem = refs[-8:]
+    left_ref, blocks = refs[0], refs[1 : 1 + count]
+    held, done, stage_ref, load_sem, store_sem, place_sem = refs[-6:]
     received_ref = refs[1 + count] if placed else None
-    out_ref, send_ref = (refs[-10], refs[-9]) if sends else (refs[-9], None)
+    out_ref, send_ref = (refs[-8], refs[-7]) if sends else (refs[-7], None)
     width, rows = held.shape[-1], out_ref.shape[0]
     tiles, panel_count = width // tile, len(sizes)
     most = max(map(sum, sizes))
-    left_copy = pltpu.make_async_copy(left_hbm.at[pl.ds(0, left_ref.shape[0])], left_ref, left_sem)
+    height, depth = done.shape[1], left_ref.shape[1] // 2
+    left = [left_ref.at[pl.ds(0, height), pl.ds(k * depth, depth)] for k in range(2)]
     loads, at = [], 0
     for index, counts in enumerate(sizes):
         loads.append([])
@@ -80,9 +80,8 @@
             copies.append((done.at[slot, pl.ds(rows, rows)], target, store_sem.at[slot, 1]))
         return [pltpu.make_async_copy(*copy) for copy in copies]
 
-    for copy in loads[0] + [left_copy] + (loads[1] if panel_count > 1 else []) + fetches:
+    for copy in loads[0] + (loads[1] if panel_count > 1 else []) + fetches:
         copy.start()
-    left_copy.wait()
     turns = panel_count * tiles
 
     def turn_body(turn, carry):
@@ -112,8 +111,8 @@
             block[1] = block[1] + jnp.where(extra, block[2], 0.0)
         halves = [split_high_low(value) for value in block[:2]]
         high, low = (jnp.concatenate(pieces, axis=0) for pieces in zip(*halves))
-        right = jnp.concatenate([high, low, high], axis=0)
-        product = jnp.dot(left_ref[...], right, preferred_element_type=jnp.float32)
+        dot = functools.partial(jnp.dot, preferred_element_type=jnp.float32)
+        product = dot(left[0][...], high) + dot(left[0][...], low) + dot(left[1][...], high)
         if diagonal is not None:
             row_ids = lax.broadcasted_iota(jnp.int32, product.shape, 0) + ids_ref[ids_ref.shape[0] - 1]
             col_ids = lax.broadcasted_iota(jnp.int32, product.shape, 1) + column
@@ -152,7 +151,7 @@
         args.append(out)
     anywhere = pl.BlockSpec(memory_space=pl.ANY)
     most = max(map(sum, sizes))
-    tile = tile or min(256, width)
+    tile = tile or min(256 if sends else 512, width)
     height = 2 * rows if sends else rows
     shapes = [jax.ShapeDtypeStruct((rows, columns), jnp.float32)]
     if sends:
@@ -160,14 +159,13 @@
     outs = pl.pallas_call(
         functools.partial(panel_kernel, sizes, diagonal, part or (0, width), placed, tile, sends),
         out_shape=shapes,
-        in_specs=[pl.BlockSpec(memory_space=pltpu.SMEM)] + [anywhere] * (len(args) - 1),
+        in_specs=[pl.BlockSpec(memory_space=pltpu.SMEM), pl.BlockSpec(memory_space=pltpu.VMEM)]
+        + [anywhere] * (len(args) - 2),
         out_specs=[anywhere] * len(shapes),
         scratch_shapes=[
-            pltpu.VMEM((height, left.shape[1]), left.dtype),
             pltpu.VMEM((2, most, depth, width), jnp.float32),
             pltpu.VMEM((2, height, tile), jnp.float32),
             pltpu.VMEM(received.shape if placed else (8, 128), jnp.float32),
-            pltpu.SemaphoreType.DMA,
             pltpu.SemaphoreType.DMA((2, most)),
             pltpu.SemaphoreType.DMA((2, 2)),
             pltpu.SemaphoreType.DMA((received.shape[0] if placed else 1, 2)),
@@ -175,7 +173,7 @@
         input_output_aliases=aliases,
         compiler_params=pltpu.CompilerParams(vmem_limit_bytes=VMEM_BYTES),
         cost_estimate=pl.CostEstimate(
-            flops=20 * height * left.shape[1] * width * len(pairs),
+            flops=30 * height * left.shape[1] * width * len(pairs),
             bytes_accessed=4 * width * len(pairs) * (height + 2 * depth),
             transcendentals=0,
         ),
@@ -220,6 +218,33 @@
     )(ids, received, out)
 
 
+def choose_kernel(flag_ref, first_ref, second_ref, out_ref, sems):
+    rows = out_ref.shape[0] // sems.shape[0]
+    pieces = [pl.ds(k * rows, rows) for k in range(sems.shape[0])]
+    for value, ref in ((1, first_ref), (0, second_ref)):
+
+        @pl.when(flag_ref[0] == value)
+        def copy(ref=ref):
+            for k, piece in enumerate(pieces):
+                pltpu.make_async_copy(ref.at[piece], out_ref.at[piece], sems.at[k]).start()
+
+    for k, piece in enumerate(pieces):
+        pltpu.make_async_copy(first_ref.at[piece], out_ref.at[piece], sems.at[k]).wait()
+
+
+def choose(flag, first, second):
+    anywhere = pl.BlockSpec(memory_space=pl.ANY)
+    return pl.pallas_call(
+        choose_kernel,
+        out_shape=jax.ShapeDtypeStruct(first.shape, first.dtype),
+        in_specs=[pl.BlockSpec(memory_space=pltpu.SMEM), anywhere, anywhere],
+        out_specs=pl.BlockSpec(memory_space=pltpu.VMEM),
+        scratch_shapes=[pltpu.SemaphoreType.DMA((4,))],
+        cost_estimate=pl.CostEstimate(flops=0, bytes_accessed=4 * first.size, transcendentals=0),
+        name="choose",
+    )(flag, first, second)
+
+
 def gathered(loop, grp, jacobian):
     rows_here = jacobian.shape[1] // grp
     me, side = lax.axis_index("loop"), lax.axis_index("grp")
@@ -250,6 +275,7 @@
     )
     swap = lambda v: lax.ppermute(v, "loop", [(i, i ^ 1) for i in range(16)])
     together = lax.optimization_barrier
+    after = lambda value, *first: together((value, first))[0]
 
     mate_z = z ^ 1
     near_z = jnp.where(z < 2, 2, 1)
@@ -259,51 +285,51 @@
     own = [zz * 4 + yy * 2 + core for zz, yy in places]
     other = [zz * 4 + yy * 2 + 1 - core for zz, yy in places]
     number = lambda *numbers: jnp.stack(numbers).astype(jnp.int32)
-    ids = tuple(number(*n) for n in (own[:1] + [shift], own[1:2], own[2:4], own[4:6], own[6:], other[6:] + other[4:6]))
-    put = tuple(number(*n) for n in (other[:1], other[1:2], other[2:4]))
+    ids = tuple(number(*n) for n in (own[:2] + [shift], own[2:4], own[4:6], own[6:], other[6:] + other[4:6]))
+    put = tuple(number(*n) for n in (other[:2], other[2:4]))
+    outer = number((z == 0) | (z == 3))
     step = lambda out, left, turn, pairs, **kw: panels(out, left, rows_here, columns, pairs, ids[turn], **kw)
     whole = 0, width
 
     c = jacobian
-    x_self, y_self, c_mate, mid0 = along_x(c), along_y(c), pair_z(c), mid_z(c)
+    x_self, mid0, c_mate, y_self = along_x(c), mid_z(c), pair_z(c), along_y(c)
     own_columns = lambda v: lax.dynamic_slice_in_dim(v, shift, rows_here, axis=1)
     own_c = own_columns(c)
     own_c_o = swap(own_c)
-    x_self, y_self, c_mate, mid0, own_c, own_c_o, ids, put = together(
-        (x_self, y_self, c_mate, mid0, own_c, own_c_o, ids, put)
-    )
-
-    d_self, y_mate, pair1, mid1 = along_x(y_self), along_y(c_mate), pair_z(mid0), mid_z(c_mate)
+    mid0, own_c, own_c_o, ids, put, outer = together((mid0, own_c, own_c_o, ids, put, outer))
+
+    pair1 = pair_z(after(mid0, c_mate))
+    mid1 = mid_z(c_mate)
+    y_mate = along_y(after(c_mate, y_self))
+    d_self = along_x(after(y_self, x_self))
     own_x = own_columns(x_self)
     left = left_operand(own_c, own_x, own_c_o, swap(own_x))
-    out, send1 = step(None, left, 0, [((c,), (x_self,))], diagonal=0, sends=True)
-    d_self, y_mate, pair1, mid1, out = together((d_self, y_mate, pair1, mid1, out))
-
-    d_mate = pair_z(d_self)
-    c_near = pair1 + mid0
-    x_near, y_near = along_x(c_near), along_y(c_near)
-    out, send2 = step(out, left, 1, [((y_self,), (d_self,))], sends=True)
-    out = place(out, swap(send1), put[0], whole)
-    d_mate, x_near, y_near, c_near, c_mate, mid1, out = together(
-        (d_mate, x_near, y_near, c_near, c_mate, mid1, out)
-    )
-
-    x_mate, d_near, pair3, mid3 = along_x(c_mate), along_y(x_near), pair_z(mid1), mid_z(d_mate)
-    out, send3 = step(out, left, 2, [((c_near,), (x_near,)), ((y_mate,), (d_mate,))], sends=True)
-    out = place(out, swap(send2), put[1], whole)
-    x_mate, d_near, pair3, mid1, mid3, out = together((x_mate, d_near, pair3, mid1, mid3, out))
-
-    d_far = pair_z(mid3)
-    c_far = pair3 + mid1
-    x_far, y_far = along_x(c_far), along_y(c_far)
-    out, send4 = step(out, left, 3, [((c_mate,), (x_mate,)), ((y_near,), (d_near,))], sends=True)
-    out = place(out, swap(send3), put[2], whole)
+
+    c_near = choose(outer, after(pair1, left), mid0)
+    d_mate = pair_z(after(d_self, pair1, left))
+    y_near = along_y(after(c_near, y_mate))
+    x_near = along_x(after(c_near, d_self))
+    out, send2 = step(None, left, 0, [((c,), (x_self,)), ((y_self,), (d_self,))], diagonal=0, sends=True)
+
+    pair3 = pair_z(after(mid1, d_mate, out))
+    mid3 = mid_z(after(d_mate, out))
+    d_near = along_y(after(x_near, y_near))
+    x_mate = along_x(after(c_mate, x_near))
+    out, send3 = step(out, left, 1, [((c_near,), (x_near,)), ((y_mate,), (d_mate,))], sends=True)
+    out = place(out, swap(send2), put[0], whole)
+
+    c_far = choose(outer, after(pair3, out), mid1)
+    x_far = along_x(after(c_far, x_mate))
+    d_far = pair_z(after(mid3, pair3, out))
+    y_far = along_y(after(c_far, d_near))
+    out, send4 = step(out, left, 2, [((c_mate,), (x_mate,)), ((y_near,), (d_near,))], sends=True)
+    out = place(out, swap(send3), put[1], whole)
     c_far_o = swap(c_far)
     x_far, y_far, d_far, c_far, c_far_o, mid3, out = together((x_far, y_far, d_far, c_far, c_far_o, mid3, out))
 
-    out = step(out, left, 4, [((c_far,), (x_far,)), ((y_far,), (d_far, mid3))])
-    pairs = [((c_far_o,), (swap(x_far),)), ((swap(y_far),), (swap(d_far + mid3),))]
-    return step(out, left, 5, pairs, received=swap(send4), placed=whole)
+    out = step(out, left, 3, [((c_far,), (x_far,)), ((y_far,), (d_far, mid3))])
+    pairs = [((c_far_o,), (swap(x_far),)), ((swap(y_far),), (swap(d_far), swap(mid3)))]
+    return step(out, left, 4, pairs, received=swap(send4), placed=whole)
 
 
 def solution(mesh):

time: 233 us -> 217 us (0.931)
  other arithmetic: 9.79 us -> 3.23 us
  Pallas kernels: 93.7 us -> 89.6 us
  waiting for transfers between devices: 92.4 us -> 89.7 us
    ppermute x5, waiting for transfers between devices: 73.2 us -> 46.3 us  [rounds(): along_x = lambda v: lax.ppermute(v, 'grp', [(0, 1), (1, 0)])]
    ppermute x5, waiting for transfers between devices: 15.3 us -> 31.5 us  [rounds(): pair_z = lambda v: lax.ppermute(v, 'loop', [(i, i ^ 4) for i in range(16)])]
    ppermute x5, waiting for transfers between devices: 3.84 us -> 11.2 us  [rounds(): along_y = lambda v: lax.ppermute(v, 'loop', [(i, i ^ 2) for i in range(16)])]
    add x3 -> x0, other arithmetic: 7.37 us -> none  [the longest x1 2.81 us: rounds(): c_near = pair1 + mid0]
    pallas_call x6 -> x5, Pallas kernels: 78.6 us -> 71.4 us  [panels(): pl.pallas_call(functools.partial(panel_kernel, sizes, diagonal, part or (...]
    pallas_call x0 -> x2, Pallas kernels: none -> 5.19 us  [choose(): pl.pallas_call(choose_kernel, out_shape=jax.ShapeDtypeStruct(first.shape,...]
    ppermute x5, starting transfers between devices: 15.1 us -> 12.2 us  [rounds(): pair_z = lambda v: lax.ppermute(v, 'loop', [(i, i ^ 4) for i in range(16)])]
    pallas_call x3 -> x2, Pallas kernels: 10.1 us -> 8.6 us  [place(): pl.pallas_call(functools.partial(place_kernel, placed), out_shape=jax.Sha...]
  transfers between devices with their start and end apart: 28 -> 28, of which waited for: 14 -> 11; matrix products, arithmetic and copies ran while one was open for 5% -> 3% of each run, Pallas kernels for 35% -> 36%
where the time goes in v3:
time: 217 us; the launch traced here: 216 us
  waiting for transfers between devices  89.7 us (41%)
  Pallas kernels  89.6 us (41%)
  starting transfers between devices  29.8 us (14%)
  local copies, waits for them, and re-layouts  3.68 us (2%)
  other arithmetic  3.23 us (1%)
    pallas_call x5, Pallas kernels, panels(): pl.pallas_call(functools.partial(panel_kernel, sizes, diagonal, part or (...  71.4 us
    ppermute x5, waiting for transfers between devices, rounds(): along_x = lambda v: lax.ppermute(v, 'grp', [(0, 1), (1, 0)])  46.3 us
    ppermute x5, waiting for transfers between devices, rounds(): pair_z = lambda v: lax.ppermute(v, 'loop', [(i, i ^ 4) for i in range(16)])  31.5 us
    ppermute x5, starting transfers between devices, rounds(): pair_z = lambda v: lax.ppermute(v, 'loop', [(i, i ^ 4) for i in range(16)])  12.2 us
    ppermute x5, waiting for transfers between devices, rounds(): along_y = lambda v: lax.ppermute(v, 'loop', [(i, i ^ 2) for i in range(16)])  11.2 us
    pallas_call x2, Pallas kernels, place(): pl.pallas_call(functools.partial(place_kernel, placed), out_shape=jax.Sha...  8.6 us
    ppermute x5, starting transfers between devices, rounds(): along_y = lambda v: lax.ppermute(v, 'loop', [(i, i ^ 2) for i in range(16)])  6.8 us
    ppermute x5, starting transfers between devices, rounds(): along_x = lambda v: lax.ppermute(v, 'grp', [(0, 1), (1, 0)])  5.99 us
  transfers between devices with their start and end apart: 28, of which 11 were waited for; matrix products, arithmetic and copies ran while one was open for 3% of the time, Pallas kernels for 36%

profile of v3, /device:TPU:0, one launch (start us, length us, event | category | flops | bytes accessed | tf_op | source)
XLA Modules:
  0.0 216.3 jit_solution(10603641399628052123)
XLA Ops:
  0.0 0.7 collective-permute-start
  0.8 3.0 %collective-permute-start.2 = (f32[384,1024]{1,0:T(8,128)}, f32[384,1024]{1,0:T(8,128)}, u32[]{:S(2)}, u32[]{:S(2)}) collective-permute-start(f32[384,1024]{1,0:T(8,128)} %refs_1_.1), channel_id=1, source_target_pairs={{0,1},{1,0},{2,3},{3,2},{4,5},{5,4},{6,7},{7,6},{8,9},{9,8},{10,11... | collective-permute-start | bytes 4718600 | tf_op jit(solution)/shard_map/ppermute | solution.py:270
  3.8 1.5 collective-permute-start.6
  5.3 4.3 %collective-permute-start.4 = (f32[384,1024]{1,0:T(8,128)}, f32[384,1024]{1,0:T(8,128)}, u32[]{:S(2)}, u32[]{:S(2)}) collective-permute-start(f32[384,1024]{1,0:T(8,128)} %refs_1_.1), channel_id=1, source_target_pairs={{0,8},{2,10},{4,12},{6,14},{8,0},{10,2},{12,4},{14,6},{16,24},{18,... | collective-permute-start | bytes 4718600 | tf_op jit(solution)/shard_map/ppermute | solution.py:272
  9.6 1.2 constant_dynamic-slice_fusion.1.refs_0_
  11.0 0.6 pad_add_fusion.6.ids_ref
  11.6 0.7 pad_add_fusion.ids_ref
  12.3 0.6 pad_add_fusion.4.ids_ref
  12.9 0.7 pad_add_fusion.3
  13.6 0.7 pad_add_fusion.1
  14.3 24.2 %collective-permute-done.2.refs_2_ = f32[384,1024]{1,0:T(8,128)} collective-permute-done((f32[384,1024]{1,0:T(8,128)}, f32[384,1024]{1,0:T(8,128)}, u32[]{:S(2)}, u32[]{:S(2)}) %collective-permute-start.2) | collective-permute-done | bytes 1572896 | tf_op jit(solution)/shard_map/ppermute | solution.py:270
  38.5 1.5 collective-permute-done.6.refs_3_
  40.3 3.2 %collective-permute-done.4.refs_1_ = f32[384,1024]{1,0:T(8,128)} collective-permute-done((f32[384,1024]{1,0:T(8,128)}, f32[384,1024]{1,0:T(8,128)}, u32[]{:S(2)}, u32[]{:S(2)}) %collective-permute-start.4) | collective-permute-done | bytes 1572896 | tf_op jit(solution)/shard_map/ppermute | solution.py:272
  43.5 1.7 collective-permute-start.8
  45.2 0.8 collective-permute-start.13
  46.0 1.2 constant_dynamic-slice_fusion.refs_1_
  47.3 1.9 collective-permute-start.5
  49.1 0.5 collective-permute-done.3.refs_3_
  49.7 4.4 %left_operand.1.refs_0_ = bf16[1024,1536]{1,0:T(8,128)(2,1)} custom-call(f32[384,512]{1,0:T(8,128)} %copy-done, f32[384,512]{1,0:T(8,128)} %copy-done.1, f32[384,512]{1,0:T(8,128)} %copy-done.4, f32[384,512]{1,0:T(8,128)} %collective-permute-done.3.refs_3_), custom_call_target="tpu_custom_call" | custom-call | flops 1024 | bytes 1024 | tf_op jit(solution)/shard_map/left_operand/pallas_call | solution.py:35
  54.1 21.1 %collective-permute-done.7.refs_4_ = f32[384,1024]{1,0:T(8,128)} collective-permute-done((f32[384,1024]{1,0:T(8,128)}, f32[384,1024]{1,0:T(8,128)}, u32[]{:S(2)}, u32[]{:S(2)}) %collective-permute-start.7) | collective-permute-done | bytes 1572896 | tf_op jit(solution)/shard_map/ppermute | solution.py:270
  75.2 3.0 %collective-permute-done.8.first_ref = f32[384,1024]{1,0:T(8,128)} collective-permute-done((f32[384,1024]{1,0:T(8,128)S(1)}, f32[384,1024]{1,0:T(8,128)}, u32[]{:S(2)}, u32[]{:S(2)}) %collective-permute-start.8) | collective-permute-done | bytes 1572896 | tf_op jit(solution)/shard_map/ppermute | solution.py:272
  78.2 1.4 collective-permute-start.9
  79.7 2.6 %choose.2.refs_1_ = f32[384,1024]{1,0:T(8,128)} custom-call(s32[1]{0:T(128)} %bitcast.17.flag_ref, f32[384,1024]{1,0:T(8,128)} %collective-permute-done.8.first_ref, f32[384,1024]{1,0:T(8,128)} %copy-done.2), custom_call_target="tpu_custom_call" | custom-call | bytes 1572864 | tf_op jit(solution)/shard_map/choose/pallas_call | solution.py:237
  82.3 0.9 collective-permute-start.12
  83.1 1.5 collective-permute-start.16
  84.7 16.2 %panels.5 = (f32[512,16384]{1,0:T(8,128)}, f32[2,512,1024]{2,1,0:T(8,128)}) custom-call(s32[3]{0:T(128)} %pad_add_fusion.ids_ref, bf16[1024,1536]{1,0:T(8,128)(2,1)} %left_operand.1.refs_0_, f32[384,1024]{1,0:T(8,128)} %refs_1_.1, f32[384,1024]{1,0:T(8,128)} %collective-permute-done.2.refs_2_, f32[384,1024]{1,0:T(8,128)} %collective-permute-done.6.refs_3_, ...), custom_call_target="tpu_custom_call" | custom-call | flops 96636764160 | bytes 14680064 | tf_op jit(solution)/shard_map/panels/pallas_call | solution.py:159
  101.0 11.2 %collective-permute-done.9.refs_4_ = f32[384,1024]{1,0:T(8,128)S(1)} collective-permute-done((f32[384,1024]{1,0:T(8,128)}, f32[384,1024]{1,0:T(8,128)S(1)}, u32[]{:S(2)}, u32[]{:S(2)}) %collective-permute-start.9) | collective-permute-done | bytes 1572896 | tf_op jit(solution)/shard_map/ppermute | solution.py:272
  112.2 1.2 copy-done.7
  113.4 0.8 collective-permute-start.19
  114.2 2.8 %collective-permute-start.10 = (f32[384,1024]{1,0:T(8,128)}, f32[384,1024]{1,0:T(8,128)S(1)}, u32[]{:S(2)}, u32[]{:S(2)}) collective-permute-start(f32[384,1024]{1,0:T(8,128)} %collective-permute-done.5.second_ref), channel_id=1, source_target_pairs={{0,8},{2,10},{4,12},{6,14},{8,0},{10,2},{12,4},{14,6},{16,24},{18,... | collective-permute-start | bytes 4718600 | tf_op jit(solution)/shard_map/ppermute | solution.py:272
  117.0 1.6 collective-permute-start.17
  118.6 0.7 collective-permute-start.14
  119.3 16.2 %panels.6 = (f32[512,16384]{1,0:T(8,128)}, f32[2,512,1024]{2,1,0:T(8,128)}) custom-call(s32[2]{0:T(128)} %get-tuple-element.57.ids_ref, bf16[1024,1536]{1,0:T(8,128)(2,1)} %left_operand.1.refs_0_, f32[384,1024]{1,0:T(8,128)} %choose.2.refs_1_, f32[384,1024]{1,0:T(8,128)} %collective-permute-done.12.refs_2_, ...), custom_call_target="tpu_custom_call", output_to_operand_aliasing={{0}: (6, {})} | custom-call | flops 96636764160 | bytes 14680064 | tf_op jit(solution)/shard_map/panels/pallas_call | solution.py:159
  135.6 4.3 %place.2.refs_5_ = f32[512,16384]{1,0:T(8,128)} custom-call(s32[2]{0:T(128)} %get-tuple-element.55.ids_ref, f32[2,512,1024]{2,1,0:T(8,128)} %collective-permute-done.11.received_ref, f32[512,16384]{1,0:T(8,128)} %get-tuple-element.61._), custom_call_target="tpu_custom_call", output_to_operand_aliasing={{}: (2, {})} | custom-call | bytes 8388608 | tf_op jit(solution)/shard_map/place/pallas_call | solution.py:205
  139.9 9.7 %collective-permute-done.10.first_ref = f32[384,1024]{1,0:T(8,128)S(1)} collective-permute-done((f32[384,1024]{1,0:T(8,128)}, f32[384,1024]{1,0:T(8,128)S(1)}, u32[]{:S(2)}, u32[]{:S(2)}) %collective-permute-start.10) | collective-permute-done | bytes 1572896 | tf_op jit(solution)/shard_map/ppermute | solution.py:272
  149.6 1.9 collective-permute-start.20
  151.6 2.6 %choose.3.refs_1_ = f32[384,1024]{1,0:T(8,128)} custom-call(s32[1]{0:T(128)} %bitcast.17.flag_ref, f32[384,1024]{1,0:T(8,128)} %copy-done.3, f32[384,1024]{1,0:T(8,128)} %collective-permute-done.5.second_ref), custom_call_target="tpu_custom_call" | custom-call | bytes 1572864 | tf_op jit(solution)/shard_map/choose/pallas_call | solution.py:237
  154.3 1.3 collective-permute-start.18
  155.6 1.1 collective-permute-start.15
  156.6 16.2 %panels.7 = (f32[512,16384]{1,0:T(8,128)}, f32[2,512,1024]{2,1,0:T(8,128)}) custom-call(s32[2]{0:T(128)} %get-tuple-element.72.ids_ref, bf16[1024,1536]{1,0:T(8,128)(2,1)} %left_operand.1.refs_0_, f32[384,1024]{1,0:T(8,128)} %collective-permute-done.4.refs_1_, f32[384,1024]{1,0:T(8,128)} %collective-permute-done.14.refs_2_, ...), custom_call_target="tpu_custom_call", output_to_operand_aliasing={{0}: (6, {})} | custom-call | flops 96636764160 | bytes 14680064 | tf_op jit(solution)/shard_map/panels/pallas_call | solution.py:159
  172.9 4.3 %place.3.refs_6_ = f32[512,16384]{1,0:T(8,128)} custom-call(s32[2]{0:T(128)} %pad_add_fusion.6.ids_ref, f32[2,512,1024]{2,1,0:T(8,128)} %collective-permute-done.22.received_ref, f32[512,16384]{1,0:T(8,128)} %get-tuple-element.73._), custom_call_target="tpu_custom_call", output_to_operand_aliasing={{}: (2, {})} | custom-call | bytes 8388608 | tf_op jit(solution)/shard_map/place/pallas_call | solution.py:205
  177.2 4.4 %collective-permute-done.20.refs_4_ = f32[384,1024]{1,0:T(8,128)} collective-permute-done((f32[384,1024]{1,0:T(8,128)S(1)}, f32[384,1024]{1,0:T(8,128)}, u32[]{:S(2)}, u32[]{:S(2)}) %collective-permute-start.20) | collective-permute-done | bytes 1572896 | tf_op jit(solution)/shard_map/ppermute | solution.py:272
  181.6 9.8 %collective-permute-done.18.refs_3_ = f32[384,1024]{1,0:T(8,128)} collective-permute-done((f32[384,1024]{1,0:T(8,128)}, f32[384,1024]{1,0:T(8,128)}, u32[]{:S(2)}, u32[]{:S(2)}) %collective-permute-start.18) | collective-permute-done | bytes 1572896 | tf_op jit(solution)/shard_map/ppermute | solution.py:271
  191.4 1.0 collective-permute-done.15.refs_2_
  192.4 0.5 collective-permute-start.24
  193.0 0.4 collective-permute-start.26
  193.4 10.5 %panels.8.refs_7_ = f32[512,16384]{1,0:T(8,128)} custom-call(s32[2]{0:T(128)} %get-tuple-element.80.ids_ref, bf16[1024,1536]{1,0:T(8,128)(2,1)} %left_operand.1.refs_0_, f32[384,1024]{1,0:T(8,128)} %choose.3.refs_1_, f32[384,1024]{1,0:T(8,128)} %collective-permute-done.15.refs_2_, ...), custom_call_target="tpu_custom_call", output_to_operand_aliasing={{}: (7, {})} | custom-call | flops 48318382080 | bytes 10485760 | tf_op jit(solution)/shard_map/panels/pallas_call | solution.py:159
  204.0 12.3 %panels.9 = f32[512,16384]{1,0:T(8,128)} custom-call(s32[4]{0:T(128)} %pad_add_fusion.4.ids_ref, bf16[1024,1536]{1,0:T(8,128)(2,1)} %left_operand.1.refs_0_, f32[384,1024]{1,0:T(8,128)} %copy-done.6, f32[384,1024]{1,0:T(8,128)} %collective-permute-done.23.refs_2_, f32[384,1024]{1,0:T(8,128)} %collective-permute-done.24.refs_3_, ...), custom_call_target="tpu_custom_call", output_to_operand_aliasing={{}: (8, {})} | custom-call | flops 48318382080 | bytes 10485760 | tf_op jit(solution)/shard_map/panels/pallas_call | solution.py:159
  (41 shorter events, 1.0 us)
Async XLA Ops:
  0.0 14.2 %collective-permute-start = (f32[384,1024]{1,0:T(8,128)}, f32[384,1024]{1,0:T(8,128)S(1)}, u32[]{:S(2)}, u32[]{:S(2)}) collective-permute-start(f32[384,1024]{1,0:T(8,128)} %refs_1_.1), channel_id=1, source_target_pairs={{8,16},{10,18},{12,20},{14,22},{16,8},{18,10},{20,12},{22,14},{9,1... | collective-permute-start | bytes 4718600 | tf_op jit(solution)/shard_map/ppermute | solution.py:273
  0.8 37.7 %collective-permute-start.2 = (f32[384,1024]{1,0:T(8,128)}, f32[384,1024]{1,0:T(8,128)}, u32[]{:S(2)}, u32[]{:S(2)}) collective-permute-start(f32[384,1024]{1,0:T(8,128)} %refs_1_.1), channel_id=1, source_target_pairs={{0,1},{1,0},{2,3},{3,2},{4,5},{5,4},{6,7},{7,6},{8,9},{9,8},{10,11... | collective-permute-start | bytes 4718600 | tf_op jit(solution)/shard_map/ppermute | solution.py:270
  3.8 36.2 %collective-permute-start.6 = (f32[384,1024]{1,0:T(8,128)}, f32[384,1024]{1,0:T(8,128)}, u32[]{:S(2)}, u32[]{:S(2)}) collective-permute-start(f32[384,1024]{1,0:T(8,128)} %refs_1_.1), channel_id=1, source_target_pairs={{0,4},{2,6},{4,0},{6,2},{8,12},{10,14},{12,8},{14,10},{16,20},{18,... | collective-permute-start | bytes 4718600 | tf_op jit(solution)/shard_map/ppermute | solution.py:271
  5.3 38.2 %collective-permute-start.4 = (f32[384,1024]{1,0:T(8,128)}, f32[384,1024]{1,0:T(8,128)}, u32[]{:S(2)}, u32[]{:S(2)}) collective-permute-start(f32[384,1024]{1,0:T(8,128)} %refs_1_.1), channel_id=1, source_target_pairs={{0,8},{2,10},{4,12},{6,14},{8,0},{10,2},{12,4},{14,6},{16,24},{18,... | collective-permute-start | bytes 4718600 | tf_op jit(solution)/shard_map/ppermute | solution.py:272
  10.8 38.9 %copy-start = (f32[384,512]{1,0:T(8,128)}, f32[384,512]{1,0:T(8,128)S(1)}, u32[]{:S(2)}) copy-start(f32[384,512]{1,0:T(8,128)S(1)} %constant_dynamic-slice_fusion.1.refs_0_) | copy-start | bytes 2359300
  10.8 3.4 %collective-permute-start.1 = (f32[384,512]{1,0:T(8,128)S(1)}, f32[384,512]{1,0:T(8,128)S(1)}, u32[]{:S(2)}, u32[]{:S(2)}) collective-permute-start(f32[384,512]{1,0:T(8,128)S(1)} %constant_dynamic-slice_fusion.1.refs_0_), channel_id=1, source_target_pairs={{0,2},{2,0},{4,6},{6,4},{8,10},{10,8},{12,14},{14,12},{16,18},{18,... | collective-permute-start | bytes 2359304 | tf_op jit(solution)/shard_map/ppermute | solution.py:276
  14.2 35.5 %copy-start.4 = (f32[384,512]{1,0:T(8,128)}, f32[384,512]{1,0:T(8,128)S(1)}, u32[]{:S(2)}) copy-start(f32[384,512]{1,0:T(8,128)S(1)} %collective-permute-done.1.refs_2_) | copy-start | bytes 2359300
  14.2 65.4 %copy-start.2 = (f32[384,1024]{1,0:T(8,128)}, f32[384,1024]{1,0:T(8,128)S(1)}, u32[]{:S(2)}) copy-start(f32[384,1024]{1,0:T(8,128)S(1)} %collective-permute-done.second_ref) | copy-start | bytes 4718596
  39.9 35.3 %collective-permute-start.7 = (f32[384,1024]{1,0:T(8,128)}, f32[384,1024]{1,0:T(8,128)}, u32[]{:S(2)}, u32[]{:S(2)}) collective-permute-start(f32[384,1024]{1,0:T(8,128)} %collective-permute-done.6.refs_3_), channel_id=1, source_target_pairs={{0,1},{1,0},{2,3},{3,2},{4,5},{5,4},{6,7},{7,6},{8,9},{9,8},{10,11... | collective-permute-start | bytes 4718600 | tf_op jit(solution)/shard_map/ppermute | solution.py:270
  43.5 34.8 %collective-permute-start.8 = (f32[384,1024]{1,0:T(8,128)S(1)}, f32[384,1024]{1,0:T(8,128)}, u32[]{:S(2)}, u32[]{:S(2)}) collective-permute-start(f32[384,1024]{1,0:T(8,128)S(1)} %collective-permute-done.second_ref), channel_id=1, source_target_pairs={{0,8},{2,10},{4,12},{6,14},{8,0},{10,2},{12,4},{14,6},{16,24},{18,... | collective-permute-start | bytes 4718600 | tf_op jit(solution)/shard_map/ppermute | solution.py:272
  45.2 37.9 %collective-permute-start.13 = (f32[384,1024]{1,0:T(8,128)}, f32[384,1024]{1,0:T(8,128)}, u32[]{:S(2)}, u32[]{:S(2)}) collective-permute-start(f32[384,1024]{1,0:T(8,128)} %collective-permute-done.4.refs_1_), channel_id=1, source_target_pairs={{0,4},{2,6},{4,0},{6,2},{8,12},{10,14},{12,8},{14,10},{16,20},{18,... | collective-permute-start | bytes 4718600 | tf_op jit(solution)/shard_map/ppermute | solution.py:271
  47.2 2.5 %copy-start.1 = (f32[384,512]{1,0:T(8,128)}, f32[384,512]{1,0:T(8,128)S(1)}, u32[]{:S(2)}) copy-start(f32[384,512]{1,0:T(8,128)S(1)} %constant_dynamic-slice_fusion.refs_1_) | copy-start | bytes 2359300
  47.2 2.5 %collective-permute-start.3 = (f32[384,512]{1,0:T(8,128)S(1)}, f32[384,512]{1,0:T(8,128)}, u32[]{:S(2)}, u32[]{:S(2)}) collective-permute-start(f32[384,512]{1,0:T(8,128)S(1)} %constant_dynamic-slice_fusion.refs_1_), channel_id=1, source_target_pairs={{0,2},{2,0},{4,6},{6,4},{8,10},{10,8},{12,14},{14,12},{16,18},{18,... | collective-permute-start | bytes 2359304 | tf_op jit(solution)/shard_map/ppermute | solution.py:276
  47.3 66.1 %collective-permute-start.5 = (f32[384,1024]{1,0:T(8,128)}, f32[384,1024]{1,0:T(8,128)}, u32[]{:S(2)}, u32[]{:S(2)}) collective-permute-start(f32[384,1024]{1,0:T(8,128)} %collective-permute-done.4.refs_1_), channel_id=1, source_target_pairs={{8,16},{10,18},{12,20},{14,22},{16,8},{18,10},{20,12},{22,14},{9,1... | collective-permute-start | bytes 4718600 | tf_op jit(solution)/shard_map/ppermute | solution.py:273
  78.2 33.9 %collective-permute-start.9 = (f32[384,1024]{1,0:T(8,128)}, f32[384,1024]{1,0:T(8,128)S(1)}, u32[]{:S(2)}, u32[]{:S(2)}) collective-permute-start(f32[384,1024]{1,0:T(8,128)} %collective-permute-done.7.refs_4_), channel_id=1, source_target_pairs={{0,8},{2,10},{4,12},{6,14},{8,0},{10,2},{12,4},{14,6},{16,24},{18,... | collective-permute-start | bytes 4718600 | tf_op jit(solution)/shard_map/ppermute | solution.py:272
  82.3 34.7 %collective-permute-start.12 = (f32[384,1024]{1,0:T(8,128)}, f32[384,1024]{1,0:T(8,128)}, u32[]{:S(2)}, u32[]{:S(2)}) collective-permute-start(f32[384,1024]{1,0:T(8,128)} %choose.2.refs_1_), channel_id=1, source_target_pairs={{0,1},{1,0},{2,3},{3,2},{4,5},{5,4},{6,7},{7,6},{8,9},{9,8},{10,11... | collective-permute-start | bytes 4718600 | tf_op jit(solution)/shard_map/ppermute | solution.py:270
  83.1 33.9 %collective-permute-start.16 = (f32[384,1024]{1,0:T(8,128)}, f32[384,1024]{1,0:T(8,128)}, u32[]{:S(2)}, u32[]{:S(2)}) collective-permute-start(f32[384,1024]{1,0:T(8,128)} %choose.2.refs_1_), channel_id=1, source_target_pairs={{0,4},{2,6},{4,0},{6,2},{8,12},{10,14},{12,8},{14,10},{16,20},{18,... | collective-permute-start | bytes 4718600 | tf_op jit(solution)/shard_map/ppermute | solution.py:271
  100.9 34.6 %collective-permute-start.11 = (f32[2,512,1024]{2,1,0:T(8,128)}, f32[2,512,1024]{2,1,0:T(8,128)}, u32[]{:S(2)}, u32[]{:S(2)}) collective-permute-start(f32[2,512,1024]{2,1,0:T(8,128)} %get-tuple-element.56), channel_id=1, source_target_pairs={{0,2},{2,0},{4,6},{6,4},{8,10},{10,8},{12,14},{14,12},{16,18},{18,... | collective-permute-start | bytes 12582920 | tf_op jit(solution)/shard_map/ppermute | solution.py:276
  112.2 1.2 copy-start.7
  113.4 26.5 %collective-permute-start.19 = (f32[384,1024]{1,0:T(8,128)}, f32[384,1024]{1,0:T(8,128)S(1)}, u32[]{:S(2)}, u32[]{:S(2)}) collective-permute-start(f32[384,1024]{1,0:T(8,128)} %copy-done.7), channel_id=1, source_target_pairs={{8,16},{10,18},{12,20},{14,22},{16,8},{18,10},{20,12},{22,14},{9,1... | collective-permute-start | bytes 4718600 | tf_op jit(solution)/shard_map/ppermute | solution.py:273
  114.2 35.5 %collective-permute-start.10 = (f32[384,1024]{1,0:T(8,128)}, f32[384,1024]{1,0:T(8,128)S(1)}, u32[]{:S(2)}, u32[]{:S(2)}) collective-permute-start(f32[384,1024]{1,0:T(8,128)} %collective-permute-done.5.second_ref), channel_id=1, source_target_pairs={{0,8},{2,10},{4,12},{6,14},{8,0},{10,2},{12,4},{14,6},{16,24},{18,... | collective-permute-start | bytes 4718600 | tf_op jit(solution)/shard_map/ppermute | solution.py:272
  117.0 37.3 %collective-permute-start.17 = (f32[384,1024]{1,0:T(8,128)}, f32[384,1024]{1,0:T(8,128)}, u32[]{:S(2)}, u32[]{:S(2)}) collective-permute-start(f32[384,1024]{1,0:T(8,128)} %collective-permute-done.12.refs_2_), channel_id=1, source_target_pairs={{0,4},{2,6},{4,0},{6,2},{8,12},{10,14},{12,8},{14,10},{16,20},{18,... | collective-permute-start | bytes 4718600 | tf_op jit(solution)/shard_map/ppermute | solution.py:271
  118.6 37.0 %collective-permute-start.14 = (f32[384,1024]{1,0:T(8,128)}, f32[384,1024]{1,0:T(8,128)}, u32[]{:S(2)}, u32[]{:S(2)}) collective-permute-start(f32[384,1024]{1,0:T(8,128)} %collective-permute-done.4.refs_1_), channel_id=1, source_target_pairs={{0,1},{1,0},{2,3},{3,2},{4,5},{5,4},{6,7},{7,6},{8,9},{9,8},{10,11... | collective-permute-start | bytes 4718600 | tf_op jit(solution)/shard_map/ppermute | solution.py:270
  135.5 37.3 %collective-permute-start.22 = (f32[2,512,1024]{2,1,0:T(8,128)}, f32[2,512,1024]{2,1,0:T(8,128)}, u32[]{:S(2)}, u32[]{:S(2)}) collective-permute-start(f32[2,512,1024]{2,1,0:T(8,128)} %get-tuple-element.71), channel_id=1, source_target_pairs={{0,2},{2,0},{4,6},{6,4},{8,10},{10,8},{12,14},{14,12},{16,18},{18,... | collective-permute-start | bytes 12582920 | tf_op jit(solution)/shard_map/ppermute | solution.py:276
  139.9 53.1 %copy-start.5 = (f32[384,1024]{1,0:T(8,128)}, f32[384,1024]{1,0:T(8,128)S(1)}, u32[]{:S(2)}) copy-start(f32[384,1024]{1,0:T(8,128)S(1)} %collective-permute-done.19.refs_5_) | copy-start | bytes 4718596
  149.6 1.9 copy-start.3
  149.6 32.0 %collective-permute-start.20 = (f32[384,1024]{1,0:T(8,128)S(1)}, f32[384,1024]{1,0:T(8,128)}, u32[]{:S(2)}, u32[]{:S(2)}) collective-permute-start(f32[384,1024]{1,0:T(8,128)S(1)} %collective-permute-done.19.refs_5_), channel_id=1, source_target_pairs={{0,8},{2,10},{4,12},{6,14},{8,0},{10,2},{12,4},{14,6},{16,24},{18,... | collective-permute-start | bytes 4718600 | tf_op jit(solution)/shard_map/ppermute | solution.py:272
  154.2 38.2 %collective-permute-start.21 = (f32[384,1024]{1,0:T(8,128)}, f32[384,1024]{1,0:T(8,128)S(1)}, u32[]{:S(2)}, u32[]{:S(2)}) collective-permute-start(f32[384,1024]{1,0:T(8,128)} %choose.3.refs_1_), channel_id=1, source_target_pairs={{0,2},{2,0},{4,6},{6,4},{8,10},{10,8},{12,14},{14,12},{16,18},{18,... | collective-permute-start | bytes 4718600 | tf_op jit(solution)/shard_map/ppermute | solution.py:276
  154.3 37.1 %collective-permute-start.18 = (f32[384,1024]{1,0:T(8,128)}, f32[384,1024]{1,0:T(8,128)}, u32[]{:S(2)}, u32[]{:S(2)}) collective-permute-start(f32[384,1024]{1,0:T(8,128)} %choose.3.refs_1_), channel_id=1, source_target_pairs={{0,4},{2,6},{4,0},{6,2},{8,12},{10,14},{12,8},{14,10},{16,20},{18,... | collective-permute-start | bytes 4718600 | tf_op jit(solution)/shard_map/ppermute | solution.py:271
  155.6 36.8 %collective-permute-start.15 = (f32[384,1024]{1,0:T(8,128)}, f32[384,1024]{1,0:T(8,128)}, u32[]{:S(2)}, u32[]{:S(2)}) collective-permute-start(f32[384,1024]{1,0:T(8,128)} %choose.3.refs_1_), channel_id=1, source_target_pairs={{0,1},{1,0},{2,3},{3,2},{4,5},{5,4},{6,7},{7,6},{8,9},{9,8},{10,11... | collective-permute-start | bytes 4718600 | tf_op jit(solution)/shard_map/ppermute | solution.py:270
  172.8 31.2 %collective-permute-start.27 = (f32[2,512,1024]{2,1,0:T(8,128)}, f32[2,512,1024]{2,1,0:T(8,128)}, u32[]{:S(2)}, u32[]{:S(2)}) collective-permute-start(f32[2,512,1024]{2,1,0:T(8,128)} %get-tuple-element.79), channel_id=1, source_target_pairs={{0,2},{2,0},{4,6},{6,4},{8,10},{10,8},{12,14},{14,12},{16,18},{18,... | collective-permute-start | bytes 12582920 | tf_op jit(solution)/shard_map/ppermute | solution.py:276
  192.4 11.6 %copy-start.6 = (f32[384,1024]{1,0:T(8,128)}, f32[384,1024]{1,0:T(8,128)S(1)}, u32[]{:S(2)}) copy-start(f32[384,1024]{1,0:T(8,128)S(1)} %collective-permute-done.21.refs_1_) | copy-start | bytes 4718596
  192.4 11.6 %collective-permute-start.23 = (f32[384,1024]{1,0:T(8,128)}, f32[384,1024]{1,0:T(8,128)}, u32[]{:S(2)}, u32[]{:S(2)}) collective-permute-start(f32[384,1024]{1,0:T(8,128)} %collective-permute-done.15.refs_2_), channel_id=1, source_target_pairs={{0,2},{2,0},{4,6},{6,4},{8,10},{10,8},{12,14},{14,12},{16,18},{18,... | collective-permute-start | bytes 4718600 | tf_op jit(solution)/shard_map/ppermute | solution.py:276
  192.4 11.6 %collective-permute-start.24 = (f32[384,1024]{1,0:T(8,128)}, f32[384,1024]{1,0:T(8,128)}, u32[]{:S(2)}, u32[]{:S(2)}) collective-permute-start(f32[384,1024]{1,0:T(8,128)} %collective-permute-done.18.refs_3_), channel_id=1, source_target_pairs={{0,2},{2,0},{4,6},{6,4},{8,10},{10,8},{12,14},{14,12},{16,18},{18,... | collective-permute-start | bytes 4718600 | tf_op jit(solution)/shard_map/ppermute | solution.py:276
  192.9 11.1 %collective-permute-start.25 = (f32[384,1024]{1,0:T(8,128)}, f32[384,1024]{1,0:T(8,128)}, u32[]{:S(2)}, u32[]{:S(2)}) collective-permute-start(f32[384,1024]{1,0:T(8,128)} %collective-permute-done.20.refs_4_), channel_id=1, source_target_pairs={{0,2},{2,0},{4,6},{6,4},{8,10},{10,8},{12,14},{14,12},{16,18},{18,... | collective-permute-start | bytes 4718600 | tf_op jit(solution)/shard_map/ppermute | solution.py:276
  193.0 11.0 %collective-permute-start.26 = (f32[384,1024]{1,0:T(8,128)S(1)}, f32[384,1024]{1,0:T(8,128)}, u32[]{:S(2)}, u32[]{:S(2)}) collective-permute-start(f32[384,1024]{1,0:T(8,128)S(1)} %collective-permute-done.19.refs_5_), channel_id=1, source_target_pairs={{0,2},{2,0},{4,6},{6,4},{8,10},{10,8},{12,14},{14,12},{16,18},{18,... | collective-permute-start | bytes 4718600 | tf_op jit(solution)/shard_map/ppermute | solution.py:276

commit v4 on v3

v4 whole, which is shorter than its diff:
```python
import functools

import jax
import jax.numpy as jnp
from jax import lax
from jax.experimental import pallas as pl
from jax.experimental.pallas import tpu as pltpu
from jax.sharding import PartitionSpec as P

damping = 0.1
VMEM_BYTES = 63 * 1024 * 1024 + 512 * 1024
COST = 1024


def split_high_low(value):
    high = value.astype(jnp.bfloat16)
    low = (value - high.astype(jnp.float32)).astype(jnp.bfloat16)
    return high, low


def left_kernel(*refs):
    left_ref = refs[-1]
    depth, rows = refs[0].shape
    for block in range(len(refs) // 2):
        for place, ref in enumerate(refs[2 * block : 2 * block + 2]):
            high, low = split_high_low(ref[...].T)
            for part, piece in enumerate((high, low)):
                target = pl.ds(rows * block, rows), pl.ds(2 * depth * part + depth * place, depth)
                left_ref[target] = piece


def left_operand(*halves):
    depth, rows = halves[0].shape
    shape = rows * (len(halves) // 2), 4 * depth
    return pl.pallas_call(
        left_kernel,
        out_shape=jax.ShapeDtypeStruct(shape, jnp.bfloat16),
        compiler_params=pltpu.CompilerParams(vmem_limit_bytes=VMEM_BYTES),
        cost_estimate=pl.CostEstimate(flops=COST, bytes_accessed=COST, transcendentals=0),
        name="left_operand",
    )(*halves)


def panel_kernel(sizes, diagonal, part, placed, width, tile, sends, ids_ref, left_hbm, *refs):
    count = sum(map(sum, sizes))
    blocks, received = refs[:count], refs[count : count + len(placed)]
    left_ref, held, done, left_sem, load_sem, store_sem, place_sem = refs[-7 - len(placed) : len(refs) - len(placed)]
    stages = refs[len(refs) - len(placed) :]
    out_ref, send_ref = refs[-9 - len(placed) : -7 - len(placed)] if sends else (refs[-8 - len(placed)], None)
    rows, (first, whole) = out_ref.shape[0], part
    tiles, panel_count = width // tile, len(sizes)
    turns = panel_count * tiles
    most = max(map(sum, sizes))
    height, depth = done.shape[1], left_ref.shape[1] // 2
    left = [left_ref.at[:, pl.ds(k * depth, depth)] for k in range(2)]
    left_copy = pltpu.make_async_copy(left_hbm.at[pl.ds(0, height)], left_ref, left_sem)

    loads, at = [], 0
    for index, counts in enumerate(sizes):
        loads.append([[] for _ in range(tiles)])
        for place in range(sum(counts)):
            skip = first if blocks[at].shape[1] > width else 0
            for t in range(tiles):
                source = blocks[at].at[:, pl.ds(skip + t * tile, tile)]
                target = held.at[index % 2, place, :, pl.ds(t * tile, tile)]
                loads[index][t].append(pltpu.make_async_copy(source, target, load_sem.at[index % 2, place, t]))
            at += 1
    fetches, puts, at = [], [], panel_count
    for number, (from_ref, stage, (begin, size)) in enumerate(zip(received, stages, placed)):
        for index in range(from_ref.shape[0]):
            column = pl.multiple_of(ids_ref[at] * size + begin, 128)
            target = out_ref.at[:, pl.ds(column, from_ref.shape[-1])]
            fetches.append(pltpu.make_async_copy(from_ref.at[index], stage.at[index], place_sem.at[number, index, 0]))
            puts.append(pltpu.make_async_copy(stage.at[index], target, place_sem.at[number, index, 1]))
            at += 1

    def stores(turn):
        index, column = turn // tiles, pl.multiple_of(lax.rem(turn, tiles) * tile, 128)
        slot = lax.rem(turn, 2)
        place = pl.multiple_of(ids_ref[index] * whole + first + column, 128)
        copies = [(done.at[slot, pl.ds(0, rows)], out_ref.at[:, pl.ds(place, tile)], store_sem.at[slot, 0])]
        if sends:
            target = send_ref.at[index, :, pl.ds(column, tile)]
            copies.append((done.at[slot, pl.ds(rows, rows)], target, store_sem.at[slot, 1]))
        return [pltpu.make_async_copy(*copy) for copy in copies]

    def start(copies):
        for copy in copies:
            copy.start()

    def wait(copies):
        for copy in copies:
            copy.wait()

    start(loads[0][0] + [left_copy])
    for copies in loads[0][1:]:
        start(copies)
    left_copy.wait()

    def turn_body(turn, carry):
        index, column = turn // tiles, pl.multiple_of(lax.rem(turn, tiles) * tile, 128)
        slot = lax.rem(index, 2)
        for here in range(turns):

            @pl.when(turn == here)
            def arrive(here=here):
                wait(loads[here // tiles][here % tiles])
                if here == 0:
                    for copies in loads[1] if panel_count > 1 else []:
                        start(copies)
                    start(fetches)

        @pl.when(turn >= 2)
        def free():
            wait(stores(turn - 2))

        @pl.when(turn == turns // 2)
        def put():
            wait(fetches)
            start(puts)

        block = [held[slot, k, :, pl.ds(column, tile)] for k in range(most)]
        if most > 2:
            extra = functools.reduce(jnp.logical_or, [index == i for i, n in enumerate(sizes) if sum(n) > 2])
            block[1] = block[1] + jnp.where(extra, block[2], 0.0)
        halves = [split_high_low(value) for value in block[:2]]
        high, low = (jnp.concatenate(pieces, axis=0) for pieces in zip(*halves))
        dot = functools.partial(jnp.dot, preferred_element_type=jnp.float32)
        product = dot(left[0][...], high) + dot(left[0][...], low) + dot(left[1][...], high)
        if diagonal is not None:
            row_ids = lax.broadcasted_iota(jnp.int32, product.shape, 0) + ids_ref[ids_ref.shape[0] - 1]
            col_ids = lax.broadcasted_iota(jnp.int32, product.shape, 1) + column
            own = lax.broadcasted_iota(jnp.int32, product.shape, 0) < rows
            hit = (row_ids == col_ids) & own & (index == diagonal)
            product = jnp.where(hit, product * jnp.float32(1.0 + damping), product)
        done[lax.rem(turn, 2)] = product
        start(stores(turn))
        for here in range(panel_count - 2):

            @pl.when(turn == here * tiles + tiles - 1)
            def fetch(later=loads[here + 2]):
                for copies in later:
                    start(copies)

        return carry

    lax.fori_loop(0, turns, turn_body, 0)
    for turn in range(max(0, turns - 2), turns):
        wait(stores(turn))
    wait(puts)


def panels(out, left, rows, columns, pairs, ids, received=(), diagonal=None, part=None, width=None, sends=False):
    depth, width = pairs[0][0][0].shape[0], width or pairs[0][0][0].shape[1]
    sizes = tuple(tuple(len(half) for half in pair) for pair in pairs)
    args = [ids, left] + [array for pair in pairs for half in pair for array in half]
    args += [stack for stack, _ in received]
    aliases = {}
    if out is not None:
        aliases = {len(args): 0}
        args.append(out)
    anywhere = pl.BlockSpec(memory_space=pl.ANY)
    most = max(map(sum, sizes))
    tile = 512 if width % 512 == 0 else min(256, width)
    height = 2 * rows if sends else rows
    shapes = [jax.ShapeDtypeStruct((rows, columns), jnp.float32)]
    if sends:
        shapes.append(jax.ShapeDtypeStruct((len(pairs), rows, width), jnp.float32))
    stacked = max([stack.shape[0] for stack, _ in received], default=1)
    outs = pl.pallas_call(
        functools.partial(
            panel_kernel,
            sizes,
            diagonal,
            part or (0, width),
            tuple(place for _, place in received),
            width,
            tile,
            sends,
        ),
        out_shape=shapes,
        in_specs=[pl.BlockSpec(memory_space=pltpu.SMEM)] + [anywhere] * (len(args) - 1),
        out_specs=[anywhere] * len(shapes),
        scratch_shapes=[
            pltpu.VMEM((height, left.shape[1]), left.dtype),
            pltpu.VMEM((2, most, depth, width), jnp.float32),
            pltpu.VMEM((2, height, tile), jnp.float32),
            pltpu.SemaphoreType.DMA,
            pltpu.SemaphoreType.DMA((2, most, width // tile)),
            pltpu.SemaphoreType.DMA((2, 2)),
            pltpu.SemaphoreType.DMA((max(1, len(received)), stacked, 2)),
            *[pltpu.VMEM(stack.shape, jnp.float32) for stack, _ in received],
        ],
        input_output_aliases=aliases,
        compiler_params=pltpu.CompilerParams(vmem_limit_bytes=VMEM_BYTES),
        cost_estimate=pl.CostEstimate(
            flops=30 * height * left.shape[1] * width * len(pairs),
            bytes_accessed=4 * width * len(pairs) * (height + 2 * depth),
            transcendentals=0,
        ),
        name="panels",
    )(*args)
    return outs if sends else outs[0]


def choose_kernel(jobs, flag_ref, *refs):
    outs = refs[-1 - 2 * len(jobs) : -1 - len(jobs)]
    stages, sems = refs[-1 - len(jobs) : -1], refs[-1]
    pieces = sems.shape[1]
    rows = [pl.ds(k * (stages[0].shape[0] // pieces), stages[0].shape[0] // pieces) for k in range(pieces)]

    def fetch(job, k, pick):
        first, columns = jobs[job], pl.ds(jobs[job][2], stages[job].shape[1])
        return pltpu.make_async_copy(refs[first[pick]].at[rows[k], columns], stages[job].at[rows[k]], sems.at[job, k, 0])

    def put(job, k):
        return pltpu.make_async_copy(stages[job].at[rows[k]], outs[job].at[rows[k]], sems.at[job, k, 1])

    every = [(job, k) for job in range(len(jobs)) for k in range(pieces)]
    for pick in range(2):

        @pl.when(flag_ref[0] == 1 - pick)
        def start(pick=pick):
            for job, k in every:
                fetch(job, k, pick).start()

    for job, k in every:
        fetch(job, k, 0).wait()
        put(job, k).start()
    for job, k in every:
        put(job, k).wait()


def choose(flag, operands, jobs):
    rows = operands[0].shape[0]
    anywhere = pl.BlockSpec(memory_space=pltpu.HBM)
    shapes = [(rows, job[3]) for job in jobs]
    return pl.pallas_call(
        functools.partial(choose_kernel, [job[:3] for job in jobs]),
        out_shape=[jax.ShapeDtypeStruct(shape, jnp.float32) for shape in shapes],
        in_specs=[pl.BlockSpec(memory_space=pltpu.SMEM)] + [anywhere] * len(operands),
        out_specs=[anywhere] * len(jobs),
        scratch_shapes=[pltpu.VMEM(shape, jnp.float32) for shape in shapes] + [pltpu.SemaphoreType.DMA((len(jobs), 3, 2))],
        compiler_params=pltpu.CompilerParams(vmem_limit_bytes=VMEM_BYTES),
        cost_estimate=pl.CostEstimate(flops=0, bytes_accessed=4 * operands[0].size, transcendentals=0),
        name="choose",
    )(flag, *operands)


def place_kernel(placed, ids_ref, *refs):
    received, out_ref, place_sem, stages = refs[: len(placed)], refs[len(placed) + 1], refs[len(placed) + 2], refs[len(placed) + 3 :]
    fetches, puts, at = [], [], 0
    for number, (from_ref, stage, (begin, size)) in enumerate(zip(received, stages, placed)):
        for index in range(from_ref.shape[0]):
            column = pl.multiple_of(ids_ref[at] * size + begin, 128)
            target = out_ref.at[:, pl.ds(column, from_ref.shape[-1])]
            fetches.append(pltpu.make_async_copy(from_ref.at[index], stage.at[index], place_sem.at[number, index, 0]))
            puts.append(pltpu.make_async_copy(stage.at[index], target, place_sem.at[number, index, 1]))
            at += 1
    for fetch in fetches:
        fetch.start()
    for fetch, put in zip(fetches, puts):
        fetch.wait()
        put.start()
    for put in puts:
        put.wait()


def place(out, received, ids):
    stacks = [stack for stack, _ in received]
    anywhere = pl.BlockSpec(memory_space=pltpu.HBM)
    return pl.pallas_call(
        functools.partial(place_kernel, [part for _, part in received]),
        out_shape=jax.ShapeDtypeStruct(out.shape, out.dtype),
        in_specs=[pl.BlockSpec(memory_space=pltpu.SMEM)] + [anywhere] * (len(stacks) + 1),
        out_specs=anywhere,
        scratch_shapes=[pltpu.SemaphoreType.DMA((len(stacks), max(v.shape[0] for v in stacks), 2))]
        + [pltpu.VMEM(v.shape, v.dtype) for v in stacks],
        input_output_aliases={len(stacks) + 1: 0},
        compiler_params=pltpu.CompilerParams(vmem_limit_bytes=VMEM_BYTES),
        cost_estimate=pl.CostEstimate(flops=0, bytes_accessed=8 * sum(v.size for v in stacks), transcendentals=0),
        name="place",
    )(ids, *stacks, out)


def gathered(loop, grp, jacobian):
    rows_here = jacobian.shape[1] // grp
    me, side = lax.axis_index("loop"), lax.axis_index("grp")
    both = lax.all_gather(jacobian, "grp")
    everything = lax.all_gather(both, "loop")
    mine = lax.dynamic_slice_in_dim(both, side * rows_here, rows_here, axis=2)
    left = left_operand(mine[0], mine[1])
    out = None
    for turn in range(loop):
        panel = (me + turn) % loop
        pair = tuple((lax.dynamic_index_in_dim(everything, panel, keepdims=False)[g],) for g in range(2))
        ids = jnp.stack([panel, side * rows_here]).astype(jnp.int32)
        out = panels(out, left, rows_here, jacobian.shape[1] * loop, [pair], ids, diagonal=None if turn else 0)
    return out


def rounds(loop, grp, jacobian):
    width = jacobian.shape[1]
    rows_here, columns = width // grp, width * loop
    me, side = lax.axis_index("loop"), lax.axis_index("grp")
    z, y, core = me // 4, (me // 2) % 2, me % 2

    along_x = lambda v: lax.ppermute(v, "grp", [(0, 1), (1, 0)])
    along_y = lambda v: lax.ppermute(v, "loop", [(i, i ^ 2) for i in range(16)])
    pair_z = lambda v: lax.ppermute(v, "loop", [(i, i ^ 4) for i in range(16)])
    mid_z = lambda v: lax.ppermute(
        v, "loop", [(i, i + 4) for i in range(4, 8)] + [(i + 4, i) for i in range(4, 8)]
    )
    swap = lambda v: lax.ppermute(v, "loop", [(i, i ^ 1) for i in range(16)])
    together = lax.optimization_barrier
    after = lambda value, *first: together((value, first))[0]

    mate_z = z ^ 1
    near_z = jnp.where(z < 2, 2, 1)
    far_z = jnp.where(z < 2, 3, 0)
    shift = side * rows_here
    places = [(z, y), (z, 1 - y), (near_z, y), (mate_z, 1 - y), (mate_z, y), (near_z, 1 - y), (far_z, y), (far_z, 1 - y)]
    own = [zz * 4 + yy * 2 + core for zz, yy in places]
    other = [zz * 4 + yy * 2 + 1 - core for zz, yy in places]
    number = lambda *numbers: jnp.stack(numbers).astype(jnp.int32)
    ids = tuple(
        number(*n)
        for n in (
            own[:2] + [shift],
            own[2:4],
            own[4:6],
            own[6:] + other[2:4],
            own[6:] + other[4:6],
        )
    )
    put = number(*other[:2]), number(*other[6:], *other[6:])
    outer = number((z == 0) | (z == 3))
    step = lambda out, left, turn, pairs, **kw: panels(out, left, rows_here, columns, pairs, ids[turn], **kw)
    whole, cut = (0, width), width * 3 // 4

    c = jacobian
    x_self, mid0, c_mate, y_self = along_x(c), mid_z(c), pair_z(c), along_y(c)
    own_columns = lambda v: lax.dynamic_slice_in_dim(v, shift, rows_here, axis=1)
    own_c = own_columns(c)
    own_c_o = swap(own_c)
    mid0, own_c, own_c_o, ids, put, outer = together((mid0, own_c, own_c_o, ids, put, outer))

    pair1 = pair_z(after(mid0, c_mate))
    mid1 = mid_z(c_mate)
    y_mate = along_y(after(c_mate, y_self))
    d_self = along_x(after(y_self, x_self))
    own_x = own_columns(x_self)
    left = left_operand(own_c, own_x, own_c_o, swap(own_x))

    (c_near,) = choose(outer, (after(pair1, left), mid0), [(0, 1, 0, width)])
    d_mate = pair_z(after(d_self, pair1, left))
    y_near = along_y(after(c_near, y_mate))
    x_near = along_x(after(c_near, d_self))
    out, send2 = step(None, left, 0, [((c,), (x_self,)), ((y_self,), (d_self,))], diagonal=0, sends=True)

    mid3 = mid_z(after(d_mate, out))
    pair3 = pair_z(after(mid1, d_mate, out))
    d_near = along_y(after(x_near, y_near))
    x_mate = along_x(after(c_mate, x_near))
    out, send3 = step(out, left, 1, [((c_near,), (x_near,)), ((y_mate,), (d_mate,))], sends=True)
    out = place(out, ((swap(send2), whole),), put[0])

    rest = width - cut
    early_c, early_3 = choose(outer, (after(pair3, out), mid1, mid3), [(0, 1, 0, cut), (2, 2, 0, cut)])
    x_early = along_x(after(early_c, x_mate))
    d_early = pair_z(early_3)
    y_early = along_y(after(early_c, d_near))
    out, send4 = step(out, left, 2, [((c_mate,), (x_mate,)), ((y_near,), (d_near,))], sends=True)
    late_c, late_3 = choose(outer, (after(pair3, out), mid1, mid3), [(0, 1, cut, rest), (2, 2, cut, rest)])
    x_early, y_early, d_early, late_c, late_3, out = together((x_early, y_early, d_early, late_c, late_3, out))

    x_late = along_x(after(late_c, x_early))
    d_late = pair_z(after(late_3, d_early))
    y_late = along_y(after(late_c, y_early))
    pairs = [((early_c,), (x_early,)), ((y_early,), (d_early, early_3))]
    out, send5 = step(out, left, 3, pairs, received=((swap(send3), whole),), part=whole, sends=True)
    x_late, y_late, d_late, out = together((x_late, y_late, d_late, out))

    pairs = [((late_c,), (x_late,)), ((y_late,), (d_late, late_3))]
    out, send6 = step(out, left, 4, pairs, received=((swap(send4), whole),), part=(cut, width), sends=True)
    return place(out, ((swap(send5), whole), (swap(send6), (cut, width))), put[1])


def solution(mesh):
    loop, grp = mesh.shape["loop"], mesh.shape["grp"]
    plan = rounds if (loop, grp) == (16, 2) else gathered
    return jax.shard_map(
        functools.partial(plan, loop, grp),
        mesh=mesh,
        in_specs=(P("grp", "loop"),),
        out_specs=P(("loop", "grp"), None),
        check_vma=False,
    )
```

time: 217 us -> 210 us (0.968)
  waiting for transfers between devices: 89.7 us -> 82.9 us
  starting transfers between devices: 29.8 us -> 33.1 us
  Pallas kernels: 89.6 us -> 87 us
    ppermute x5 -> x6, waiting for transfers between devices: 31.5 us -> 23.8 us  [rounds(): pair_z = lambda v: lax.ppermute(v, 'loop', [(i, i ^ 4) for i in range(16)])]
    pallas_call x5, Pallas kernels: 71.4 us -> 67.5 us  [panels(): pl.pallas_call(functools.partial(panel_kernel, sizes, diagonal, part or (...]
    ppermute x5 -> x6, waiting for transfers between devices: 11.2 us -> 7.32 us  [rounds(): along_y = lambda v: lax.ppermute(v, 'loop', [(i, i ^ 2) for i in range(16)])]
    ppermute x10 -> x7, waiting for transfers between devices: 0.57 us -> 3.61 us  [rounds(): swap = lambda v: lax.ppermute(v, 'loop', [(i, i ^ 1) for i in range(16)])]
    ppermute x5 -> x6, waiting for transfers between devices: 46.3 us -> 48.2 us  [rounds(): along_x = lambda v: lax.ppermute(v, 'grp', [(0, 1), (1, 0)])]
    ppermute x5 -> x6, starting transfers between devices: 6.8 us -> 8.36 us  [rounds(): along_y = lambda v: lax.ppermute(v, 'loop', [(i, i ^ 2) for i in range(16)])]
    pallas_call x4 -> x5, Pallas kernels: 13.8 us -> 15.1 us  [the longest x2 8.44 us: place(): pl.pallas_call(functools.partial(place_kernel, [part for _, part in recei...]
    ppermute x5 -> x6, starting transfers between devices: 12.2 us -> 12.7 us  [rounds(): pair_z = lambda v: lax.ppermute(v, 'loop', [(i, i ^ 4) for i in range(16)])]
  transfers between devices with their start and end apart: 28 -> 28, of which waited for: 11 -> 14; matrix products, arithmetic and copies ran while one was open for 3% -> 2% of each run, Pallas kernels for 36% -> 39%
where the time goes in v4:
time: 210 us
  Pallas kernels  87 us (41%)
  waiting for transfers between devices  82.9 us (39%)
  starting transfers between devices  33.1 us (16%)
  local copies, waits for them, and re-layouts  3.68 us (2%)
  other arithmetic  3.22 us (2%)
    pallas_call x5, Pallas kernels, panels(): pl.pallas_call(functools.partial(panel_kernel, sizes, diagonal, part or (...  67.5 us
    ppermute x6, waiting for transfers between devices, rounds(): along_x = lambda v: lax.ppermute(v, 'grp', [(0, 1), (1, 0)])  48.2 us
    ppermute x6, waiting for transfers between devices, rounds(): pair_z = lambda v: lax.ppermute(v, 'loop', [(i, i ^ 4) for i in range(16)])  23.8 us
    ppermute x6, starting transfers between devices, rounds(): pair_z = lambda v: lax.ppermute(v, 'loop', [(i, i ^ 4) for i in range(16)])  12.7 us
    pallas_call x2, Pallas kernels, place(): pl.pallas_call(functools.partial(place_kernel, [part for _, part in recei...  8.44 us
    ppermute x6, starting transfers between devices, rounds(): along_y = lambda v: lax.ppermute(v, 'loop', [(i, i ^ 2) for i in range(16)])  8.36 us
    ppermute x6, waiting for transfers between devices, rounds(): along_y = lambda v: lax.ppermute(v, 'loop', [(i, i ^ 2) for i in range(16)])  7.32 us
    pallas_call x3, Pallas kernels, choose(): pl.pallas_call(functools.partial(choose_kernel, [job[:3] for job in jobs]...  6.67 us
  transfers between devices with their start and end apart: 28, of which 14 were waited for; matrix products, arithmetic and copies ran while one was open for 2% of the time, Pallas kernels for 39%

profile of v4, /device:TPU:0, one launch (start us, length us, event | category | flops | bytes accessed | tf_op | source)
XLA Modules:
  0.0 210.1 jit_solution(10179263254987265060)
XLA Ops:
  0.0 1.8 collective-permute-start
  1.8 2.9 %collective-permute-start.2 = (f32[384,1024]{1,0:T(8,128)}, f32[384,1024]{1,0:T(8,128)S(1)}, u32[]{:S(2)}, u32[]{:S(2)}) collective-permute-start(f32[384,1024]{1,0:T(8,128)} %refs_0_.1), channel_id=1, source_target_pairs={{0,1},{1,0},{2,3},{3,2},{4,5},{5,4},{6,7},{7,6},{8,9},{9,8},{10,11... | collective-permute-start | bytes 4718600 | tf_op jit(solution)/shard_map/ppermute | solution.py:308
  4.8 1.5 collective-permute-start.6
  6.3 3.3 %collective-permute-start.4 = (f32[384,1024]{1,0:T(8,128)}, f32[384,1024]{1,0:T(8,128)}, u32[]{:S(2)}, u32[]{:S(2)}) collective-permute-start(f32[384,1024]{1,0:T(8,128)} %refs_0_.1), channel_id=1, source_target_pairs={{0,8},{2,10},{4,12},{6,14},{8,0},{10,2},{12,4},{14,6},{16,24},{18,... | collective-permute-start | bytes 4718600 | tf_op jit(solution)/shard_map/ppermute | solution.py:310
  9.6 1.2 constant_dynamic-slice_fusion.1.refs_0_
  10.8 0.9 copy-done
  12.3 0.7 pad_add_fusion.6.ids_ref
  13.6 0.7 pad_add_fusion.1
  14.2 0.7 pad_add_fusion.3
  14.9 24.5 %collective-permute-done.2.refs_1_ = f32[384,1024]{1,0:T(8,128)S(1)} collective-permute-done((f32[384,1024]{1,0:T(8,128)}, f32[384,1024]{1,0:T(8,128)S(1)}, u32[]{:S(2)}, u32[]{:S(2)}) %collective-permute-start.2) | collective-permute-done | bytes 1572896 | tf_op jit(solution)/shard_map/ppermute | solution.py:308
  39.4 1.6 collective-permute-done.6.refs_2_
  41.3 2.2 %collective-permute-done.4.refs_0_ = f32[384,1024]{1,0:T(8,128)} collective-permute-done((f32[384,1024]{1,0:T(8,128)}, f32[384,1024]{1,0:T(8,128)}, u32[]{:S(2)}, u32[]{:S(2)}) %collective-permute-start.4) | collective-permute-done | bytes 1572896 | tf_op jit(solution)/shard_map/ppermute | solution.py:310
  43.5 1.7 collective-permute-start.8
  45.2 0.8 collective-permute-start.13
  46.1 0.9 copy-done.1
  47.0 1.8 collective-permute-start.5
  49.4 4.4 %left_operand.1.left_hbm = bf16[1024,1536]{1,0:T(8,128)(2,1)} custom-call(f32[384,512]{1,0:T(8,128)} %copy-done, f32[384,512]{1,0:T(8,128)} %copy-done.1, f32[384,512]{1,0:T(8,128)} %copy-done.2, f32[384,512]{1,0:T(8,128)} %collective-permute-done.3.refs_3_), custom_call_target="tpu_custom_call" | custom-call | flops 1024 | bytes 1024 | tf_op jit(solution)/shard_map/left_operand/pallas_call | solution.py:35
  53.8 22.5 %collective-permute-done.7.refs_3_ = f32[384,1024]{1,0:T(8,128)} collective-permute-done((f32[384,1024]{1,0:T(8,128)}, f32[384,1024]{1,0:T(8,128)}, u32[]{:S(2)}, u32[]{:S(2)}) %collective-permute-start.7) | collective-permute-done | bytes 1572896 | tf_op jit(solution)/shard_map/ppermute | solution.py:308
  76.2 2.2 %collective-permute-done.8.refs_0_ = f32[384,1024]{1,0:T(8,128)} collective-permute-done((f32[384,1024]{1,0:T(8,128)}, f32[384,1024]{1,0:T(8,128)}, u32[]{:S(2)}, u32[]{:S(2)}) %collective-permute-start.8) | collective-permute-done | bytes 1572896 | tf_op jit(solution)/shard_map/ppermute | solution.py:310
  78.4 1.4 collective-permute-start.9
  79.9 2.2 %choose.3.refs_0_ = f32[384,1024]{1,0:T(8,128)} custom-call(s32[1]{0:T(128)} %bitcast.17.flag_ref, f32[384,1024]{1,0:T(8,128)} %collective-permute-done.8.refs_0_, f32[384,1024]{1,0:T(8,128)} %collective-permute-done.refs_1_), custom_call_target="tpu_custom_call" | custom-call | bytes 1572864 | tf_op jit(solution)/shard_map/choose/pallas_call | solution.py:238
  82.1 0.9 collective-permute-start.12
  83.0 1.5 collective-permute-start.17
  84.5 15.4 %panels.5 = (f32[512,16384]{1,0:T(8,128)}, f32[2,512,1024]{2,1,0:T(8,128)}) custom-call(s32[3]{0:T(128)} %pad_add_fusion.ids_ref, bf16[1024,1536]{1,0:T(8,128)(2,1)} %left_operand.1.left_hbm, f32[384,1024]{1,0:T(8,128)} %refs_0_.1, f32[384,1024]{1,0:T(8,128)} %copy-done.3, f32[384,1024]{1,0:T(8,128)} %collective-permute-done.6.refs_2_, ...), custom_call_target="tpu_custom_call" | custom-call | flops 96636764160 | bytes 14680064 | tf_op jit(solution)/shard_map/panels/pallas_call | solution.py:170
  100.0 13.0 %collective-permute-done.9.refs_3_ = f32[384,1024]{1,0:T(8,128)} collective-permute-done((f32[384,1024]{1,0:T(8,128)}, f32[384,1024]{1,0:T(8,128)}, u32[]{:S(2)}, u32[]{:S(2)}) %collective-permute-start.9) | collective-permute-done | bytes 1572896 | tf_op jit(solution)/shard_map/ppermute | solution.py:310
  113.0 1.4 collective-permute-start.10
  114.4 1.2 collective-permute-done.12.refs_1_
  115.7 1.9 collective-permute-done.17.refs_2_
  117.5 1.5 collective-permute-start.18
  119.6 1.9 collective-permute-start.14
  121.5 15.4 %panels.6 = (f32[512,16384]{1,0:T(8,128)}, f32[2,512,1024]{2,1,0:T(8,128)}) custom-call(s32[2]{0:T(128)} %get-tuple-element.72.ids_ref, bf16[1024,1536]{1,0:T(8,128)(2,1)} %left_operand.1.left_hbm, f32[384,1024]{1,0:T(8,128)} %choose.3.refs_0_, f32[384,1024]{1,0:T(8,128)} %collective-permute-done.12.refs_1_, ...), custom_call_target="tpu_custom_call", output_to_operand_aliasing={{0}: (6, {})} | custom-call | flops 96636764160 | bytes 14680064 | tf_op jit(solution)/shard_map/panels/pallas_call | solution.py:170
  137.0 4.3 %place.2.refs_4_ = f32[512,16384]{1,0:T(8,128)} custom-call(s32[2]{0:T(128)} %pad_add_fusion.6.ids_ref, f32[2,512,1024]{2,1,0:T(8,128)} %collective-permute-done.11.refs_0_, f32[512,16384]{1,0:T(8,128)} %get-tuple-element.76.refs_1_), custom_call_target="tpu_custom_call", output_to_operand_aliasing={{}: (2, {})} | custom-call | bytes 8388608 | tf_op jit(solution)/shard_map/place/pallas_call | solution.py:272
  141.3 4.9 %collective-permute-done.10.refs_0_ = f32[384,1024]{1,0:T(8,128)} collective-permute-done((f32[384,1024]{1,0:T(8,128)}, f32[384,1024]{1,0:T(8,128)}, u32[]{:S(2)}, u32[]{:S(2)}) %collective-permute-start.10) | collective-permute-done | bytes 1572896 | tf_op jit(solution)/shard_map/ppermute | solution.py:310
  146.2 2.5 %choose.4 = (f32[384,768]{1,0:T(8,128)}, f32[384,768]{1,0:T(8,128)}) custom-call(s32[1]{0:T(128)} %bitcast.17.flag_ref, f32[384,1024]{1,0:T(8,128)} %collective-permute-done.10.refs_0_, f32[384,1024]{1,0:T(8,128)} %collective-permute-done.5.refs_1_, f32[384,1024]{1,0:T(8,128)} %collective-permute-done.14.refs_2_), custom_call_target="tpu_custom_call" | custom-call | bytes 1572864 | tf_op jit(solution)/shard_map/choose/pallas_call | solution.py:238
  148.7 3.4 %collective-permute-done.18.refs_3_ = f32[384,1024]{1,0:T(8,128)} collective-permute-done((f32[384,1024]{1,0:T(8,128)}, f32[384,1024]{1,0:T(8,128)}, u32[]{:S(2)}, u32[]{:S(2)}) %collective-permute-start.18) | collective-permute-done | bytes 1572896 | tf_op jit(solution)/shard_map/ppermute | solution.py:309
  152.1 1.5 collective-permute-start.19
  154.2 3.1 %collective-permute-start.20 = (f32[384,768]{1,0:T(8,128)}, f32[384,768]{1,0:T(8,128)}, u32[]{:S(2)}, u32[]{:S(2)}) collective-permute-start(f32[384,768]{1,0:T(8,128)} %get-tuple-element.85.refs_4_), channel_id=1, source_target_pairs={{0,8},{2,10},{4,12},{6,14},{8,0},{10,2},{12,4},{14,6},{16,24},{18,... | collective-permute-start | bytes 3538952 | tf_op jit(solution)/shard_map/ppermute | solution.py:310
  157.3 15.3 %panels.7 = (f32[512,16384]{1,0:T(8,128)}, f32[2,512,1024]{2,1,0:T(8,128)}) custom-call(s32[2]{0:T(128)} %get-tuple-element.86.ids_ref, bf16[1024,1536]{1,0:T(8,128)(2,1)} %left_operand.1.left_hbm, f32[384,1024]{1,0:T(8,128)} %collective-permute-done.4.refs_0_, f32[384,1024]{1,0:T(8,128)} %collective-permute-done.15.refs_1_, ...), custom_call_target="tpu_custom_call", output_to_operand_aliasing={{0}: (6, {})} | custom-call | flops 96636764160 | bytes 14680064 | tf_op jit(solution)/shard_map/panels/pallas_call | solution.py:170
  172.7 2.0 choose.5
  175.2 1.5 collective-permute-done.20.refs_3_
  176.6 1.7 collective-permute-start.25
  178.4 1.5 collective-permute-start.24
  179.9 0.9 collective-permute-start.23
  180.7 13.1 %panels.8 = (f32[512,16384]{1,0:T(8,128)}, f32[2,512,768]{2,1,0:T(8,128)}) custom-call(s32[4]{0:T(128)} %get-tuple-element.59.ids_ref, bf16[1024,1536]{1,0:T(8,128)(2,1)} %left_operand.1.left_hbm, f32[384,768]{1,0:T(8,128)} %get-tuple-element.84.refs_0_, f32[384,768]{1,0:T(8,128)} %collective-permute-done.16.refs_1_, ...), custom_call_target="tpu_custom_call", output_to_operand_aliasing={{0}: (8, {})} | custom-call | flops 72477573120 | bytes 11010048 | tf_op jit(solution)/shard_map/panels/pallas_call | solution.py:170
  193.9 0.6 copy-done.4
  194.6 8.3 %panels.9 = (f32[512,16384]{1,0:T(8,128)}, f32[2,512,256]{2,1,0:T(8,128)}) custom-call(s32[4]{0:T(128)} %get-tuple-element.97.ids_ref, bf16[1024,1536]{1,0:T(8,128)(2,1)} %left_operand.1.left_hbm, f32[384,256]{1,0:T(8,128)} %get-tuple-element.100.refs_0_, f32[384,256]{1,0:T(8,128)} %collective-permute-done.23.refs_1_, ...), custom_call_target="tpu_custom_call", output_to_operand_aliasing={{0}: (8, {})} | custom-call | flops 24159191040 | bytes 3670016 | tf_op jit(solution)/shard_map/panels/pallas_call | solution.py:170
  203.0 3.0 %collective-permute-done.27.refs_1_ = f32[2,512,256]{2,1,0:T(8,128)} collective-permute-done((f32[2,512,256]{2,1,0:T(8,128)}, f32[2,512,256]{2,1,0:T(8,128)}, u32[]{:S(2)}, u32[]{:S(2)}) %collective-permute-start.27) | collective-permute-done | bytes 1048608 | tf_op jit(solution)/shard_map/ppermute | solution.py:314
  206.0 4.1 %place.3 = f32[512,16384]{1,0:T(8,128)} custom-call(s32[4]{0:T(128)} %pad_add_fusion.7.ids_ref, f32[2,512,768]{2,1,0:T(8,128)} %collective-permute-done.22.refs_0_, f32[2,512,256]{2,1,0:T(8,128)} %collective-permute-done.27.refs_1_, f32[512,16384]{1,0:T(8,128)} %get-tuple-element.110.refs_2_), custom_call_target="tpu_custom_call", output_to_operand_aliasing={{}: (3, {})} | custom-call | bytes 8388608 | tf_op jit(solution)/shard_map/place/pallas_call | solution.py:272
  (36 shorter events, 4.3 us)
Async XLA Ops:
  0.0 14.9 %collective-permute-start = (f32[384,1024]{1,0:T(8,128)}, f32[384,1024]{1,0:T(8,128)}, u32[]{:S(2)}, u32[]{:S(2)}) collective-permute-start(f32[384,1024]{1,0:T(8,128)} %refs_0_.1), channel_id=1, source_target_pairs={{8,16},{10,18},{12,20},{14,22},{16,8},{18,10},{20,12},{22,14},{9,1... | collective-permute-start | bytes 4718600 | tf_op jit(solution)/shard_map/ppermute | solution.py:311
  1.8 37.5 %collective-permute-start.2 = (f32[384,1024]{1,0:T(8,128)}, f32[384,1024]{1,0:T(8,128)S(1)}, u32[]{:S(2)}, u32[]{:S(2)}) collective-permute-start(f32[384,1024]{1,0:T(8,128)} %refs_0_.1), channel_id=1, source_target_pairs={{0,1},{1,0},{2,3},{3,2},{4,5},{5,4},{6,7},{7,6},{8,9},{9,8},{10,11... | collective-permute-start | bytes 4718600 | tf_op jit(solution)/shard_map/ppermute | solution.py:308
  4.8 36.2 %collective-permute-start.6 = (f32[384,1024]{1,0:T(8,128)}, f32[384,1024]{1,0:T(8,128)}, u32[]{:S(2)}, u32[]{:S(2)}) collective-permute-start(f32[384,1024]{1,0:T(8,128)} %refs_0_.1), channel_id=1, source_target_pairs={{0,4},{2,6},{4,0},{6,2},{8,12},{10,14},{12,8},{14,10},{16,20},{18,... | collective-permute-start | bytes 4718600 | tf_op jit(solution)/shard_map/ppermute | solution.py:309
  6.3 37.2 %collective-permute-start.4 = (f32[384,1024]{1,0:T(8,128)}, f32[384,1024]{1,0:T(8,128)}, u32[]{:S(2)}, u32[]{:S(2)}) collective-permute-start(f32[384,1024]{1,0:T(8,128)} %refs_0_.1), channel_id=1, source_target_pairs={{0,8},{2,10},{4,12},{6,14},{8,0},{10,2},{12,4},{14,6},{16,24},{18,... | collective-permute-start | bytes 4718600 | tf_op jit(solution)/shard_map/ppermute | solution.py:310
  10.8 0.9 copy-start
  11.7 3.2 %collective-permute-start.1 = (f32[384,512]{1,0:T(8,128)S(1)}, f32[384,512]{1,0:T(8,128)S(1)}, u32[]{:S(2)}, u32[]{:S(2)}) collective-permute-start(f32[384,512]{1,0:T(8,128)S(1)} %constant_dynamic-slice_fusion.1.refs_0_), channel_id=1, source_target_pairs={{0,2},{2,0},{4,6},{6,4},{8,10},{10,8},{12,14},{14,12},{16,18},{18,... | collective-permute-start | bytes 2359304 | tf_op jit(solution)/shard_map/ppermute | solution.py:314
  14.9 32.1 %copy-start.2 = (f32[384,512]{1,0:T(8,128)}, f32[384,512]{1,0:T(8,128)S(1)}, u32[]{:S(2)}) copy-start(f32[384,512]{1,0:T(8,128)S(1)} %collective-permute-done.1.refs_2_) | copy-start | bytes 2359300
  39.4 9.4 %copy-start.3 = (f32[384,1024]{1,0:T(8,128)}, f32[384,1024]{1,0:T(8,128)S(1)}, u32[]{:S(2)}) copy-start(f32[384,1024]{1,0:T(8,128)S(1)} %collective-permute-done.2.refs_1_) | copy-start | bytes 4718596
  41.0 35.3 %collective-permute-start.7 = (f32[384,1024]{1,0:T(8,128)}, f32[384,1024]{1,0:T(8,128)}, u32[]{:S(2)}, u32[]{:S(2)}) collective-permute-start(f32[384,1024]{1,0:T(8,128)} %collective-permute-done.6.refs_2_), channel_id=1, source_target_pairs={{0,1},{1,0},{2,3},{3,2},{4,5},{5,4},{6,7},{7,6},{8,9},{9,8},{10,11... | collective-permute-start | bytes 4718600 | tf_op jit(solution)/shard_map/ppermute | solution.py:308
  43.5 35.0 %collective-permute-start.8 = (f32[384,1024]{1,0:T(8,128)}, f32[384,1024]{1,0:T(8,128)}, u32[]{:S(2)}, u32[]{:S(2)}) collective-permute-start(f32[384,1024]{1,0:T(8,128)} %collective-permute-done.refs_1_), channel_id=1, source_target_pairs={{0,8},{2,10},{4,12},{6,14},{8,0},{10,2},{12,4},{14,6},{16,24},{18,... | collective-permute-start | bytes 4718600 | tf_op jit(solution)/shard_map/ppermute | solution.py:310
  45.2 37.8 %collective-permute-start.13 = (f32[384,1024]{1,0:T(8,128)}, f32[384,1024]{1,0:T(8,128)}, u32[]{:S(2)}, u32[]{:S(2)}) collective-permute-start(f32[384,1024]{1,0:T(8,128)} %collective-permute-done.4.refs_0_), channel_id=1, source_target_pairs={{0,4},{2,6},{4,0},{6,2},{8,12},{10,14},{12,8},{14,10},{16,20},{18,... | collective-permute-start | bytes 4718600 | tf_op jit(solution)/shard_map/ppermute | solution.py:309
  46.1 0.9 copy-start.1
  47.0 2.4 %collective-permute-start.3 = (f32[384,512]{1,0:T(8,128)S(1)}, f32[384,512]{1,0:T(8,128)}, u32[]{:S(2)}, u32[]{:S(2)}) collective-permute-start(f32[384,512]{1,0:T(8,128)S(1)} %constant_dynamic-slice_fusion.refs_1_), channel_id=1, source_target_pairs={{0,2},{2,0},{4,6},{6,4},{8,10},{10,8},{12,14},{14,12},{16,18},{18,... | collective-permute-start | bytes 2359304 | tf_op jit(solution)/shard_map/ppermute | solution.py:314
  47.0 66.0 %collective-permute-start.5 = (f32[384,1024]{1,0:T(8,128)}, f32[384,1024]{1,0:T(8,128)}, u32[]{:S(2)}, u32[]{:S(2)}) collective-permute-start(f32[384,1024]{1,0:T(8,128)} %collective-permute-done.4.refs_0_), channel_id=1, source_target_pairs={{8,16},{10,18},{12,20},{14,22},{16,8},{18,10},{20,12},{22,14},{9,1... | collective-permute-start | bytes 4718600 | tf_op jit(solution)/shard_map/ppermute | solution.py:311
  78.4 34.6 %collective-permute-start.9 = (f32[384,1024]{1,0:T(8,128)}, f32[384,1024]{1,0:T(8,128)}, u32[]{:S(2)}, u32[]{:S(2)}) collective-permute-start(f32[384,1024]{1,0:T(8,128)} %collective-permute-done.7.refs_3_), channel_id=1, source_target_pairs={{0,8},{2,10},{4,12},{6,14},{8,0},{10,2},{12,4},{14,6},{16,24},{18,... | collective-permute-start | bytes 4718600 | tf_op jit(solution)/shard_map/ppermute | solution.py:310
  82.1 33.5 %collective-permute-start.12 = (f32[384,1024]{1,0:T(8,128)}, f32[384,1024]{1,0:T(8,128)}, u32[]{:S(2)}, u32[]{:S(2)}) collective-permute-start(f32[384,1024]{1,0:T(8,128)} %choose.3.refs_0_), channel_id=1, source_target_pairs={{0,1},{1,0},{2,3},{3,2},{4,5},{5,4},{6,7},{7,6},{8,9},{9,8},{10,11... | collective-permute-start | bytes 4718600 | tf_op jit(solution)/shard_map/ppermute | solution.py:308
  83.0 34.6 %collective-permute-start.17 = (f32[384,1024]{1,0:T(8,128)}, f32[384,1024]{1,0:T(8,128)}, u32[]{:S(2)}, u32[]{:S(2)}) collective-permute-start(f32[384,1024]{1,0:T(8,128)} %choose.3.refs_0_), channel_id=1, source_target_pairs={{0,4},{2,6},{4,0},{6,2},{8,12},{10,14},{12,8},{14,10},{16,20},{18,... | collective-permute-start | bytes 4718600 | tf_op jit(solution)/shard_map/ppermute | solution.py:309
  100.0 36.9 %collective-permute-start.11 = (f32[2,512,1024]{2,1,0:T(8,128)}, f32[2,512,1024]{2,1,0:T(8,128)}, u32[]{:S(2)}, u32[]{:S(2)}) collective-permute-start(f32[2,512,1024]{2,1,0:T(8,128)} %get-tuple-element.71), channel_id=1, source_target_pairs={{0,2},{2,0},{4,6},{6,4},{8,10},{10,8},{12,14},{14,12},{16,18},{18,... | collective-permute-start | bytes 12582920 | tf_op jit(solution)/shard_map/ppermute | solution.py:314
  113.0 33.2 %collective-permute-start.10 = (f32[384,1024]{1,0:T(8,128)}, f32[384,1024]{1,0:T(8,128)}, u32[]{:S(2)}, u32[]{:S(2)}) collective-permute-start(f32[384,1024]{1,0:T(8,128)} %collective-permute-done.5.refs_1_), channel_id=1, source_target_pairs={{0,8},{2,10},{4,12},{6,14},{8,0},{10,2},{12,4},{14,6},{16,24},{18,... | collective-permute-start | bytes 4718600 | tf_op jit(solution)/shard_map/ppermute | solution.py:310
  117.5 34.6 %collective-permute-start.18 = (f32[384,1024]{1,0:T(8,128)}, f32[384,1024]{1,0:T(8,128)}, u32[]{:S(2)}, u32[]{:S(2)}) collective-permute-start(f32[384,1024]{1,0:T(8,128)} %collective-permute-done.12.refs_1_), channel_id=1, source_target_pairs={{0,4},{2,6},{4,0},{6,2},{8,12},{10,14},{12,8},{14,10},{16,20},{18,... | collective-permute-start | bytes 4718600 | tf_op jit(solution)/shard_map/ppermute | solution.py:309
  119.1 34.6 %collective-permute-start.15 = (f32[384,1024]{1,0:T(8,128)}, f32[384,1024]{1,0:T(8,128)}, u32[]{:S(2)}, u32[]{:S(2)}) collective-permute-start(f32[384,1024]{1,0:T(8,128)} %collective-permute-done.4.refs_0_), channel_id=1, source_target_pairs={{0,1},{1,0},{2,3},{3,2},{4,5},{5,4},{6,7},{7,6},{8,9},{9,8},{10,11... | collective-permute-start | bytes 4718600 | tf_op jit(solution)/shard_map/ppermute | solution.py:308
  119.6 26.6 %collective-permute-start.14 = (f32[384,1024]{1,0:T(8,128)}, f32[384,1024]{1,0:T(8,128)}, u32[]{:S(2)}, u32[]{:S(2)}) collective-permute-start(f32[384,1024]{1,0:T(8,128)} %collective-permute-done.9.refs_3_), channel_id=1, source_target_pairs={{8,16},{10,18},{12,20},{14,22},{16,8},{18,10},{20,12},{22,14},{9,1... | collective-permute-start | bytes 4718600 | tf_op jit(solution)/shard_map/ppermute | solution.py:311
  136.9 43.9 %collective-permute-start.21 = (f32[2,512,1024]{2,1,0:T(8,128)}, f32[2,512,1024]{2,1,0:T(8,128)}, u32[]{:S(2)}, u32[]{:S(2)}) collective-permute-start(f32[2,512,1024]{2,1,0:T(8,128)} %get-tuple-element.94), channel_id=1, source_target_pairs={{0,2},{2,0},{4,6},{6,4},{8,10},{10,8},{12,14},{14,12},{16,18},{18,... | collective-permute-start | bytes 12582920 | tf_op jit(solution)/shard_map/ppermute | solution.py:314
  152.1 23.1 %collective-permute-start.19 = (f32[384,768]{1,0:T(8,128)}, f32[384,768]{1,0:T(8,128)}, u32[]{:S(2)}, u32[]{:S(2)}) collective-permute-start(f32[384,768]{1,0:T(8,128)} %get-tuple-element.84.refs_0_), channel_id=1, source_target_pairs={{0,4},{2,6},{4,0},{6,2},{8,12},{10,14},{12,8},{14,10},{16,20},{18,... | collective-permute-start | bytes 3538952 | tf_op jit(solution)/shard_map/ppermute | solution.py:309
  153.6 21.5 %collective-permute-start.16 = (f32[384,768]{1,0:T(8,128)}, f32[384,768]{1,0:T(8,128)}, u32[]{:S(2)}, u32[]{:S(2)}) collective-permute-start(f32[384,768]{1,0:T(8,128)} %get-tuple-element.84.refs_0_), channel_id=1, source_target_pairs={{0,1},{1,0},{2,3},{3,2},{4,5},{5,4},{6,7},{7,6},{8,9},{9,8},{10,11... | collective-permute-start | bytes 3538952 | tf_op jit(solution)/shard_map/ppermute | solution.py:308
  154.2 22.4 %collective-permute-start.20 = (f32[384,768]{1,0:T(8,128)}, f32[384,768]{1,0:T(8,128)}, u32[]{:S(2)}, u32[]{:S(2)}) collective-permute-start(f32[384,768]{1,0:T(8,128)} %get-tuple-element.85.refs_4_), channel_id=1, source_target_pairs={{0,8},{2,10},{4,12},{6,14},{8,0},{10,2},{12,4},{14,6},{16,24},{18,... | collective-permute-start | bytes 3538952 | tf_op jit(solution)/shard_map/ppermute | solution.py:310
  172.7 21.3 %collective-permute-start.26 = (f32[2,512,1024]{2,1,0:T(8,128)}, f32[2,512,1024]{2,1,0:T(8,128)}, u32[]{:S(2)}, u32[]{:S(2)}) collective-permute-start(f32[2,512,1024]{2,1,0:T(8,128)} %get-tuple-element.107), channel_id=1, source_target_pairs={{0,2},{2,0},{4,6},{6,4},{8,10},{10,8},{12,14},{14,12},{16,18},{18,... | collective-permute-start | bytes 12582920 | tf_op jit(solution)/shard_map/ppermute | solution.py:314
  176.6 17.2 %collective-permute-start.25 = (f32[384,256]{1,0:T(8,128)}, f32[384,256]{1,0:T(8,128)S(1)}, u32[]{:S(2)}, u32[]{:S(2)}) collective-permute-start(f32[384,256]{1,0:T(8,128)} %get-tuple-element.102.refs_4_), channel_id=1, source_target_pairs={{0,8},{2,10},{4,12},{6,14},{8,0},{10,2},{12,4},{14,6},{16,24},{18,... | collective-permute-start | bytes 1179656 | tf_op jit(solution)/shard_map/ppermute | solution.py:310
  178.4 15.5 %collective-permute-start.24 = (f32[384,256]{1,0:T(8,128)}, f32[384,256]{1,0:T(8,128)}, u32[]{:S(2)}, u32[]{:S(2)}) collective-permute-start(f32[384,256]{1,0:T(8,128)} %get-tuple-element.100.refs_0_), channel_id=1, source_target_pairs={{0,4},{2,6},{4,0},{6,2},{8,12},{10,14},{12,8},{14,10},{16,20},{18,... | collective-permute-start | bytes 1179656 | tf_op jit(solution)/shard_map/ppermute | solution.py:309
  179.9 14.0 %collective-permute-start.23 = (f32[384,256]{1,0:T(8,128)}, f32[384,256]{1,0:T(8,128)}, u32[]{:S(2)}, u32[]{:S(2)}) collective-permute-start(f32[384,256]{1,0:T(8,128)} %get-tuple-element.100.refs_0_), channel_id=1, source_target_pairs={{0,1},{1,0},{2,3},{3,2},{4,5},{5,4},{6,7},{7,6},{8,9},{9,8},{10,11... | collective-permute-start | bytes 1179656 | tf_op jit(solution)/shard_map/ppermute | solution.py:308
  193.8 0.8 copy-start.4
  193.9 9.1 %collective-permute-start.22 = (f32[2,512,768]{2,1,0:T(8,128)}, f32[2,512,768]{2,1,0:T(8,128)}, u32[]{:S(2)}, u32[]{:S(2)}) collective-permute-start(f32[2,512,768]{2,1,0:T(8,128)} %get-tuple-element.96), channel_id=1, source_target_pairs={{0,2},{2,0},{4,6},{6,4},{8,10},{10,8},{12,14},{14,12},{16,18},{18,... | collective-permute-start | bytes 9437192 | tf_op jit(solution)/shard_map/ppermute | solution.py:314
  202.9 3.1 %collective-permute-start.27 = (f32[2,512,256]{2,1,0:T(8,128)}, f32[2,512,256]{2,1,0:T(8,128)}, u32[]{:S(2)}, u32[]{:S(2)}) collective-permute-start(f32[2,512,256]{2,1,0:T(8,128)} %get-tuple-element.109), channel_id=1, source_target_pairs={{0,2},{2,0},{4,6},{6,4},{8,10},{10,8},{12,14},{14,12},{16,18},{18,... | collective-permute-start | bytes 3145736 | tf_op jit(solution)/shard_map/ppermute | solution.py:314

commit v5 on v4

--- a/solution.py
+++ b/solution.py
@@ -122,7 +122,7 @@
         block = [held[slot, k, :, pl.ds(column, tile)] for k in range(most)]
         if most > 2:
             extra = functools.reduce(jnp.logical_or, [index == i for i, n in enumerate(sizes) if sum(n) > 2])
-            block[1] = block[1] + jnp.where(extra, block[2], 0.0)
+            block[1] = jnp.where(extra & (ids_ref[ids_ref.shape[0] - 1] == 0), block[2], block[1])
         halves = [split_high_low(value) for value in block[:2]]
         high, low = (jnp.concatenate(pieces, axis=0) for pieces in zip(*halves))
         dot = functools.partial(jnp.dot, preferred_element_type=jnp.float32)
@@ -161,7 +161,7 @@
         args.append(out)
     anywhere = pl.BlockSpec(memory_space=pl.ANY)
     most = max(map(sum, sizes))
-    tile = 512 if width % 512 == 0 else min(256, width)
+    tile = 512 if width % 512 == 0 else 256 if width % 256 == 0 else width
     height = 2 * rows if sends else rows
     shapes = [jax.ShapeDtypeStruct((rows, columns), jnp.float32)]
     if sends:
@@ -308,9 +308,9 @@
     along_x = lambda v: lax.ppermute(v, "grp", [(0, 1), (1, 0)])
     along_y = lambda v: lax.ppermute(v, "loop", [(i, i ^ 2) for i in range(16)])
     pair_z = lambda v: lax.ppermute(v, "loop", [(i, i ^ 4) for i in range(16)])
-    mid_z = lambda v: lax.ppermute(
-        v, "loop", [(i, i + 4) for i in range(4, 8)] + [(i + 4, i) for i in range(4, 8)]
-    )
+    inner = [(i, i + 4) for i in range(4, 8)] + [(i + 4, i) for i in range(4, 8)]
+    mid_z = lambda v: lax.ppermute(v, "loop", inner)
+    mid_z_all = lambda v: lax.ppermute(v, "loop", inner + [(i, i ^ 1) for i in (0, 1, 2, 3, 12, 13, 14, 15)])
     swap = lambda v: lax.ppermute(v, "loop", [(i, i ^ 1) for i in range(16)])
     together = lax.optimization_barrier
     after = lambda value, *first: together((value, first))[0]
@@ -322,21 +322,22 @@
     places = [(z, y), (z, 1 - y), (near_z, y), (mate_z, 1 - y), (mate_z, y), (near_z, 1 - y), (far_z, y), (far_z, 1 - y)]
     own = [zz * 4 + yy * 2 + core for zz, yy in places]
     other = [zz * 4 + yy * 2 + 1 - core for zz, yy in places]
-    number = lambda *numbers: jnp.stack(numbers).astype(jnp.int32)
+    number = lambda *numbers: jnp.stack([jnp.int32(n) for n in numbers])
+    outer = jnp.int32((z == 0) | (z == 3))
     ids = tuple(
         number(*n)
         for n in (
             own[:2] + [shift],
             own[2:4],
             own[4:6],
-            own[6:] + other[2:4],
-            own[6:] + other[4:6],
+            own[6:] + other[2:4] + [outer],
+            own[6:] + other[4:6] + [outer],
         )
     )
-    put = number(*other[:2]), number(*other[6:], *other[6:])
-    outer = number((z == 0) | (z == 3))
+    put = number(*other[:2]), number(*other[6:])
+    outer = number(outer)
     step = lambda out, left, turn, pairs, **kw: panels(out, left, rows_here, columns, pairs, ids[turn], **kw)
-    whole, cut = (0, width), width * 3 // 4
+    whole, cut = (0, width), width * 5 // 8
 
     c = jacobian
     x_self, mid0, c_mate, y_self = along_x(c), mid_z(c), pair_z(c), along_y(c)
@@ -358,7 +359,7 @@
     x_near = along_x(after(c_near, d_self))
     out, send2 = step(None, left, 0, [((c,), (x_self,)), ((y_self,), (d_self,))], diagonal=0, sends=True)
 
-    mid3 = mid_z(after(d_mate, out))
+    mid3 = mid_z_all(after(d_mate, out))
     pair3 = pair_z(after(mid1, d_mate, out))
     d_near = along_y(after(x_near, y_near))
     x_mate = along_x(after(c_mate, x_near))
@@ -366,13 +367,16 @@
     out = place(out, ((swap(send2), whole),), put[0])
 
     rest = width - cut
-    early_c, early_3 = choose(outer, (after(pair3, out), mid1, mid3), [(0, 1, 0, cut), (2, 2, 0, cut)])
+    early_c, early_3, late_c, late_3 = choose(
+        outer,
+        (after(pair3, out), mid1, mid3),
+        [(0, 1, 0, cut), (2, 2, 0, cut), (0, 1, cut, rest), (2, 2, cut, rest)],
+    )
     x_early = along_x(after(early_c, x_mate))
     d_early = pair_z(early_3)
     y_early = along_y(after(early_c, d_near))
     out, send4 = step(out, left, 2, [((c_mate,), (x_mate,)), ((y_near,), (d_near,))], sends=True)
-    late_c, late_3 = choose(outer, (after(pair3, out), mid1, mid3), [(0, 1, cut, rest), (2, 2, cut, rest)])
-    x_early, y_early, d_early, late_c, late_3, out = together((x_early, y_early, d_early, late_c, late_3, out))
+    x_early, y_early, d_early, out = together((x_early, y_early, d_early, out))
 
     x_late = along_x(after(late_c, x_early))
     d_late = pair_z(after(late_3, d_early))
@@ -383,7 +387,8 @@
 
     pairs = [((late_c,), (x_late,)), ((y_late,), (d_late, late_3))]
     out, send6 = step(out, left, 4, pairs, received=((swap(send4), whole),), part=(cut, width), sends=True)
-    return place(out, ((swap(send5), whole), (swap(send6), (cut, width))), put[1])
+    out = place(out, ((swap(send5), whole),), put[1])
+    return place(out, ((swap(send6), (cut, width)),), put[1])
 
 
 def solution(mesh):

time: 210 us -> 206 us (0.981)
  waiting for transfers between devices: 82.9 us -> 80 us
  starting transfers between devices: 33.1 us -> 30.4 us
    ppermute x7, waiting for transfers between devices: 3.61 us -> 0.62 us  [rounds(): swap = lambda v: lax.ppermute(v, 'loop', [(i, i ^ 1) for i in range(16)])]
    pallas_call x2 -> x3, Pallas kernels: 8.44 us -> 10.8 us  [place(): pl.pallas_call(functools.partial(place_kernel, [part for _, part in recei...]
    pallas_call x3 -> x2, Pallas kernels: 6.67 us -> 5.08 us  [choose(): pl.pallas_call(functools.partial(choose_kernel, [job[:3] for job in jobs]...]
  transfers between devices with their start and end apart: 28 -> 28, of which waited for: 14 -> 12; matrix products, arithmetic and copies ran while one was open for 2% -> 2% of each run, Pallas kernels for 39% -> 42%
where the time goes in v5:
time: 206 us; the launch traced here: 205 us
  Pallas kernels  88.4 us (43%)
  waiting for transfers between devices  80 us (39%)
  starting transfers between devices  30.4 us (15%)
  local copies, waits for them, and re-layouts  4.27 us (2%)
    pallas_call x5, Pallas kernels, panels(): pl.pallas_call(functools.partial(panel_kernel, sizes, diagonal, part or (...  68.2 us
    ppermute x6, waiting for transfers between devices, rounds(): along_x = lambda v: lax.ppermute(v, 'grp', [(0, 1), (1, 0)])  49.3 us
    ppermute x6, waiting for transfers between devices, rounds(): pair_z = lambda v: lax.ppermute(v, 'loop', [(i, i ^ 4) for i in range(16)])  23.7 us
    ppermute x6, starting transfers between devices, rounds(): pair_z = lambda v: lax.ppermute(v, 'loop', [(i, i ^ 4) for i in range(16)])  10.8 us
    pallas_call x3, Pallas kernels, place(): pl.pallas_call(functools.partial(place_kernel, [part for _, part in recei...  10.8 us
    ppermute x6, starting transfers between devices, rounds(): along_y = lambda v: lax.ppermute(v, 'loop', [(i, i ^ 2) for i in range(16)])  8.42 us
    ppermute x6, waiting for transfers between devices, rounds(): along_y = lambda v: lax.ppermute(v, 'loop', [(i, i ^ 2) for i in range(16)])  6.46 us
    ppermute x6, starting transfers between devices, rounds(): along_x = lambda v: lax.ppermute(v, 'grp', [(0, 1), (1, 0)])  6.19 us
  transfers between devices with their start and end apart: 28, of which 12 were waited for; matrix products, arithmetic and copies ran while one was open for 2% of the time, Pallas kernels for 42%

profile of v5, /device:TPU:0, one launch (start us, length us, event | category | flops | bytes accessed | tf_op | source)
XLA Modules:
  0.0 205.3 jit_solution(12399161371439022248)
XLA Ops:
  0.0 1.9 collective-permute-start
  1.9 2.9 %collective-permute-start.2 = (f32[384,1024]{1,0:T(8,128)}, f32[384,1024]{1,0:T(8,128)S(1)}, u32[]{:S(2)}, u32[]{:S(2)}) collective-permute-start(f32[384,1024]{1,0:T(8,128)} %refs_0_.1), channel_id=1, source_target_pairs={{0,1},{1,0},{2,3},{3,2},{4,5},{5,4},{6,7},{7,6},{8,9},{9,8},{10,11... | collective-permute-start | bytes 4718600 | tf_op jit(solution)/shard_map/ppermute | solution.py:308
  4.8 1.5 collective-permute-start.6
  6.3 3.3 %collective-permute-start.4 = (f32[384,1024]{1,0:T(8,128)}, f32[384,1024]{1,0:T(8,128)}, u32[]{:S(2)}, u32[]{:S(2)}) collective-permute-start(f32[384,1024]{1,0:T(8,128)} %refs_0_.1), channel_id=1, source_target_pairs={{0,8},{2,10},{4,12},{6,14},{8,0},{10,2},{12,4},{14,6},{16,24},{18,... | collective-permute-start | bytes 4718600 | tf_op jit(solution)/shard_map/ppermute | solution.py:310
  9.6 1.2 constant_dynamic-slice_fusion.1.refs_0_
  10.8 0.9 copy-done
  11.7 0.6 stack.101.ids_ref
  12.3 0.6 stack.98.ids_ref
  12.9 0.7 pad_add_fusion.ids_ref
  13.6 0.6 pad_add_fusion.3
  14.2 0.7 pad_add_fusion.1
  14.9 24.5 %collective-permute-done.2.refs_1_ = f32[384,1024]{1,0:T(8,128)S(1)} collective-permute-done((f32[384,1024]{1,0:T(8,128)}, f32[384,1024]{1,0:T(8,128)S(1)}, u32[]{:S(2)}, u32[]{:S(2)}) %collective-permute-start.2) | collective-permute-done | bytes 1572896 | tf_op jit(solution)/shard_map/ppermute | solution.py:308
  39.4 1.6 collective-permute-done.6.refs_2_
  41.3 2.2 %collective-permute-done.4.refs_0_ = f32[384,1024]{1,0:T(8,128)} collective-permute-done((f32[384,1024]{1,0:T(8,128)}, f32[384,1024]{1,0:T(8,128)}, u32[]{:S(2)}, u32[]{:S(2)}) %collective-permute-start.4) | collective-permute-done | bytes 1572896 | tf_op jit(solution)/shard_map/ppermute | solution.py:310
  43.5 1.7 collective-permute-start.8
  45.2 0.8 collective-permute-start.13
  46.1 0.9 copy-done.1
  47.0 1.8 collective-permute-start.5
  48.8 0.6 collective-permute-done.3.refs_3_
  49.4 4.4 %left_operand.1.left_hbm = bf16[1024,1536]{1,0:T(8,128)(2,1)} custom-call(f32[384,512]{1,0:T(8,128)} %copy-done, f32[384,512]{1,0:T(8,128)} %copy-done.1, f32[384,512]{1,0:T(8,128)} %copy-done.2, f32[384,512]{1,0:T(8,128)} %collective-permute-done.3.refs_3_), custom_call_target="tpu_custom_call" | custom-call | flops 1024 | bytes 1024 | tf_op jit(solution)/shard_map/left_operand/pallas_call | solution.py:35
  53.7 22.5 %collective-permute-done.7.refs_3_ = f32[384,1024]{1,0:T(8,128)} collective-permute-done((f32[384,1024]{1,0:T(8,128)}, f32[384,1024]{1,0:T(8,128)}, u32[]{:S(2)}, u32[]{:S(2)}) %collective-permute-start.7) | collective-permute-done | bytes 1572896 | tf_op jit(solution)/shard_map/ppermute | solution.py:308
  76.2 2.2 %collective-permute-done.8.refs_0_ = f32[384,1024]{1,0:T(8,128)} collective-permute-done((f32[384,1024]{1,0:T(8,128)}, f32[384,1024]{1,0:T(8,128)}, u32[]{:S(2)}, u32[]{:S(2)}) %collective-permute-start.8) | collective-permute-done | bytes 1572896 | tf_op jit(solution)/shard_map/ppermute | solution.py:310
  78.4 1.4 collective-permute-start.9
  79.9 2.2 %choose.2.refs_0_ = f32[384,1024]{1,0:T(8,128)} custom-call(s32[1]{0:T(128)} %bitcast.11.flag_ref, f32[384,1024]{1,0:T(8,128)} %collective-permute-done.8.refs_0_, f32[384,1024]{1,0:T(8,128)} %collective-permute-done.refs_1_), custom_call_target="tpu_custom_call" | custom-call | bytes 1572864 | tf_op jit(solution)/shard_map/choose/pallas_call | solution.py:238
  82.1 0.9 collective-permute-start.12
  83.0 1.5 collective-permute-start.17
  84.5 15.4 %panels.5 = (f32[512,16384]{1,0:T(8,128)}, f32[2,512,1024]{2,1,0:T(8,128)}) custom-call(s32[3]{0:T(128)} %pad_add_fusion.ids_ref, bf16[1024,1536]{1,0:T(8,128)(2,1)} %left_operand.1.left_hbm, f32[384,1024]{1,0:T(8,128)} %refs_0_.1, f32[384,1024]{1,0:T(8,128)} %copy-done.3, f32[384,1024]{1,0:T(8,128)} %collective-permute-done.6.refs_2_, ...), custom_call_target="tpu_custom_call" | custom-call | flops 96636764160 | bytes 14680064 | tf_op jit(solution)/shard_map/panels/pallas_call | solution.py:170
  100.0 13.0 %collective-permute-done.9.refs_3_ = f32[384,1024]{1,0:T(8,128)} collective-permute-done((f32[384,1024]{1,0:T(8,128)}, f32[384,1024]{1,0:T(8,128)}, u32[]{:S(2)}, u32[]{:S(2)}) %collective-permute-start.9) | collective-permute-done | bytes 1572896 | tf_op jit(solution)/shard_map/ppermute | solution.py:310
  113.0 1.4 collective-permute-start.10
  114.4 1.2 collective-permute-done.12.refs_1_
  115.7 1.9 collective-permute-done.17.refs_2_
  117.6 1.5 collective-permute-start.18
  119.7 15.4 %panels.6 = (f32[512,16384]{1,0:T(8,128)}, f32[2,512,1024]{2,1,0:T(8,128)}) custom-call(s32[2]{0:T(128)} %get-tuple-element.69.ids_ref, bf16[1024,1536]{1,0:T(8,128)(2,1)} %left_operand.1.left_hbm, f32[384,1024]{1,0:T(8,128)} %choose.2.refs_0_, f32[384,1024]{1,0:T(8,128)} %collective-permute-done.12.refs_1_, ...), custom_call_target="tpu_custom_call", output_to_operand_aliasing={{0}: (6, {})} | custom-call | flops 96636764160 | bytes 14680064 | tf_op jit(solution)/shard_map/panels/pallas_call | solution.py:170
  135.6 4.3 %place.3.refs_4_ = f32[512,16384]{1,0:T(8,128)} custom-call(s32[2]{0:T(128)} %get-tuple-element.67.ids_ref, f32[2,512,1024]{2,1,0:T(8,128)} %collective-permute-done.11.refs_0_, f32[512,16384]{1,0:T(8,128)} %get-tuple-element.73.refs_1_), custom_call_target="tpu_custom_call", output_to_operand_aliasing={{}: (2, {})} | custom-call | bytes 8388608 | tf_op jit(solution)/shard_map/place/pallas_call | solution.py:272
  139.9 6.3 %collective-permute-done.10.refs_0_ = f32[384,1024]{1,0:T(8,128)} collective-permute-done((f32[384,1024]{1,0:T(8,128)}, f32[384,1024]{1,0:T(8,128)}, u32[]{:S(2)}, u32[]{:S(2)}) %collective-permute-start.10) | collective-permute-done | bytes 1572896 | tf_op jit(solution)/shard_map/ppermute | solution.py:310
  146.2 2.8 %choose.3 = (f32[384,640]{1,0:T(8,128)}, f32[384,640]{1,0:T(8,128)}, f32[384,384]{1,0:T(8,128)}, f32[384,384]{1,0:T(8,128)}) custom-call(s32[1]{0:T(128)} %bitcast.11.flag_ref, f32[384,1024]{1,0:T(8,128)} %collective-permute-done.10.refs_0_, f32[384,1024]{1,0:T(8,128)} %collective-permute-done.5.refs_1_, f32[384,1024]{1,0:T(8,128)} %collective-permute-done.14.refs_2_), custom_call_target="tpu_custom_call" | custom-call | bytes 1572864 | tf_op jit(solution)/shard_map/choose/pallas_call | solution.py:238
  149.0 3.0 %collective-permute-done.18.refs_3_ = f32[384,1024]{1,0:T(8,128)} collective-permute-done((f32[384,1024]{1,0:T(8,128)}, f32[384,1024]{1,0:T(8,128)}, u32[]{:S(2)}, u32[]{:S(2)}) %collective-permute-start.18) | collective-permute-done | bytes 1572896 | tf_op jit(solution)/shard_map/ppermute | solution.py:309
  152.1 1.6 collective-permute-start.19
  154.2 1.6 collective-permute-start.20
  155.8 15.3 %panels.7 = (f32[512,16384]{1,0:T(8,128)}, f32[2,512,1024]{2,1,0:T(8,128)}) custom-call(s32[2]{0:T(128)} %get-tuple-element.84.ids_ref, bf16[1024,1536]{1,0:T(8,128)(2,1)} %left_operand.1.left_hbm, f32[384,1024]{1,0:T(8,128)} %collective-permute-done.4.refs_0_, f32[384,1024]{1,0:T(8,128)} %collective-permute-done.15.refs_1_, ...), custom_call_target="tpu_custom_call", output_to_operand_aliasing={{0}: (6, {})} | custom-call | flops 96636764160 | bytes 14680064 | tf_op jit(solution)/shard_map/panels/pallas_call | solution.py:170
  171.3 1.4 collective-permute-start.23
  172.7 1.5 collective-permute-start.22
  174.1 0.9 collective-permute-start.21
  175.0 12.5 %panels.8 = (f32[512,16384]{1,0:T(8,128)}, f32[2,512,640]{2,1,0:T(8,128)}) custom-call(s32[5]{0:T(128)} %stack.98.ids_ref, bf16[1024,1536]{1,0:T(8,128)(2,1)} %left_operand.1.left_hbm, f32[384,640]{1,0:T(8,128)} %get-tuple-element.82.refs_0_, f32[384,640]{1,0:T(8,128)} %collective-permute-done.16.refs_1_, ...), custom_call_target="tpu_custom_call", output_to_operand_aliasing={{0}: (8, {})} | custom-call | flops 60397977600 | bytes 9175040 | tf_op jit(solution)/shard_map/panels/pallas_call | solution.py:170
  187.6 1.0 collective-permute-done.21.refs_1_
  188.6 9.6 %panels.9 = (f32[512,16384]{1,0:T(8,128)}, f32[2,512,384]{2,1,0:T(8,128)}) custom-call(s32[5]{0:T(128)} %stack.101.ids_ref, bf16[1024,1536]{1,0:T(8,128)(2,1)} %left_operand.1.left_hbm, f32[384,384]{1,0:T(8,128)} %get-tuple-element.89.refs_0_, f32[384,384]{1,0:T(8,128)} %collective-permute-done.21.refs_1_, ...), custom_call_target="tpu_custom_call", output_to_operand_aliasing={{0}: (8, {})} | custom-call | flops 36238786560 | bytes 5505024 | tf_op jit(solution)/shard_map/panels/pallas_call | solution.py:170
  198.8 3.5 %place.4.refs_1_ = f32[512,16384]{1,0:T(8,128)} custom-call(s32[2]{0:T(128)} %get-tuple-element.55.ids_ref, f32[2,512,640]{2,1,0:T(8,128)} %collective-permute-done.27.refs_0_, f32[512,16384]{1,0:T(8,128)} %get-tuple-element.104.refs_1_), custom_call_target="tpu_custom_call", output_to_operand_aliasing={{}: (2, {})} | custom-call | bytes 5242880 | tf_op jit(solution)/shard_map/place/pallas_call | solution.py:272
  202.3 3.0 %place.5 = f32[512,16384]{1,0:T(8,128)} custom-call(s32[2]{0:T(128)} %get-tuple-element.55.ids_ref, f32[2,512,384]{2,1,0:T(8,128)} %collective-permute-done.26.refs_0_, f32[512,16384]{1,0:T(8,128)} %place.4.refs_1_), custom_call_target="tpu_custom_call", output_to_operand_aliasing={{}: (2, {})} | custom-call | bytes 3145728 | tf_op jit(solution)/shard_map/place/pallas_call | solution.py:272
  (34 shorter events, 2.9 us)
Async XLA Ops:
  0.0 14.9 %collective-permute-start = (f32[384,1024]{1,0:T(8,128)}, f32[384,1024]{1,0:T(8,128)}, u32[]{:S(2)}, u32[]{:S(2)}) collective-permute-start(f32[384,1024]{1,0:T(8,128)} %refs_0_.1), channel_id=1, source_target_pairs={{8,16},{10,18},{12,20},{14,22},{16,8},{18,10},{20,12},{22,14},{9,1... | collective-permute-start | bytes 4718600 | tf_op jit(solution)/shard_map/ppermute | solution.py:312
  1.9 37.5 %collective-permute-start.2 = (f32[384,1024]{1,0:T(8,128)}, f32[384,1024]{1,0:T(8,128)S(1)}, u32[]{:S(2)}, u32[]{:S(2)}) collective-permute-start(f32[384,1024]{1,0:T(8,128)} %refs_0_.1), channel_id=1, source_target_pairs={{0,1},{1,0},{2,3},{3,2},{4,5},{5,4},{6,7},{7,6},{8,9},{9,8},{10,11... | collective-permute-start | bytes 4718600 | tf_op jit(solution)/shard_map/ppermute | solution.py:308
  4.8 36.2 %collective-permute-start.6 = (f32[384,1024]{1,0:T(8,128)}, f32[384,1024]{1,0:T(8,128)}, u32[]{:S(2)}, u32[]{:S(2)}) collective-permute-start(f32[384,1024]{1,0:T(8,128)} %refs_0_.1), channel_id=1, source_target_pairs={{0,4},{2,6},{4,0},{6,2},{8,12},{10,14},{12,8},{14,10},{16,20},{18,... | collective-permute-start | bytes 4718600 | tf_op jit(solution)/shard_map/ppermute | solution.py:309
  6.3 37.2 %collective-permute-start.4 = (f32[384,1024]{1,0:T(8,128)}, f32[384,1024]{1,0:T(8,128)}, u32[]{:S(2)}, u32[]{:S(2)}) collective-permute-start(f32[384,1024]{1,0:T(8,128)} %refs_0_.1), channel_id=1, source_target_pairs={{0,8},{2,10},{4,12},{6,14},{8,0},{10,2},{12,4},{14,6},{16,24},{18,... | collective-permute-start | bytes 4718600 | tf_op jit(solution)/shard_map/ppermute | solution.py:310
  10.8 0.9 copy-start
  11.7 3.2 %collective-permute-start.1 = (f32[384,512]{1,0:T(8,128)S(1)}, f32[384,512]{1,0:T(8,128)S(1)}, u32[]{:S(2)}, u32[]{:S(2)}) collective-permute-start(f32[384,512]{1,0:T(8,128)S(1)} %constant_dynamic-slice_fusion.1.refs_0_), channel_id=1, source_target_pairs={{0,2},{2,0},{4,6},{6,4},{8,10},{10,8},{12,14},{14,12},{16,18},{18,... | collective-permute-start | bytes 2359304 | tf_op jit(solution)/shard_map/ppermute | solution.py:314
  14.9 32.1 %copy-start.2 = (f32[384,512]{1,0:T(8,128)}, f32[384,512]{1,0:T(8,128)S(1)}, u32[]{:S(2)}) copy-start(f32[384,512]{1,0:T(8,128)S(1)} %collective-permute-done.1.refs_2_) | copy-start | bytes 2359300
  39.4 9.4 %copy-start.3 = (f32[384,1024]{1,0:T(8,128)}, f32[384,1024]{1,0:T(8,128)S(1)}, u32[]{:S(2)}) copy-start(f32[384,1024]{1,0:T(8,128)S(1)} %collective-permute-done.2.refs_1_) | copy-start | bytes 4718596
  41.0 35.3 %collective-permute-start.7 = (f32[384,1024]{1,0:T(8,128)}, f32[384,1024]{1,0:T(8,128)}, u32[]{:S(2)}, u32[]{:S(2)}) collective-permute-start(f32[384,1024]{1,0:T(8,128)} %collective-permute-done.6.refs_2_), channel_id=1, source_target_pairs={{0,1},{1,0},{2,3},{3,2},{4,5},{5,4},{6,7},{7,6},{8,9},{9,8},{10,11... | collective-permute-start | bytes 4718600 | tf_op jit(solution)/shard_map/ppermute | solution.py:308
  43.5 35.0 %collective-permute-start.8 = (f32[384,1024]{1,0:T(8,128)}, f32[384,1024]{1,0:T(8,128)}, u32[]{:S(2)}, u32[]{:S(2)}) collective-permute-start(f32[384,1024]{1,0:T(8,128)} %collective-permute-done.refs_1_), channel_id=1, source_target_pairs={{0,8},{2,10},{4,12},{6,14},{8,0},{10,2},{12,4},{14,6},{16,24},{18,... | collective-permute-start | bytes 4718600 | tf_op jit(solution)/shard_map/ppermute | solution.py:310
  45.2 37.8 %collective-permute-start.13 = (f32[384,1024]{1,0:T(8,128)}, f32[384,1024]{1,0:T(8,128)}, u32[]{:S(2)}, u32[]{:S(2)}) collective-permute-start(f32[384,1024]{1,0:T(8,128)} %collective-permute-done.4.refs_0_), channel_id=1, source_target_pairs={{0,4},{2,6},{4,0},{6,2},{8,12},{10,14},{12,8},{14,10},{16,20},{18,... | collective-permute-start | bytes 4718600 | tf_op jit(solution)/shard_map/ppermute | solution.py:309
  46.1 0.9 copy-start.1
  47.0 2.4 %collective-permute-start.3 = (f32[384,512]{1,0:T(8,128)S(1)}, f32[384,512]{1,0:T(8,128)}, u32[]{:S(2)}, u32[]{:S(2)}) collective-permute-start(f32[384,512]{1,0:T(8,128)S(1)} %constant_dynamic-slice_fusion.refs_1_), channel_id=1, source_target_pairs={{0,2},{2,0},{4,6},{6,4},{8,10},{10,8},{12,14},{14,12},{16,18},{18,... | collective-permute-start | bytes 2359304 | tf_op jit(solution)/shard_map/ppermute | solution.py:314
  47.0 66.0 %collective-permute-start.5 = (f32[384,1024]{1,0:T(8,128)}, f32[384,1024]{1,0:T(8,128)}, u32[]{:S(2)}, u32[]{:S(2)}) collective-permute-start(f32[384,1024]{1,0:T(8,128)} %collective-permute-done.4.refs_0_), channel_id=1, source_target_pairs={{8,16},{10,18},{12,20},{14,22},{16,8},{18,10},{20,12},{22,14},{9,1... | collective-permute-start | bytes 4718600 | tf_op jit(solution)/shard_map/ppermute | solution.py:312
  78.4 34.6 %collective-permute-start.9 = (f32[384,1024]{1,0:T(8,128)}, f32[384,1024]{1,0:T(8,128)}, u32[]{:S(2)}, u32[]{:S(2)}) collective-permute-start(f32[384,1024]{1,0:T(8,128)} %collective-permute-done.7.refs_3_), channel_id=1, source_target_pairs={{0,8},{2,10},{4,12},{6,14},{8,0},{10,2},{12,4},{14,6},{16,24},{18,... | collective-permute-start | bytes 4718600 | tf_op jit(solution)/shard_map/ppermute | solution.py:310
  82.1 33.5 %collective-permute-start.12 = (f32[384,1024]{1,0:T(8,128)}, f32[384,1024]{1,0:T(8,128)}, u32[]{:S(2)}, u32[]{:S(2)}) collective-permute-start(f32[384,1024]{1,0:T(8,128)} %choose.2.refs_0_), channel_id=1, source_target_pairs={{0,1},{1,0},{2,3},{3,2},{4,5},{5,4},{6,7},{7,6},{8,9},{9,8},{10,11... | collective-permute-start | bytes 4718600 | tf_op jit(solution)/shard_map/ppermute | solution.py:308
  83.0 34.6 %collective-permute-start.17 = (f32[384,1024]{1,0:T(8,128)}, f32[384,1024]{1,0:T(8,128)}, u32[]{:S(2)}, u32[]{:S(2)}) collective-permute-start(f32[384,1024]{1,0:T(8,128)} %choose.2.refs_0_), channel_id=1, source_target_pairs={{0,4},{2,6},{4,0},{6,2},{8,12},{10,14},{12,8},{14,10},{16,20},{18,... | collective-permute-start | bytes 4718600 | tf_op jit(solution)/shard_map/ppermute | solution.py:309
  100.0 35.1 %collective-permute-start.11 = (f32[2,512,1024]{2,1,0:T(8,128)}, f32[2,512,1024]{2,1,0:T(8,128)}, u32[]{:S(2)}, u32[]{:S(2)}) collective-permute-start(f32[2,512,1024]{2,1,0:T(8,128)} %get-tuple-element.68), channel_id=1, source_target_pairs={{0,2},{2,0},{4,6},{6,4},{8,10},{10,8},{12,14},{14,12},{16,18},{18,... | collective-permute-start | bytes 12582920 | tf_op jit(solution)/shard_map/ppermute | solution.py:314
  113.0 33.2 %collective-permute-start.10 = (f32[384,1024]{1,0:T(8,128)}, f32[384,1024]{1,0:T(8,128)}, u32[]{:S(2)}, u32[]{:S(2)}) collective-permute-start(f32[384,1024]{1,0:T(8,128)} %collective-permute-done.5.refs_1_), channel_id=1, source_target_pairs={{0,8},{2,10},{4,12},{6,14},{8,0},{10,2},{12,4},{14,6},{16,24},{18,... | collective-permute-start | bytes 4718600 | tf_op jit(solution)/shard_map/ppermute | solution.py:310
  117.6 34.5 %collective-permute-start.18 = (f32[384,1024]{1,0:T(8,128)}, f32[384,1024]{1,0:T(8,128)}, u32[]{:S(2)}, u32[]{:S(2)}) collective-permute-start(f32[384,1024]{1,0:T(8,128)} %collective-permute-done.12.refs_1_), channel_id=1, source_target_pairs={{0,4},{2,6},{4,0},{6,2},{8,12},{10,14},{12,8},{14,10},{16,20},{18,... | collective-permute-start | bytes 4718600 | tf_op jit(solution)/shard_map/ppermute | solution.py:309
  119.1 34.6 %collective-permute-start.15 = (f32[384,1024]{1,0:T(8,128)}, f32[384,1024]{1,0:T(8,128)}, u32[]{:S(2)}, u32[]{:S(2)}) collective-permute-start(f32[384,1024]{1,0:T(8,128)} %collective-permute-done.4.refs_0_), channel_id=1, source_target_pairs={{0,1},{1,0},{2,3},{3,2},{4,5},{5,4},{6,7},{7,6},{8,9},{9,8},{10,11... | collective-permute-start | bytes 4718600 | tf_op jit(solution)/shard_map/ppermute | solution.py:308
  119.7 26.5 %collective-permute-start.14 = (f32[384,1024]{1,0:T(8,128)}, f32[384,1024]{1,0:T(8,128)}, u32[]{:S(2)}, u32[]{:S(2)}) collective-permute-start(f32[384,1024]{1,0:T(8,128)} %collective-permute-done.9.refs_3_), channel_id=1, source_target_pairs={{8,16},{10,18},{12,20},{14,22},{16,8},{18,10},{20,12},{22,14},{0,2... | collective-permute-start | bytes 4718600 | tf_op jit(solution)/shard_map/ppermute | solution.py:313
  135.0 40.0 %collective-permute-start.24 = (f32[2,512,1024]{2,1,0:T(8,128)}, f32[2,512,1024]{2,1,0:T(8,128)}, u32[]{:S(2)}, u32[]{:S(2)}) collective-permute-start(f32[2,512,1024]{2,1,0:T(8,128)} %get-tuple-element.94), channel_id=1, source_target_pairs={{0,2},{2,0},{4,6},{6,4},{8,10},{10,8},{12,14},{14,12},{16,18},{18,... | collective-permute-start | bytes 12582920 | tf_op jit(solution)/shard_map/ppermute | solution.py:314
  152.1 19.2 %collective-permute-start.19 = (f32[384,640]{1,0:T(8,128)}, f32[384,640]{1,0:T(8,128)}, u32[]{:S(2)}, u32[]{:S(2)}) collective-permute-start(f32[384,640]{1,0:T(8,128)} %get-tuple-element.82.refs_0_), channel_id=1, source_target_pairs={{0,4},{2,6},{4,0},{6,2},{8,12},{10,14},{12,8},{14,10},{16,20},{18,... | collective-permute-start | bytes 2949128 | tf_op jit(solution)/shard_map/ppermute | solution.py:309
  153.6 17.6 %collective-permute-start.16 = (f32[384,640]{1,0:T(8,128)}, f32[384,640]{1,0:T(8,128)}, u32[]{:S(2)}, u32[]{:S(2)}) collective-permute-start(f32[384,640]{1,0:T(8,128)} %get-tuple-element.82.refs_0_), channel_id=1, source_target_pairs={{0,1},{1,0},{2,3},{3,2},{4,5},{5,4},{6,7},{7,6},{8,9},{9,8},{10,11... | collective-permute-start | bytes 2949128 | tf_op jit(solution)/shard_map/ppermute | solution.py:308
  154.2 17.0 %collective-permute-start.20 = (f32[384,640]{1,0:T(8,128)}, f32[384,640]{1,0:T(8,128)}, u32[]{:S(2)}, u32[]{:S(2)}) collective-permute-start(f32[384,640]{1,0:T(8,128)} %get-tuple-element.83.refs_4_), channel_id=1, source_target_pairs={{0,8},{2,10},{4,12},{6,14},{8,0},{10,2},{12,4},{14,6},{16,24},{18,... | collective-permute-start | bytes 2949128 | tf_op jit(solution)/shard_map/ppermute | solution.py:310
  171.2 17.5 %collective-permute-start.25 = (f32[2,512,1024]{2,1,0:T(8,128)}, f32[2,512,1024]{2,1,0:T(8,128)}, u32[]{:S(2)}, u32[]{:S(2)}) collective-permute-start(f32[2,512,1024]{2,1,0:T(8,128)} %get-tuple-element.100), channel_id=1, source_target_pairs={{0,2},{2,0},{4,6},{6,4},{8,10},{10,8},{12,14},{14,12},{16,18},{18,... | collective-permute-start | bytes 12582920 | tf_op jit(solution)/shard_map/ppermute | solution.py:314
  171.3 16.3 %collective-permute-start.23 = (f32[384,384]{1,0:T(8,128)}, f32[384,384]{1,0:T(8,128)}, u32[]{:S(2)}, u32[]{:S(2)}) collective-permute-start(f32[384,384]{1,0:T(8,128)} %get-tuple-element.92.refs_4_), channel_id=1, source_target_pairs={{0,8},{2,10},{4,12},{6,14},{8,0},{10,2},{12,4},{14,6},{16,24},{18,... | collective-permute-start | bytes 1769480 | tf_op jit(solution)/shard_map/ppermute | solution.py:310
  172.7 14.9 %collective-permute-start.22 = (f32[384,384]{1,0:T(8,128)}, f32[384,384]{1,0:T(8,128)}, u32[]{:S(2)}, u32[]{:S(2)}) collective-permute-start(f32[384,384]{1,0:T(8,128)} %get-tuple-element.89.refs_0_), channel_id=1, source_target_pairs={{0,4},{2,6},{4,0},{6,2},{8,12},{10,14},{12,8},{14,10},{16,20},{18,... | collective-permute-start | bytes 1769480 | tf_op jit(solution)/shard_map/ppermute | solution.py:309
  174.1 14.5 %collective-permute-start.21 = (f32[384,384]{1,0:T(8,128)}, f32[384,384]{1,0:T(8,128)}, u32[]{:S(2)}, u32[]{:S(2)}) collective-permute-start(f32[384,384]{1,0:T(8,128)} %get-tuple-element.89.refs_0_), channel_id=1, source_target_pairs={{0,1},{1,0},{2,3},{3,2},{4,5},{5,4},{6,7},{7,6},{8,9},{9,8},{10,11... | collective-permute-start | bytes 1769480 | tf_op jit(solution)/shard_map/ppermute | solution.py:308
  188.6 10.2 %collective-permute-start.27 = (f32[2,512,640]{2,1,0:T(8,128)}, f32[2,512,640]{2,1,0:T(8,128)}, u32[]{:S(2)}, u32[]{:S(2)}) collective-permute-start(f32[2,512,640]{2,1,0:T(8,128)} %get-tuple-element.103), channel_id=1, source_target_pairs={{0,2},{2,0},{4,6},{6,4},{8,10},{10,8},{12,14},{14,12},{16,18},{18,... | collective-permute-start | bytes 7864328 | tf_op jit(solution)/shard_map/ppermute | solution.py:314
  198.2 4.1 %collective-permute-start.26 = (f32[2,512,384]{2,1,0:T(8,128)}, f32[2,512,384]{2,1,0:T(8,128)}, u32[]{:S(2)}, u32[]{:S(2)}) collective-permute-start(f32[2,512,384]{2,1,0:T(8,128)} %get-tuple-element.102), channel_id=1, source_target_pairs={{0,2},{2,0},{4,6},{6,4},{8,10},{10,8},{12,14},{14,12},{16,18},{18,... | collective-permute-start | bytes 4718600 | tf_op jit(solution)/shard_map/ppermute | solution.py:314

commit v6 on v5

--- a/solution.py
+++ b/solution.py
@@ -53,7 +53,10 @@
     most = max(map(sum, sizes))
     height, depth = done.shape[1], left_ref.shape[1] // 2
     left = [left_ref.at[:, pl.ds(k * depth, depth)] for k in range(2)]
-    left_copy = pltpu.make_async_copy(left_hbm.at[pl.ds(0, height)], left_ref, left_sem)
+    left_copies = [
+        pltpu.make_async_copy(left_hbm.at[pl.ds(0, height), pl.ds(k * depth, depth)], left[k], left_sem.at[k])
+        for k in range(2)
+    ]
 
     loads, at = [], 0
     for index, counts in enumerate(sizes):
@@ -92,10 +95,12 @@
         for copy in copies:
             copy.wait()
 
-    start(loads[0][0] + [left_copy])
+    start(loads[0][0] + left_copies)
     for copies in loads[0][1:]:
         start(copies)
-    left_copy.wait()
+    left_copies[0].wait()
+    if tile != 512:
+        left_copies[1].wait()
 
     def turn_body(turn, carry):
         index, column = turn // tiles, pl.multiple_of(lax.rem(turn, tiles) * tile, 128)
@@ -126,7 +131,14 @@
         halves = [split_high_low(value) for value in block[:2]]
         high, low = (jnp.concatenate(pieces, axis=0) for pieces in zip(*halves))
         dot = functools.partial(jnp.dot, preferred_element_type=jnp.float32)
-        product = dot(left[0][...], high) + dot(left[0][...], low) + dot(left[1][...], high)
+        product = dot(left[0][...], high) + dot(left[0][...], low)
+        if tile == 512:
+
+            @pl.when(turn == 0)
+            def rest_of_left():
+                left_copies[1].wait()
+
+        product += dot(left[1][...], high)
         if diagonal is not None:
             row_ids = lax.broadcasted_iota(jnp.int32, product.shape, 0) + ids_ref[ids_ref.shape[0] - 1]
             col_ids = lax.broadcasted_iota(jnp.int32, product.shape, 1) + column
@@ -185,7 +197,7 @@
             pltpu.VMEM((height, left.shape[1]), left.dtype),
             pltpu.VMEM((2, most, depth, width), jnp.float32),
             pltpu.VMEM((2, height, tile), jnp.float32),
-            pltpu.SemaphoreType.DMA,
+            pltpu.SemaphoreType.DMA((2,)),
             pltpu.SemaphoreType.DMA((2, most, width // tile)),
             pltpu.SemaphoreType.DMA((2, 2)),
             pltpu.SemaphoreType.DMA((max(1, len(received)), stacked, 2)),

time: 206 us -> 205 us (level)
  transfers between devices with their start and end apart: 28 -> 28, of which waited for: 12 -> 13; matrix products, arithmetic and copies ran while one was open for 2% -> 2% of each run, Pallas kernels for 42% -> 41%
where the time goes in v6:
time: 205 us
  Pallas kernels  86.8 us (42%)
  waiting for transfers between devices  80.9 us (39%)
  starting transfers between devices  30.7 us (15%)
  local copies, waits for them, and re-layouts  4.27 us (2%)
    pallas_call x5, Pallas kernels, panels(): pl.pallas_call(functools.partial(panel_kernel, sizes, diagonal, part or (...  66.6 us
    ppermute x6, waiting for transfers between devices, rounds(): along_x = lambda v: lax.ppermute(v, 'grp', [(0, 1), (1, 0)])  48.7 us
    ppermute x6, waiting for transfers between devices, rounds(): pair_z = lambda v: lax.ppermute(v, 'loop', [(i, i ^ 4) for i in range(16)])  24.8 us
    ppermute x6, starting transfers between devices, rounds(): pair_z = lambda v: lax.ppermute(v, 'loop', [(i, i ^ 4) for i in range(16)])  11.1 us
    pallas_call x3, Pallas kernels, place(): pl.pallas_call(functools.partial(place_kernel, [part for _, part in recei...  10.8 us
    ppermute x6, starting transfers between devices, rounds(): along_y = lambda v: lax.ppermute(v, 'loop', [(i, i ^ 2) for i in range(16)])  8.42 us
    ppermute x6, waiting for transfers between devices, rounds(): along_y = lambda v: lax.ppermute(v, 'loop', [(i, i ^ 2) for i in range(16)])  6.74 us
    ppermute x6, starting transfers between devices, rounds(): along_x = lambda v: lax.ppermute(v, 'grp', [(0, 1), (1, 0)])  6.19 us
  transfers between devices with their start and end apart: 28, of which 13 were waited for; matrix products, arithmetic and copies ran while one was open for 2% of the time, Pallas kernels for 41%

profile of v6, /device:TPU:0, one launch (start us, length us, event | category | flops | bytes accessed | tf_op | source)
XLA Modules:
  0.0 204.7 jit_solution(7894534712862076311)
XLA Ops:
  0.0 1.9 collective-permute-start
  1.9 2.9 %collective-permute-start.2 = (f32[384,1024]{1,0:T(8,128)}, f32[384,1024]{1,0:T(8,128)S(1)}, u32[]{:S(2)}, u32[]{:S(2)}) collective-permute-start(f32[384,1024]{1,0:T(8,128)} %refs_0_.1), channel_id=1, source_target_pairs={{0,1},{1,0},{2,3},{3,2},{4,5},{5,4},{6,7},{7,6},{8,9},{9,8},{10,11... | collective-permute-start | bytes 4718600 | tf_op jit(solution)/shard_map/ppermute | solution.py:320
  4.8 1.5 collective-permute-start.6
  6.3 3.3 %collective-permute-start.4 = (f32[384,1024]{1,0:T(8,128)}, f32[384,1024]{1,0:T(8,128)}, u32[]{:S(2)}, u32[]{:S(2)}) collective-permute-start(f32[384,1024]{1,0:T(8,128)} %refs_0_.1), channel_id=1, source_target_pairs={{0,8},{2,10},{4,12},{6,14},{8,0},{10,2},{12,4},{14,6},{16,24},{18,... | collective-permute-start | bytes 4718600 | tf_op jit(solution)/shard_map/ppermute | solution.py:322
  9.6 1.2 constant_dynamic-slice_fusion.1.refs_0_
  10.8 0.9 copy-done
  11.7 0.6 stack.101.ids_ref
  12.3 0.6 stack.98.ids_ref
  12.9 0.7 pad_add_fusion.ids_ref
  13.6 0.6 pad_add_fusion.3
  14.2 0.7 pad_add_fusion.1
  14.9 24.5 %collective-permute-done.2.refs_1_ = f32[384,1024]{1,0:T(8,128)S(1)} collective-permute-done((f32[384,1024]{1,0:T(8,128)}, f32[384,1024]{1,0:T(8,128)S(1)}, u32[]{:S(2)}, u32[]{:S(2)}) %collective-permute-start.2) | collective-permute-done | bytes 1572896 | tf_op jit(solution)/shard_map/ppermute | solution.py:320
  39.4 1.6 collective-permute-done.6.refs_2_
  41.3 2.2 %collective-permute-done.4.refs_0_ = f32[384,1024]{1,0:T(8,128)} collective-permute-done((f32[384,1024]{1,0:T(8,128)}, f32[384,1024]{1,0:T(8,128)}, u32[]{:S(2)}, u32[]{:S(2)}) %collective-permute-start.4) | collective-permute-done | bytes 1572896 | tf_op jit(solution)/shard_map/ppermute | solution.py:322
  43.5 1.7 collective-permute-start.8
  45.2 0.8 collective-permute-start.13
  46.1 0.9 copy-done.1
  47.0 1.8 collective-permute-start.5
  48.8 0.6 collective-permute-done.3.refs_3_
  49.4 4.4 %left_operand.1.left_hbm = bf16[1024,1536]{1,0:T(8,128)(2,1)} custom-call(f32[384,512]{1,0:T(8,128)} %copy-done, f32[384,512]{1,0:T(8,128)} %copy-done.1, f32[384,512]{1,0:T(8,128)} %copy-done.2, f32[384,512]{1,0:T(8,128)} %collective-permute-done.3.refs_3_), custom_call_target="tpu_custom_call" | custom-call | flops 1024 | bytes 1024 | tf_op jit(solution)/shard_map/left_operand/pallas_call | solution.py:35
  53.7 22.5 %collective-permute-done.7.refs_3_ = f32[384,1024]{1,0:T(8,128)} collective-permute-done((f32[384,1024]{1,0:T(8,128)}, f32[384,1024]{1,0:T(8,128)}, u32[]{:S(2)}, u32[]{:S(2)}) %collective-permute-start.7) | collective-permute-done | bytes 1572896 | tf_op jit(solution)/shard_map/ppermute | solution.py:320
  76.2 2.2 %collective-permute-done.8.refs_0_ = f32[384,1024]{1,0:T(8,128)} collective-permute-done((f32[384,1024]{1,0:T(8,128)}, f32[384,1024]{1,0:T(8,128)}, u32[]{:S(2)}, u32[]{:S(2)}) %collective-permute-start.8) | collective-permute-done | bytes 1572896 | tf_op jit(solution)/shard_map/ppermute | solution.py:322
  78.4 1.4 collective-permute-start.9
  79.9 2.2 %choose.2.refs_0_ = f32[384,1024]{1,0:T(8,128)} custom-call(s32[1]{0:T(128)} %bitcast.11.flag_ref, f32[384,1024]{1,0:T(8,128)} %collective-permute-done.8.refs_0_, f32[384,1024]{1,0:T(8,128)} %collective-permute-done.refs_1_), custom_call_target="tpu_custom_call" | custom-call | bytes 1572864 | tf_op jit(solution)/shard_map/choose/pallas_call | solution.py:250
  82.1 0.9 collective-permute-start.12
  83.0 1.5 collective-permute-start.17
  84.5 14.9 %panels.5 = (f32[512,16384]{1,0:T(8,128)}, f32[2,512,1024]{2,1,0:T(8,128)}) custom-call(s32[3]{0:T(128)} %pad_add_fusion.ids_ref, bf16[1024,1536]{1,0:T(8,128)(2,1)} %left_operand.1.left_hbm, f32[384,1024]{1,0:T(8,128)} %refs_0_.1, f32[384,1024]{1,0:T(8,128)} %copy-done.3, f32[384,1024]{1,0:T(8,128)} %collective-permute-done.6.refs_2_, ...), custom_call_target="tpu_custom_call" | custom-call | flops 96636764160 | bytes 14680064 | tf_op jit(solution)/shard_map/panels/pallas_call | solution.py:182
  99.5 13.5 %collective-permute-done.9.refs_3_ = f32[384,1024]{1,0:T(8,128)} collective-permute-done((f32[384,1024]{1,0:T(8,128)}, f32[384,1024]{1,0:T(8,128)}, u32[]{:S(2)}, u32[]{:S(2)}) %collective-permute-start.9) | collective-permute-done | bytes 1572896 | tf_op jit(solution)/shard_map/ppermute | solution.py:322
  113.0 1.4 collective-permute-start.10
  114.4 1.2 collective-permute-done.12.refs_1_
  115.7 1.9 collective-permute-done.17.refs_2_
  117.6 1.5 collective-permute-start.18
  119.7 14.8 %panels.6 = (f32[512,16384]{1,0:T(8,128)}, f32[2,512,1024]{2,1,0:T(8,128)}) custom-call(s32[2]{0:T(128)} %get-tuple-element.69.ids_ref, bf16[1024,1536]{1,0:T(8,128)(2,1)} %left_operand.1.left_hbm, f32[384,1024]{1,0:T(8,128)} %choose.2.refs_0_, f32[384,1024]{1,0:T(8,128)} %collective-permute-done.12.refs_1_, ...), custom_call_target="tpu_custom_call", output_to_operand_aliasing={{0}: (6, {})} | custom-call | flops 96636764160 | bytes 14680064 | tf_op jit(solution)/shard_map/panels/pallas_call | solution.py:182
  135.1 4.3 %place.3.refs_4_ = f32[512,16384]{1,0:T(8,128)} custom-call(s32[2]{0:T(128)} %get-tuple-element.67.ids_ref, f32[2,512,1024]{2,1,0:T(8,128)} %collective-permute-done.11.refs_0_, f32[512,16384]{1,0:T(8,128)} %get-tuple-element.73.refs_1_), custom_call_target="tpu_custom_call", output_to_operand_aliasing={{}: (2, {})} | custom-call | bytes 8388608 | tf_op jit(solution)/shard_map/place/pallas_call | solution.py:284
  139.4 6.8 %collective-permute-done.10.refs_0_ = f32[384,1024]{1,0:T(8,128)} collective-permute-done((f32[384,1024]{1,0:T(8,128)}, f32[384,1024]{1,0:T(8,128)}, u32[]{:S(2)}, u32[]{:S(2)}) %collective-permute-start.10) | collective-permute-done | bytes 1572896 | tf_op jit(solution)/shard_map/ppermute | solution.py:322
  146.2 2.8 %choose.3 = (f32[384,640]{1,0:T(8,128)}, f32[384,640]{1,0:T(8,128)}, f32[384,384]{1,0:T(8,128)}, f32[384,384]{1,0:T(8,128)}) custom-call(s32[1]{0:T(128)} %bitcast.11.flag_ref, f32[384,1024]{1,0:T(8,128)} %collective-permute-done.10.refs_0_, f32[384,1024]{1,0:T(8,128)} %collective-permute-done.5.refs_1_, f32[384,1024]{1,0:T(8,128)} %collective-permute-done.14.refs_2_), custom_call_target="tpu_custom_call" | custom-call | bytes 1572864 | tf_op jit(solution)/shard_map/choose/pallas_call | solution.py:250
  149.0 3.0 %collective-permute-done.18.refs_3_ = f32[384,1024]{1,0:T(8,128)} collective-permute-done((f32[384,1024]{1,0:T(8,128)}, f32[384,1024]{1,0:T(8,128)}, u32[]{:S(2)}, u32[]{:S(2)}) %collective-permute-start.18) | collective-permute-done | bytes 1572896 | tf_op jit(solution)/shard_map/ppermute | solution.py:321
  152.1 1.6 collective-permute-start.19
  153.6 0.6 collective-permute-start.16
  154.2 1.6 collective-permute-start.20
  155.8 14.8 %panels.7 = (f32[512,16384]{1,0:T(8,128)}, f32[2,512,1024]{2,1,0:T(8,128)}) custom-call(s32[2]{0:T(128)} %get-tuple-element.84.ids_ref, bf16[1024,1536]{1,0:T(8,128)(2,1)} %left_operand.1.left_hbm, f32[384,1024]{1,0:T(8,128)} %collective-permute-done.4.refs_0_, f32[384,1024]{1,0:T(8,128)} %collective-permute-done.15.refs_1_, ...), custom_call_target="tpu_custom_call", output_to_operand_aliasing={{0}: (6, {})} | custom-call | flops 96636764160 | bytes 14680064 | tf_op jit(solution)/shard_map/panels/pallas_call | solution.py:182
  171.0 1.7 collective-permute-start.23
  172.7 1.5 collective-permute-start.22
  174.1 0.9 collective-permute-start.21
  175.0 12.5 %panels.8 = (f32[512,16384]{1,0:T(8,128)}, f32[2,512,640]{2,1,0:T(8,128)}) custom-call(s32[5]{0:T(128)} %stack.98.ids_ref, bf16[1024,1536]{1,0:T(8,128)(2,1)} %left_operand.1.left_hbm, f32[384,640]{1,0:T(8,128)} %get-tuple-element.82.refs_0_, f32[384,640]{1,0:T(8,128)} %collective-permute-done.16.refs_1_, ...), custom_call_target="tpu_custom_call", output_to_operand_aliasing={{0}: (8, {})} | custom-call | flops 60397977600 | bytes 9175040 | tf_op jit(solution)/shard_map/panels/pallas_call | solution.py:182
  188.1 9.6 %panels.9 = (f32[512,16384]{1,0:T(8,128)}, f32[2,512,384]{2,1,0:T(8,128)}) custom-call(s32[5]{0:T(128)} %stack.101.ids_ref, bf16[1024,1536]{1,0:T(8,128)(2,1)} %left_operand.1.left_hbm, f32[384,384]{1,0:T(8,128)} %get-tuple-element.89.refs_0_, f32[384,384]{1,0:T(8,128)} %collective-permute-done.21.refs_1_, ...), custom_call_target="tpu_custom_call", output_to_operand_aliasing={{0}: (8, {})} | custom-call | flops 36238786560 | bytes 5505024 | tf_op jit(solution)/shard_map/panels/pallas_call | solution.py:182
  198.3 3.5 %place.4.refs_1_ = f32[512,16384]{1,0:T(8,128)} custom-call(s32[2]{0:T(128)} %get-tuple-element.55.ids_ref, f32[2,512,640]{2,1,0:T(8,128)} %collective-permute-done.27.refs_0_, f32[512,16384]{1,0:T(8,128)} %get-tuple-element.104.refs_1_), custom_call_target="tpu_custom_call", output_to_operand_aliasing={{}: (2, {})} | custom-call | bytes 5242880 | tf_op jit(solution)/shard_map/place/pallas_call | solution.py:284
  201.8 3.0 %place.5 = f32[512,16384]{1,0:T(8,128)} custom-call(s32[2]{0:T(128)} %get-tuple-element.55.ids_ref, f32[2,512,384]{2,1,0:T(8,128)} %collective-permute-done.26.refs_0_, f32[512,16384]{1,0:T(8,128)} %place.4.refs_1_), custom_call_target="tpu_custom_call", output_to_operand_aliasing={{}: (2, {})} | custom-call | bytes 3145728 | tf_op jit(solution)/shard_map/place/pallas_call | solution.py:284
  (34 shorter events, 3.1 us)
Async XLA Ops:
  0.0 14.9 %collective-permute-start = (f32[384,1024]{1,0:T(8,128)}, f32[384,1024]{1,0:T(8,128)}, u32[]{:S(2)}, u32[]{:S(2)}) collective-permute-start(f32[384,1024]{1,0:T(8,128)} %refs_0_.1), channel_id=1, source_target_pairs={{8,16},{10,18},{12,20},{14,22},{16,8},{18,10},{20,12},{22,14},{9,1... | collective-permute-start | bytes 4718600 | tf_op jit(solution)/shard_map/ppermute | solution.py:324
  1.9 37.5 %collective-permute-start.2 = (f32[384,1024]{1,0:T(8,128)}, f32[384,1024]{1,0:T(8,128)S(1)}, u32[]{:S(2)}, u32[]{:S(2)}) collective-permute-start(f32[384,1024]{1,0:T(8,128)} %refs_0_.1), channel_id=1, source_target_pairs={{0,1},{1,0},{2,3},{3,2},{4,5},{5,4},{6,7},{7,6},{8,9},{9,8},{10,11... | collective-permute-start | bytes 4718600 | tf_op jit(solution)/shard_map/ppermute | solution.py:320
  4.8 36.2 %collective-permute-start.6 = (f32[384,1024]{1,0:T(8,128)}, f32[384,1024]{1,0:T(8,128)}, u32[]{:S(2)}, u32[]{:S(2)}) collective-permute-start(f32[384,1024]{1,0:T(8,128)} %refs_0_.1), channel_id=1, source_target_pairs={{0,4},{2,6},{4,0},{6,2},{8,12},{10,14},{12,8},{14,10},{16,20},{18,... | collective-permute-start | bytes 4718600 | tf_op jit(solution)/shard_map/ppermute | solution.py:321
  6.3 37.2 %collective-permute-start.4 = (f32[384,1024]{1,0:T(8,128)}, f32[384,1024]{1,0:T(8,128)}, u32[]{:S(2)}, u32[]{:S(2)}) collective-permute-start(f32[384,1024]{1,0:T(8,128)} %refs_0_.1), channel_id=1, source_target_pairs={{0,8},{2,10},{4,12},{6,14},{8,0},{10,2},{12,4},{14,6},{16,24},{18,... | collective-permute-start | bytes 4718600 | tf_op jit(solution)/shard_map/ppermute | solution.py:322
  10.8 0.9 copy-start
  11.7 3.2 %collective-permute-start.1 = (f32[384,512]{1,0:T(8,128)S(1)}, f32[384,512]{1,0:T(8,128)S(1)}, u32[]{:S(2)}, u32[]{:S(2)}) collective-permute-start(f32[384,512]{1,0:T(8,128)S(1)} %constant_dynamic-slice_fusion.1.refs_0_), channel_id=1, source_target_pairs={{0,2},{2,0},{4,6},{6,4},{8,10},{10,8},{12,14},{14,12},{16,18},{18,... | collective-permute-start | bytes 2359304 | tf_op jit(solution)/shard_map/ppermute | solution.py:326
  14.9 32.1 %copy-start.2 = (f32[384,512]{1,0:T(8,128)}, f32[384,512]{1,0:T(8,128)S(1)}, u32[]{:S(2)}) copy-start(f32[384,512]{1,0:T(8,128)S(1)} %collective-permute-done.1.refs_2_) | copy-start | bytes 2359300
  39.4 9.4 %copy-start.3 = (f32[384,1024]{1,0:T(8,128)}, f32[384,1024]{1,0:T(8,128)S(1)}, u32[]{:S(2)}) copy-start(f32[384,1024]{1,0:T(8,128)S(1)} %collective-permute-done.2.refs_1_) | copy-start | bytes 4718596
  41.0 35.3 %collective-permute-start.7 = (f32[384,1024]{1,0:T(8,128)}, f32[384,1024]{1,0:T(8,128)}, u32[]{:S(2)}, u32[]{:S(2)}) collective-permute-start(f32[384,1024]{1,0:T(8,128)} %collective-permute-done.6.refs_2_), channel_id=1, source_target_pairs={{0,1},{1,0},{2,3},{3,2},{4,5},{5,4},{6,7},{7,6},{8,9},{9,8},{10,11... | collective-permute-start | bytes 4718600 | tf_op jit(solution)/shard_map/ppermute | solution.py:320
  43.5 35.0 %collective-permute-start.8 = (f32[384,1024]{1,0:T(8,128)}, f32[384,1024]{1,0:T(8,128)}, u32[]{:S(2)}, u32[]{:S(2)}) collective-permute-start(f32[384,1024]{1,0:T(8,128)} %collective-permute-done.refs_1_), channel_id=1, source_target_pairs={{0,8},{2,10},{4,12},{6,14},{8,0},{10,2},{12,4},{14,6},{16,24},{18,... | collective-permute-start | bytes 4718600 | tf_op jit(solution)/shard_map/ppermute | solution.py:322
  45.2 37.8 %collective-permute-start.13 = (f32[384,1024]{1,0:T(8,128)}, f32[384,1024]{1,0:T(8,128)}, u32[]{:S(2)}, u32[]{:S(2)}) collective-permute-start(f32[384,1024]{1,0:T(8,128)} %collective-permute-done.4.refs_0_), channel_id=1, source_target_pairs={{0,4},{2,6},{4,0},{6,2},{8,12},{10,14},{12,8},{14,10},{16,20},{18,... | collective-permute-start | bytes 4718600 | tf_op jit(solution)/shard_map/ppermute | solution.py:321
  46.1 0.9 copy-start.1
  47.0 2.4 %collective-permute-start.3 = (f32[384,512]{1,0:T(8,128)S(1)}, f32[384,512]{1,0:T(8,128)}, u32[]{:S(2)}, u32[]{:S(2)}) collective-permute-start(f32[384,512]{1,0:T(8,128)S(1)} %constant_dynamic-slice_fusion.refs_1_), channel_id=1, source_target_pairs={{0,2},{2,0},{4,6},{6,4},{8,10},{10,8},{12,14},{14,12},{16,18},{18,... | collective-permute-start | bytes 2359304 | tf_op jit(solution)/shard_map/ppermute | solution.py:326
  47.0 66.0 %collective-permute-start.5 = (f32[384,1024]{1,0:T(8,128)}, f32[384,1024]{1,0:T(8,128)}, u32[]{:S(2)}, u32[]{:S(2)}) collective-permute-start(f32[384,1024]{1,0:T(8,128)} %collective-permute-done.4.refs_0_), channel_id=1, source_target_pairs={{8,16},{10,18},{12,20},{14,22},{16,8},{18,10},{20,12},{22,14},{9,1... | collective-permute-start | bytes 4718600 | tf_op jit(solution)/shard_map/ppermute | solution.py:324
  78.4 34.6 %collective-permute-start.9 = (f32[384,1024]{1,0:T(8,128)}, f32[384,1024]{1,0:T(8,128)}, u32[]{:S(2)}, u32[]{:S(2)}) collective-permute-start(f32[384,1024]{1,0:T(8,128)} %collective-permute-done.7.refs_3_), channel_id=1, source_target_pairs={{0,8},{2,10},{4,12},{6,14},{8,0},{10,2},{12,4},{14,6},{16,24},{18,... | collective-permute-start | bytes 4718600 | tf_op jit(solution)/shard_map/ppermute | solution.py:322
  82.1 33.5 %collective-permute-start.12 = (f32[384,1024]{1,0:T(8,128)}, f32[384,1024]{1,0:T(8,128)}, u32[]{:S(2)}, u32[]{:S(2)}) collective-permute-start(f32[384,1024]{1,0:T(8,128)} %choose.2.refs_0_), channel_id=1, source_target_pairs={{0,1},{1,0},{2,3},{3,2},{4,5},{5,4},{6,7},{7,6},{8,9},{9,8},{10,11... | collective-permute-start | bytes 4718600 | tf_op jit(solution)/shard_map/ppermute | solution.py:320
  83.0 34.6 %collective-permute-start.17 = (f32[384,1024]{1,0:T(8,128)}, f32[384,1024]{1,0:T(8,128)}, u32[]{:S(2)}, u32[]{:S(2)}) collective-permute-start(f32[384,1024]{1,0:T(8,128)} %choose.2.refs_0_), channel_id=1, source_target_pairs={{0,4},{2,6},{4,0},{6,2},{8,12},{10,14},{12,8},{14,10},{16,20},{18,... | collective-permute-start | bytes 4718600 | tf_op jit(solution)/shard_map/ppermute | solution.py:321
  99.4 35.1 %collective-permute-start.11 = (f32[2,512,1024]{2,1,0:T(8,128)}, f32[2,512,1024]{2,1,0:T(8,128)}, u32[]{:S(2)}, u32[]{:S(2)}) collective-permute-start(f32[2,512,1024]{2,1,0:T(8,128)} %get-tuple-element.68), channel_id=1, source_target_pairs={{0,2},{2,0},{4,6},{6,4},{8,10},{10,8},{12,14},{14,12},{16,18},{18,... | collective-permute-start | bytes 12582920 | tf_op jit(solution)/shard_map/ppermute | solution.py:326
  113.0 33.2 %collective-permute-start.10 = (f32[384,1024]{1,0:T(8,128)}, f32[384,1024]{1,0:T(8,128)}, u32[]{:S(2)}, u32[]{:S(2)}) collective-permute-start(f32[384,1024]{1,0:T(8,128)} %collective-permute-done.5.refs_1_), channel_id=1, source_target_pairs={{0,8},{2,10},{4,12},{6,14},{8,0},{10,2},{12,4},{14,6},{16,24},{18,... | collective-permute-start | bytes 4718600 | tf_op jit(solution)/shard_map/ppermute | solution.py:322
  117.6 34.5 %collective-permute-start.18 = (f32[384,1024]{1,0:T(8,128)}, f32[384,1024]{1,0:T(8,128)}, u32[]{:S(2)}, u32[]{:S(2)}) collective-permute-start(f32[384,1024]{1,0:T(8,128)} %collective-permute-done.12.refs_1_), channel_id=1, source_target_pairs={{0,4},{2,6},{4,0},{6,2},{8,12},{10,14},{12,8},{14,10},{16,20},{18,... | collective-permute-start | bytes 4718600 | tf_op jit(solution)/shard_map/ppermute | solution.py:321
  119.1 34.6 %collective-permute-start.15 = (f32[384,1024]{1,0:T(8,128)}, f32[384,1024]{1,0:T(8,128)}, u32[]{:S(2)}, u32[]{:S(2)}) collective-permute-start(f32[384,1024]{1,0:T(8,128)} %collective-permute-done.4.refs_0_), channel_id=1, source_target_pairs={{0,1},{1,0},{2,3},{3,2},{4,5},{5,4},{6,7},{7,6},{8,9},{9,8},{10,11... | collective-permute-start | bytes 4718600 | tf_op jit(solution)/shard_map/ppermute | solution.py:320
  119.7 26.5 %collective-permute-start.14 = (f32[384,1024]{1,0:T(8,128)}, f32[384,1024]{1,0:T(8,128)}, u32[]{:S(2)}, u32[]{:S(2)}) collective-permute-start(f32[384,1024]{1,0:T(8,128)} %collective-permute-done.9.refs_3_), channel_id=1, source_target_pairs={{8,16},{10,18},{12,20},{14,22},{16,8},{18,10},{20,12},{22,14},{0,2... | collective-permute-start | bytes 4718600 | tf_op jit(solution)/shard_map/ppermute | solution.py:325
  134.5 40.5 %collective-permute-start.24 = (f32[2,512,1024]{2,1,0:T(8,128)}, f32[2,512,1024]{2,1,0:T(8,128)}, u32[]{:S(2)}, u32[]{:S(2)}) collective-permute-start(f32[2,512,1024]{2,1,0:T(8,128)} %get-tuple-element.94), channel_id=1, source_target_pairs={{0,2},{2,0},{4,6},{6,4},{8,10},{10,8},{12,14},{14,12},{16,18},{18,... | collective-permute-start | bytes 12582920 | tf_op jit(solution)/shard_map/ppermute | solution.py:326
  152.1 18.9 %collective-permute-start.19 = (f32[384,640]{1,0:T(8,128)}, f32[384,640]{1,0:T(8,128)}, u32[]{:S(2)}, u32[]{:S(2)}) collective-permute-start(f32[384,640]{1,0:T(8,128)} %get-tuple-element.82.refs_0_), channel_id=1, source_target_pairs={{0,4},{2,6},{4,0},{6,2},{8,12},{10,14},{12,8},{14,10},{16,20},{18,... | collective-permute-start | bytes 2949128 | tf_op jit(solution)/shard_map/ppermute | solution.py:321
  153.6 17.3 %collective-permute-start.16 = (f32[384,640]{1,0:T(8,128)}, f32[384,640]{1,0:T(8,128)}, u32[]{:S(2)}, u32[]{:S(2)}) collective-permute-start(f32[384,640]{1,0:T(8,128)} %get-tuple-element.82.refs_0_), channel_id=1, source_target_pairs={{0,1},{1,0},{2,3},{3,2},{4,5},{5,4},{6,7},{7,6},{8,9},{9,8},{10,11... | collective-permute-start | bytes 2949128 | tf_op jit(solution)/shard_map/ppermute | solution.py:320
  154.2 16.8 %collective-permute-start.20 = (f32[384,640]{1,0:T(8,128)}, f32[384,640]{1,0:T(8,128)}, u32[]{:S(2)}, u32[]{:S(2)}) collective-permute-start(f32[384,640]{1,0:T(8,128)} %get-tuple-element.83.refs_4_), channel_id=1, source_target_pairs={{0,8},{2,10},{4,12},{6,14},{8,0},{10,2},{12,4},{14,6},{16,24},{18,... | collective-permute-start | bytes 2949128 | tf_op jit(solution)/shard_map/ppermute | solution.py:322
  170.6 17.5 %collective-permute-start.25 = (f32[2,512,1024]{2,1,0:T(8,128)}, f32[2,512,1024]{2,1,0:T(8,128)}, u32[]{:S(2)}, u32[]{:S(2)}) collective-permute-start(f32[2,512,1024]{2,1,0:T(8,128)} %get-tuple-element.100), channel_id=1, source_target_pairs={{0,2},{2,0},{4,6},{6,4},{8,10},{10,8},{12,14},{14,12},{16,18},{18,... | collective-permute-start | bytes 12582920 | tf_op jit(solution)/shard_map/ppermute | solution.py:326
  171.0 16.6 %collective-permute-start.23 = (f32[384,384]{1,0:T(8,128)}, f32[384,384]{1,0:T(8,128)}, u32[]{:S(2)}, u32[]{:S(2)}) collective-permute-start(f32[384,384]{1,0:T(8,128)} %get-tuple-element.92.refs_4_), channel_id=1, source_target_pairs={{0,8},{2,10},{4,12},{6,14},{8,0},{10,2},{12,4},{14,6},{16,24},{18,... | collective-permute-start | bytes 1769480 | tf_op jit(solution)/shard_map/ppermute | solution.py:322
  172.7 14.9 %collective-permute-start.22 = (f32[384,384]{1,0:T(8,128)}, f32[384,384]{1,0:T(8,128)}, u32[]{:S(2)}, u32[]{:S(2)}) collective-permute-start(f32[384,384]{1,0:T(8,128)} %get-tuple-element.89.refs_0_), channel_id=1, source_target_pairs={{0,4},{2,6},{4,0},{6,2},{8,12},{10,14},{12,8},{14,10},{16,20},{18,... | collective-permute-start | bytes 1769480 | tf_op jit(solution)/shard_map/ppermute | solution.py:321
  174.1 13.9 %collective-permute-start.21 = (f32[384,384]{1,0:T(8,128)}, f32[384,384]{1,0:T(8,128)}, u32[]{:S(2)}, u32[]{:S(2)}) collective-permute-start(f32[384,384]{1,0:T(8,128)} %get-tuple-element.89.refs_0_), channel_id=1, source_target_pairs={{0,1},{1,0},{2,3},{3,2},{4,5},{5,4},{6,7},{7,6},{8,9},{9,8},{10,11... | collective-permute-start | bytes 1769480 | tf_op jit(solution)/shard_map/ppermute | solution.py:320
  188.1 10.2 %collective-permute-start.27 = (f32[2,512,640]{2,1,0:T(8,128)}, f32[2,512,640]{2,1,0:T(8,128)}, u32[]{:S(2)}, u32[]{:S(2)}) collective-permute-start(f32[2,512,640]{2,1,0:T(8,128)} %get-tuple-element.103), channel_id=1, source_target_pairs={{0,2},{2,0},{4,6},{6,4},{8,10},{10,8},{12,14},{14,12},{16,18},{18,... | collective-permute-start | bytes 7864328 | tf_op jit(solution)/shard_map/ppermute | solution.py:326
  197.7 4.1 %collective-permute-start.26 = (f32[2,512,384]{2,1,0:T(8,128)}, f32[2,512,384]{2,1,0:T(8,128)}, u32[]{:S(2)}, u32[]{:S(2)}) collective-permute-start(f32[2,512,384]{2,1,0:T(8,128)} %get-tuple-element.102), channel_id=1, source_target_pairs={{0,2},{2,0},{4,6},{6,4},{8,10},{10,8},{12,14},{14,12},{16,18},{18,... | collective-permute-start | bytes 4718600 | tf_op jit(solution)/shard_map/ppermute | solution.py:326

commit v7 on v6

--- a/solution.py
+++ b/solution.py
@@ -358,7 +358,7 @@
     own_c_o = swap(own_c)
     mid0, own_c, own_c_o, ids, put, outer = together((mid0, own_c, own_c_o, ids, put, outer))
 
-    pair1 = pair_z(after(mid0, c_mate))
+    pair1 = pair_z(mid0)
     mid1 = mid_z(c_mate)
     y_mate = along_y(after(c_mate, y_self))
     d_self = along_x(after(y_self, x_self))
@@ -372,7 +372,7 @@
     out, send2 = step(None, left, 0, [((c,), (x_self,)), ((y_self,), (d_self,))], diagonal=0, sends=True)
 
     mid3 = mid_z_all(after(d_mate, out))
-    pair3 = pair_z(after(mid1, d_mate, out))
+    pair3 = pair_z(after(mid1, out))
     d_near = along_y(after(x_near, y_near))
     x_mate = along_x(after(c_mate, x_near))
     out, send3 = step(out, left, 1, [((c_near,), (x_near,)), ((y_mate,), (d_mate,))], sends=True)

time: 205 us -> 205 us (level)
    ppermute x6, waiting for transfers between devices: 24.8 us -> 22.5 us  [rounds(): pair_z = lambda v: lax.ppermute(v, 'loop', [(i, i ^ 4) for i in range(16)])]
  transfers between devices with their start and end apart: 28 -> 28, of which waited for: 13 -> 12; matrix products, arithmetic and copies ran while one was open for 2% -> 2% of each run, Pallas kernels for 41% -> 41%
where the time goes in v7:
time: 205 us
  Pallas kernels  86.8 us (42%)
  waiting for transfers between devices  78.9 us (38%)
  starting transfers between devices  32.6 us (16%)
  local copies, waits for them, and re-layouts  4.27 us (2%)
    pallas_call x5, Pallas kernels, panels(): pl.pallas_call(functools.partial(panel_kernel, sizes, diagonal, part or (...  66.6 us
    ppermute x6, waiting for transfers between devices, rounds(): along_x = lambda v: lax.ppermute(v, 'grp', [(0, 1), (1, 0)])  47.5 us
    ppermute x6, waiting for transfers between devices, rounds(): pair_z = lambda v: lax.ppermute(v, 'loop', [(i, i ^ 4) for i in range(16)])  22.5 us
    ppermute x6, starting transfers between devices, rounds(): pair_z = lambda v: lax.ppermute(v, 'loop', [(i, i ^ 4) for i in range(16)])  12.3 us
    pallas_call x3, Pallas kernels, place(): pl.pallas_call(functools.partial(place_kernel, [part for _, part in recei...  10.8 us
    ppermute x6, starting transfers between devices, rounds(): along_y = lambda v: lax.ppermute(v, 'loop', [(i, i ^ 2) for i in range(16)])  9.12 us
    ppermute x6, waiting for transfers between devices, rounds(): along_y = lambda v: lax.ppermute(v, 'loop', [(i, i ^ 2) for i in range(16)])  8.28 us
    ppermute x6, starting transfers between devices, rounds(): along_x = lambda v: lax.ppermute(v, 'grp', [(0, 1), (1, 0)])  6.26 us
  transfers between devices with their start and end apart: 28, of which 12 were waited for; matrix products, arithmetic and copies ran while one was open for 2% of the time, Pallas kernels for 41%

profile of v7, /device:TPU:0, one launch (start us, length us, event | category | flops | bytes accessed | tf_op | source)
XLA Modules:
  0.0 204.7 jit_solution(6568257723614533779)
XLA Ops:
  0.0 1.9 collective-permute-start
  1.9 2.9 %collective-permute-start.2 = (f32[384,1024]{1,0:T(8,128)}, f32[384,1024]{1,0:T(8,128)S(1)}, u32[]{:S(2)}, u32[]{:S(2)}) collective-permute-start(f32[384,1024]{1,0:T(8,128)} %refs_0_.1), channel_id=1, source_target_pairs={{0,1},{1,0},{2,3},{3,2},{4,5},{5,4},{6,7},{7,6},{8,9},{9,8},{10,11... | collective-permute-start | bytes 4718600 | tf_op jit(solution)/shard_map/ppermute | solution.py:320
  4.8 1.5 collective-permute-start.6
  6.3 3.3 %collective-permute-start.4 = (f32[384,1024]{1,0:T(8,128)}, f32[384,1024]{1,0:T(8,128)}, u32[]{:S(2)}, u32[]{:S(2)}) collective-permute-start(f32[384,1024]{1,0:T(8,128)} %refs_0_.1), channel_id=1, source_target_pairs={{0,8},{2,10},{4,12},{6,14},{8,0},{10,2},{12,4},{14,6},{16,24},{18,... | collective-permute-start | bytes 4718600 | tf_op jit(solution)/shard_map/ppermute | solution.py:322
  9.6 1.2 constant_dynamic-slice_fusion.1.refs_0_
  10.8 0.9 copy-done
  11.7 0.6 stack.101.ids_ref
  12.3 0.6 stack.98.ids_ref
  12.9 0.7 pad_add_fusion.ids_ref
  13.6 0.6 pad_add_fusion.3
  14.2 0.7 pad_add_fusion.1
  14.9 24.5 %collective-permute-done.2.refs_1_ = f32[384,1024]{1,0:T(8,128)S(1)} collective-permute-done((f32[384,1024]{1,0:T(8,128)}, f32[384,1024]{1,0:T(8,128)S(1)}, u32[]{:S(2)}, u32[]{:S(2)}) %collective-permute-start.2) | collective-permute-done | bytes 1572896 | tf_op jit(solution)/shard_map/ppermute | solution.py:320
  39.4 1.6 collective-permute-done.6.refs_2_
  41.3 3.2 %collective-permute-start.10 = (f32[384,1024]{1,0:T(8,128)}, f32[384,1024]{1,0:T(8,128)}, u32[]{:S(2)}, u32[]{:S(2)}) collective-permute-start(f32[384,1024]{1,0:T(8,128)} %collective-permute-done.refs_1_), channel_id=1, source_target_pairs={{0,8},{2,10},{4,12},{6,14},{8,0},{10,2},{12,4},{14,6},{16,24},{18,... | collective-permute-start | bytes 4718600 | tf_op jit(solution)/shard_map/ppermute | solution.py:322
  44.5 1.5 collective-permute-start.12
  46.1 0.9 copy-done.1
  47.0 1.8 collective-permute-start.5
  48.8 0.6 collective-permute-done.3.refs_3_
  49.4 4.4 %left_operand.1.left_hbm = bf16[1024,1536]{1,0:T(8,128)(2,1)} custom-call(f32[384,512]{1,0:T(8,128)} %copy-done, f32[384,512]{1,0:T(8,128)} %copy-done.1, f32[384,512]{1,0:T(8,128)} %copy-done.2, f32[384,512]{1,0:T(8,128)} %collective-permute-done.3.refs_3_), custom_call_target="tpu_custom_call" | custom-call | flops 1024 | bytes 1024 | tf_op jit(solution)/shard_map/left_operand/pallas_call | solution.py:35
  53.7 22.5 %collective-permute-done.7.refs_3_ = f32[384,1024]{1,0:T(8,128)} collective-permute-done((f32[384,1024]{1,0:T(8,128)}, f32[384,1024]{1,0:T(8,128)}, u32[]{:S(2)}, u32[]{:S(2)}) %collective-permute-start.7) | collective-permute-done | bytes 1572896 | tf_op jit(solution)/shard_map/ppermute | solution.py:320
  76.2 1.3 collective-permute-done.10.refs_0_
  77.5 1.7 collective-permute-start.13
  79.2 2.2 %choose.2.refs_0_ = f32[384,1024]{1,0:T(8,128)} custom-call(s32[1]{0:T(128)} %bitcast.11.flag_ref, f32[384,1024]{1,0:T(8,128)} %collective-permute-done.10.refs_0_, f32[384,1024]{1,0:T(8,128)} %collective-permute-done.refs_1_), custom_call_target="tpu_custom_call" | custom-call | bytes 1572864 | tf_op jit(solution)/shard_map/choose/pallas_call | solution.py:250
  81.5 1.5 collective-permute-start.11
  83.0 1.5 collective-permute-start.17
  84.5 14.9 %panels.5 = (f32[512,16384]{1,0:T(8,128)}, f32[2,512,1024]{2,1,0:T(8,128)}) custom-call(s32[3]{0:T(128)} %pad_add_fusion.ids_ref, bf16[1024,1536]{1,0:T(8,128)(2,1)} %left_operand.1.left_hbm, f32[384,1024]{1,0:T(8,128)} %refs_0_.1, f32[384,1024]{1,0:T(8,128)} %copy-done.3, f32[384,1024]{1,0:T(8,128)} %collective-permute-done.6.refs_2_, ...), custom_call_target="tpu_custom_call" | custom-call | flops 96636764160 | bytes 14680064 | tf_op jit(solution)/shard_map/panels/pallas_call | solution.py:182
  99.8 15.3 %collective-permute-done.13.refs_3_ = f32[384,1024]{1,0:T(8,128)} collective-permute-done((f32[384,1024]{1,0:T(8,128)}, f32[384,1024]{1,0:T(8,128)}, u32[]{:S(2)}, u32[]{:S(2)}) %collective-permute-start.13) | collective-permute-done | bytes 1572896 | tf_op jit(solution)/shard_map/ppermute | solution.py:322
  115.1 2.4 %collective-permute-done.17.refs_2_ = f32[384,1024]{1,0:T(8,128)} collective-permute-done((f32[384,1024]{1,0:T(8,128)}, f32[384,1024]{1,0:T(8,128)}, u32[]{:S(2)}, u32[]{:S(2)}) %collective-permute-start.17) | collective-permute-done | bytes 1572896 | tf_op jit(solution)/shard_map/ppermute | solution.py:321
  117.5 1.5 collective-permute-start.18
  119.1 0.6 collective-permute-start.15
  119.7 14.8 %panels.6 = (f32[512,16384]{1,0:T(8,128)}, f32[2,512,1024]{2,1,0:T(8,128)}) custom-call(s32[2]{0:T(128)} %get-tuple-element.65.ids_ref, bf16[1024,1536]{1,0:T(8,128)(2,1)} %left_operand.1.left_hbm, f32[384,1024]{1,0:T(8,128)} %choose.2.refs_0_, f32[384,1024]{1,0:T(8,128)} %collective-permute-done.11.refs_1_, ...), custom_call_target="tpu_custom_call", output_to_operand_aliasing={{0}: (6, {})} | custom-call | flops 96636764160 | bytes 14680064 | tf_op jit(solution)/shard_map/panels/pallas_call | solution.py:182
  134.5 0.6 collective-permute-start.24
  135.1 4.3 %place.3.refs_4_ = f32[512,16384]{1,0:T(8,128)} custom-call(s32[2]{0:T(128)} %get-tuple-element.63.ids_ref, f32[2,512,1024]{2,1,0:T(8,128)} %collective-permute-done.9.refs_0_, f32[512,16384]{1,0:T(8,128)} %get-tuple-element.71.refs_1_), custom_call_target="tpu_custom_call", output_to_operand_aliasing={{}: (2, {})} | custom-call | bytes 8388608 | tf_op jit(solution)/shard_map/place/pallas_call | solution.py:284
  139.4 5.9 %collective-permute-done.8.refs_0_ = f32[384,1024]{1,0:T(8,128)} collective-permute-done((f32[384,1024]{1,0:T(8,128)}, f32[384,1024]{1,0:T(8,128)}, u32[]{:S(2)}, u32[]{:S(2)}) %collective-permute-start.8) | collective-permute-done | bytes 1572896 | tf_op jit(solution)/shard_map/ppermute | solution.py:322
  145.3 2.8 %choose.3 = (f32[384,640]{1,0:T(8,128)}, f32[384,640]{1,0:T(8,128)}, f32[384,384]{1,0:T(8,128)}, f32[384,384]{1,0:T(8,128)}) custom-call(s32[1]{0:T(128)} %bitcast.11.flag_ref, f32[384,1024]{1,0:T(8,128)} %collective-permute-done.8.refs_0_, f32[384,1024]{1,0:T(8,128)} %collective-permute-done.5.refs_1_, f32[384,1024]{1,0:T(8,128)} %collective-permute-done.14.refs_2_), custom_call_target="tpu_custom_call" | custom-call | bytes 1572864 | tf_op jit(solution)/shard_map/choose/pallas_call | solution.py:250
  148.1 4.0 %collective-permute-done.18.refs_3_ = f32[384,1024]{1,0:T(8,128)} collective-permute-done((f32[384,1024]{1,0:T(8,128)}, f32[384,1024]{1,0:T(8,128)}, u32[]{:S(2)}, u32[]{:S(2)}) %collective-permute-start.18) | collective-permute-done | bytes 1572896 | tf_op jit(solution)/shard_map/ppermute | solution.py:321
  152.1 1.5 collective-permute-start.19
  153.6 2.2 %collective-permute-start.20 = (f32[384,640]{1,0:T(8,128)}, f32[384,640]{1,0:T(8,128)}, u32[]{:S(2)}, u32[]{:S(2)}) collective-permute-start(f32[384,640]{1,0:T(8,128)} %get-tuple-element.81.refs_4_), channel_id=1, source_target_pairs={{0,8},{2,10},{4,12},{6,14},{8,0},{10,2},{12,4},{14,6},{16,24},{18,... | collective-permute-start | bytes 2949128 | tf_op jit(solution)/shard_map/ppermute | solution.py:322
  155.8 14.8 %panels.7 = (f32[512,16384]{1,0:T(8,128)}, f32[2,512,1024]{2,1,0:T(8,128)}) custom-call(s32[2]{0:T(128)} %get-tuple-element.82.ids_ref, bf16[1024,1536]{1,0:T(8,128)(2,1)} %left_operand.1.left_hbm, f32[384,1024]{1,0:T(8,128)} %collective-permute-done.4.refs_0_, f32[384,1024]{1,0:T(8,128)} %collective-permute-done.15.refs_1_, ...), custom_call_target="tpu_custom_call", output_to_operand_aliasing={{0}: (6, {})} | custom-call | flops 96636764160 | bytes 14680064 | tf_op jit(solution)/shard_map/panels/pallas_call | solution.py:182
  171.0 1.6 collective-permute-start.23
  172.6 1.5 collective-permute-start.22
  174.1 0.9 collective-permute-start.21
  175.0 12.5 %panels.8 = (f32[512,16384]{1,0:T(8,128)}, f32[2,512,640]{2,1,0:T(8,128)}) custom-call(s32[5]{0:T(128)} %stack.98.ids_ref, bf16[1024,1536]{1,0:T(8,128)(2,1)} %left_operand.1.left_hbm, f32[384,640]{1,0:T(8,128)} %get-tuple-element.80.refs_0_, f32[384,640]{1,0:T(8,128)} %collective-permute-done.16.refs_1_, ...), custom_call_target="tpu_custom_call", output_to_operand_aliasing={{0}: (8, {})} | custom-call | flops 60397977600 | bytes 9175040 | tf_op jit(solution)/shard_map/panels/pallas_call | solution.py:182
  187.6 0.5 collective-permute-done.21.refs_1_
  188.1 9.6 %panels.9 = (f32[512,16384]{1,0:T(8,128)}, f32[2,512,384]{2,1,0:T(8,128)}) custom-call(s32[5]{0:T(128)} %stack.101.ids_ref, bf16[1024,1536]{1,0:T(8,128)(2,1)} %left_operand.1.left_hbm, f32[384,384]{1,0:T(8,128)} %get-tuple-element.87.refs_0_, f32[384,384]{1,0:T(8,128)} %collective-permute-done.21.refs_1_, ...), custom_call_target="tpu_custom_call", output_to_operand_aliasing={{0}: (8, {})} | custom-call | flops 36238786560 | bytes 5505024 | tf_op jit(solution)/shard_map/panels/pallas_call | solution.py:182
  197.7 0.6 collective-permute-start.26
  198.3 3.5 %place.4.refs_1_ = f32[512,16384]{1,0:T(8,128)} custom-call(s32[2]{0:T(128)} %get-tuple-element.54.ids_ref, f32[2,512,640]{2,1,0:T(8,128)} %collective-permute-done.27.refs_0_, f32[512,16384]{1,0:T(8,128)} %get-tuple-element.102.refs_1_), custom_call_target="tpu_custom_call", output_to_operand_aliasing={{}: (2, {})} | custom-call | bytes 5242880 | tf_op jit(solution)/shard_map/place/pallas_call | solution.py:284
  201.8 3.0 %place.5 = f32[512,16384]{1,0:T(8,128)} custom-call(s32[2]{0:T(128)} %get-tuple-element.54.ids_ref, f32[2,512,384]{2,1,0:T(8,128)} %collective-permute-done.26.refs_0_, f32[512,16384]{1,0:T(8,128)} %place.4.refs_1_), custom_call_target="tpu_custom_call", output_to_operand_aliasing={{}: (2, {})} | custom-call | bytes 3145728 | tf_op jit(solution)/shard_map/place/pallas_call | solution.py:284
  (34 shorter events, 1.4 us)
Async XLA Ops:
  0.0 14.9 %collective-permute-start = (f32[384,1024]{1,0:T(8,128)}, f32[384,1024]{1,0:T(8,128)}, u32[]{:S(2)}, u32[]{:S(2)}) collective-permute-start(f32[384,1024]{1,0:T(8,128)} %refs_0_.1), channel_id=1, source_target_pairs={{8,16},{10,18},{12,20},{14,22},{16,8},{18,10},{20,12},{22,14},{9,1... | collective-permute-start | bytes 4718600 | tf_op jit(solution)/shard_map/ppermute | solution.py:324
  1.9 37.5 %collective-permute-start.2 = (f32[384,1024]{1,0:T(8,128)}, f32[384,1024]{1,0:T(8,128)S(1)}, u32[]{:S(2)}, u32[]{:S(2)}) collective-permute-start(f32[384,1024]{1,0:T(8,128)} %refs_0_.1), channel_id=1, source_target_pairs={{0,1},{1,0},{2,3},{3,2},{4,5},{5,4},{6,7},{7,6},{8,9},{9,8},{10,11... | collective-permute-start | bytes 4718600 | tf_op jit(solution)/shard_map/ppermute | solution.py:320
  4.8 36.2 %collective-permute-start.6 = (f32[384,1024]{1,0:T(8,128)}, f32[384,1024]{1,0:T(8,128)}, u32[]{:S(2)}, u32[]{:S(2)}) collective-permute-start(f32[384,1024]{1,0:T(8,128)} %refs_0_.1), channel_id=1, source_target_pairs={{0,4},{2,6},{4,0},{6,2},{8,12},{10,14},{12,8},{14,10},{16,20},{18,... | collective-permute-start | bytes 4718600 | tf_op jit(solution)/shard_map/ppermute | solution.py:321
  6.3 38.2 %collective-permute-start.4 = (f32[384,1024]{1,0:T(8,128)}, f32[384,1024]{1,0:T(8,128)}, u32[]{:S(2)}, u32[]{:S(2)}) collective-permute-start(f32[384,1024]{1,0:T(8,128)} %refs_0_.1), channel_id=1, source_target_pairs={{0,8},{2,10},{4,12},{6,14},{8,0},{10,2},{12,4},{14,6},{16,24},{18,... | collective-permute-start | bytes 4718600 | tf_op jit(solution)/shard_map/ppermute | solution.py:322
  10.8 0.9 copy-start
  11.7 3.2 %collective-permute-start.1 = (f32[384,512]{1,0:T(8,128)S(1)}, f32[384,512]{1,0:T(8,128)S(1)}, u32[]{:S(2)}, u32[]{:S(2)}) collective-permute-start(f32[384,512]{1,0:T(8,128)S(1)} %constant_dynamic-slice_fusion.1.refs_0_), channel_id=1, source_target_pairs={{0,2},{2,0},{4,6},{6,4},{8,10},{10,8},{12,14},{14,12},{16,18},{18,... | collective-permute-start | bytes 2359304 | tf_op jit(solution)/shard_map/ppermute | solution.py:326
  14.9 32.1 %copy-start.2 = (f32[384,512]{1,0:T(8,128)}, f32[384,512]{1,0:T(8,128)S(1)}, u32[]{:S(2)}) copy-start(f32[384,512]{1,0:T(8,128)S(1)} %collective-permute-done.1.refs_2_) | copy-start | bytes 2359300
  39.4 9.4 %copy-start.3 = (f32[384,1024]{1,0:T(8,128)}, f32[384,1024]{1,0:T(8,128)S(1)}, u32[]{:S(2)}) copy-start(f32[384,1024]{1,0:T(8,128)S(1)} %collective-permute-done.2.refs_1_) | copy-start | bytes 4718596
  41.0 35.3 %collective-permute-start.7 = (f32[384,1024]{1,0:T(8,128)}, f32[384,1024]{1,0:T(8,128)}, u32[]{:S(2)}, u32[]{:S(2)}) collective-permute-start(f32[384,1024]{1,0:T(8,128)} %collective-permute-done.6.refs_2_), channel_id=1, source_target_pairs={{0,1},{1,0},{2,3},{3,2},{4,5},{5,4},{6,7},{7,6},{8,9},{9,8},{10,11... | collective-permute-start | bytes 4718600 | tf_op jit(solution)/shard_map/ppermute | solution.py:320
  41.3 36.2 %collective-permute-start.10 = (f32[384,1024]{1,0:T(8,128)}, f32[384,1024]{1,0:T(8,128)}, u32[]{:S(2)}, u32[]{:S(2)}) collective-permute-start(f32[384,1024]{1,0:T(8,128)} %collective-permute-done.refs_1_), channel_id=1, source_target_pairs={{0,8},{2,10},{4,12},{6,14},{8,0},{10,2},{12,4},{14,6},{16,24},{18,... | collective-permute-start | bytes 4718600 | tf_op jit(solution)/shard_map/ppermute | solution.py:322
  44.5 38.5 %collective-permute-start.12 = (f32[384,1024]{1,0:T(8,128)}, f32[384,1024]{1,0:T(8,128)}, u32[]{:S(2)}, u32[]{:S(2)}) collective-permute-start(f32[384,1024]{1,0:T(8,128)} %collective-permute-done.4.refs_0_), channel_id=1, source_target_pairs={{0,4},{2,6},{4,0},{6,2},{8,12},{10,14},{12,8},{14,10},{16,20},{18,... | collective-permute-start | bytes 4718600 | tf_op jit(solution)/shard_map/ppermute | solution.py:321
  46.1 0.9 copy-start.1
  47.0 2.4 %collective-permute-start.3 = (f32[384,512]{1,0:T(8,128)S(1)}, f32[384,512]{1,0:T(8,128)}, u32[]{:S(2)}, u32[]{:S(2)}) collective-permute-start(f32[384,512]{1,0:T(8,128)S(1)} %constant_dynamic-slice_fusion.refs_1_), channel_id=1, source_target_pairs={{0,2},{2,0},{4,6},{6,4},{8,10},{10,8},{12,14},{14,12},{16,18},{18,... | collective-permute-start | bytes 2359304 | tf_op jit(solution)/shard_map/ppermute | solution.py:326
  47.0 52.4 %collective-permute-start.5 = (f32[384,1024]{1,0:T(8,128)}, f32[384,1024]{1,0:T(8,128)}, u32[]{:S(2)}, u32[]{:S(2)}) collective-permute-start(f32[384,1024]{1,0:T(8,128)} %collective-permute-done.4.refs_0_), channel_id=1, source_target_pairs={{8,16},{10,18},{12,20},{14,22},{16,8},{18,10},{20,12},{22,14},{9,1... | collective-permute-start | bytes 4718600 | tf_op jit(solution)/shard_map/ppermute | solution.py:324
  77.5 37.6 %collective-permute-start.13 = (f32[384,1024]{1,0:T(8,128)}, f32[384,1024]{1,0:T(8,128)}, u32[]{:S(2)}, u32[]{:S(2)}) collective-permute-start(f32[384,1024]{1,0:T(8,128)} %collective-permute-done.7.refs_3_), channel_id=1, source_target_pairs={{0,8},{2,10},{4,12},{6,14},{8,0},{10,2},{12,4},{14,6},{16,24},{18,... | collective-permute-start | bytes 4718600 | tf_op jit(solution)/shard_map/ppermute | solution.py:322
  81.5 33.7 %collective-permute-start.11 = (f32[384,1024]{1,0:T(8,128)}, f32[384,1024]{1,0:T(8,128)}, u32[]{:S(2)}, u32[]{:S(2)}) collective-permute-start(f32[384,1024]{1,0:T(8,128)} %choose.2.refs_0_), channel_id=1, source_target_pairs={{0,1},{1,0},{2,3},{3,2},{4,5},{5,4},{6,7},{7,6},{8,9},{9,8},{10,11... | collective-permute-start | bytes 4718600 | tf_op jit(solution)/shard_map/ppermute | solution.py:320
  83.0 34.6 %collective-permute-start.17 = (f32[384,1024]{1,0:T(8,128)}, f32[384,1024]{1,0:T(8,128)}, u32[]{:S(2)}, u32[]{:S(2)}) collective-permute-start(f32[384,1024]{1,0:T(8,128)} %choose.2.refs_0_), channel_id=1, source_target_pairs={{0,4},{2,6},{4,0},{6,2},{8,12},{10,14},{12,8},{14,10},{16,20},{18,... | collective-permute-start | bytes 4718600 | tf_op jit(solution)/shard_map/ppermute | solution.py:321
  99.4 35.1 %collective-permute-start.9 = (f32[2,512,1024]{2,1,0:T(8,128)}, f32[2,512,1024]{2,1,0:T(8,128)}, u32[]{:S(2)}, u32[]{:S(2)}) collective-permute-start(f32[2,512,1024]{2,1,0:T(8,128)} %get-tuple-element.64), channel_id=1, source_target_pairs={{0,2},{2,0},{4,6},{6,4},{8,10},{10,8},{12,14},{14,12},{16,18},{18,... | collective-permute-start | bytes 12582920 | tf_op jit(solution)/shard_map/ppermute | solution.py:326
  99.5 45.8 %collective-permute-start.8 = (f32[384,1024]{1,0:T(8,128)}, f32[384,1024]{1,0:T(8,128)}, u32[]{:S(2)}, u32[]{:S(2)}) collective-permute-start(f32[384,1024]{1,0:T(8,128)} %collective-permute-done.5.refs_1_), channel_id=1, source_target_pairs={{0,8},{2,10},{4,12},{6,14},{8,0},{10,2},{12,4},{14,6},{16,24},{18,... | collective-permute-start | bytes 4718600 | tf_op jit(solution)/shard_map/ppermute | solution.py:322
  117.5 34.5 %collective-permute-start.18 = (f32[384,1024]{1,0:T(8,128)}, f32[384,1024]{1,0:T(8,128)}, u32[]{:S(2)}, u32[]{:S(2)}) collective-permute-start(f32[384,1024]{1,0:T(8,128)} %collective-permute-done.11.refs_1_), channel_id=1, source_target_pairs={{0,4},{2,6},{4,0},{6,2},{8,12},{10,14},{12,8},{14,10},{16,20},{18,... | collective-permute-start | bytes 4718600 | tf_op jit(solution)/shard_map/ppermute | solution.py:321
  119.1 34.5 %collective-permute-start.15 = (f32[384,1024]{1,0:T(8,128)}, f32[384,1024]{1,0:T(8,128)}, u32[]{:S(2)}, u32[]{:S(2)}) collective-permute-start(f32[384,1024]{1,0:T(8,128)} %collective-permute-done.4.refs_0_), channel_id=1, source_target_pairs={{0,1},{1,0},{2,3},{3,2},{4,5},{5,4},{6,7},{7,6},{8,9},{9,8},{10,11... | collective-permute-start | bytes 4718600 | tf_op jit(solution)/shard_map/ppermute | solution.py:320
  119.7 25.6 %collective-permute-start.14 = (f32[384,1024]{1,0:T(8,128)}, f32[384,1024]{1,0:T(8,128)}, u32[]{:S(2)}, u32[]{:S(2)}) collective-permute-start(f32[384,1024]{1,0:T(8,128)} %collective-permute-done.13.refs_3_), channel_id=1, source_target_pairs={{8,16},{10,18},{12,20},{14,22},{16,8},{18,10},{20,12},{22,14},{0,2... | collective-permute-start | bytes 4718600 | tf_op jit(solution)/shard_map/ppermute | solution.py:325
  134.5 40.5 %collective-permute-start.24 = (f32[2,512,1024]{2,1,0:T(8,128)}, f32[2,512,1024]{2,1,0:T(8,128)}, u32[]{:S(2)}, u32[]{:S(2)}) collective-permute-start(f32[2,512,1024]{2,1,0:T(8,128)} %get-tuple-element.92), channel_id=1, source_target_pairs={{0,2},{2,0},{4,6},{6,4},{8,10},{10,8},{12,14},{14,12},{16,18},{18,... | collective-permute-start | bytes 12582920 | tf_op jit(solution)/shard_map/ppermute | solution.py:326
  152.1 18.9 %collective-permute-start.19 = (f32[384,640]{1,0:T(8,128)}, f32[384,640]{1,0:T(8,128)}, u32[]{:S(2)}, u32[]{:S(2)}) collective-permute-start(f32[384,640]{1,0:T(8,128)} %get-tuple-element.80.refs_0_), channel_id=1, source_target_pairs={{0,4},{2,6},{4,0},{6,2},{8,12},{10,14},{12,8},{14,10},{16,20},{18,... | collective-permute-start | bytes 2949128 | tf_op jit(solution)/shard_map/ppermute | solution.py:321
  153.6 17.4 %collective-permute-start.16 = (f32[384,640]{1,0:T(8,128)}, f32[384,640]{1,0:T(8,128)}, u32[]{:S(2)}, u32[]{:S(2)}) collective-permute-start(f32[384,640]{1,0:T(8,128)} %get-tuple-element.80.refs_0_), channel_id=1, source_target_pairs={{0,1},{1,0},{2,3},{3,2},{4,5},{5,4},{6,7},{7,6},{8,9},{9,8},{10,11... | collective-permute-start | bytes 2949128 | tf_op jit(solution)/shard_map/ppermute | solution.py:320
  153.6 17.4 %collective-permute-start.20 = (f32[384,640]{1,0:T(8,128)}, f32[384,640]{1,0:T(8,128)}, u32[]{:S(2)}, u32[]{:S(2)}) collective-permute-start(f32[384,640]{1,0:T(8,128)} %get-tuple-element.81.refs_4_), channel_id=1, source_target_pairs={{0,8},{2,10},{4,12},{6,14},{8,0},{10,2},{12,4},{14,6},{16,24},{18,... | collective-permute-start | bytes 2949128 | tf_op jit(solution)/shard_map/ppermute | solution.py:322
  170.6 17.5 %collective-permute-start.25 = (f32[2,512,1024]{2,1,0:T(8,128)}, f32[2,512,1024]{2,1,0:T(8,128)}, u32[]{:S(2)}, u32[]{:S(2)}) collective-permute-start(f32[2,512,1024]{2,1,0:T(8,128)} %get-tuple-element.98), channel_id=1, source_target_pairs={{0,2},{2,0},{4,6},{6,4},{8,10},{10,8},{12,14},{14,12},{16,18},{18,... | collective-permute-start | bytes 12582920 | tf_op jit(solution)/shard_map/ppermute | solution.py:326
  171.0 16.5 %collective-permute-start.23 = (f32[384,384]{1,0:T(8,128)}, f32[384,384]{1,0:T(8,128)}, u32[]{:S(2)}, u32[]{:S(2)}) collective-permute-start(f32[384,384]{1,0:T(8,128)} %get-tuple-element.90.refs_4_), channel_id=1, source_target_pairs={{0,8},{2,10},{4,12},{6,14},{8,0},{10,2},{12,4},{14,6},{16,24},{18,... | collective-permute-start | bytes 1769480 | tf_op jit(solution)/shard_map/ppermute | solution.py:322
  172.6 15.0 %collective-permute-start.22 = (f32[384,384]{1,0:T(8,128)}, f32[384,384]{1,0:T(8,128)}, u32[]{:S(2)}, u32[]{:S(2)}) collective-permute-start(f32[384,384]{1,0:T(8,128)} %get-tuple-element.87.refs_0_), channel_id=1, source_target_pairs={{0,4},{2,6},{4,0},{6,2},{8,12},{10,14},{12,8},{14,10},{16,20},{18,... | collective-permute-start | bytes 1769480 | tf_op jit(solution)/shard_map/ppermute | solution.py:321
  174.1 13.9 %collective-permute-start.21 = (f32[384,384]{1,0:T(8,128)}, f32[384,384]{1,0:T(8,128)}, u32[]{:S(2)}, u32[]{:S(2)}) collective-permute-start(f32[384,384]{1,0:T(8,128)} %get-tuple-element.87.refs_0_), channel_id=1, source_target_pairs={{0,1},{1,0},{2,3},{3,2},{4,5},{5,4},{6,7},{7,6},{8,9},{9,8},{10,11... | collective-permute-start | bytes 1769480 | tf_op jit(solution)/shard_map/ppermute | solution.py:320
  188.1 10.2 %collective-permute-start.27 = (f32[2,512,640]{2,1,0:T(8,128)}, f32[2,512,640]{2,1,0:T(8,128)}, u32[]{:S(2)}, u32[]{:S(2)}) collective-permute-start(f32[2,512,640]{2,1,0:T(8,128)} %get-tuple-element.101), channel_id=1, source_target_pairs={{0,2},{2,0},{4,6},{6,4},{8,10},{10,8},{12,14},{14,12},{16,18},{18,... | collective-permute-start | bytes 7864328 | tf_op jit(solution)/shard_map/ppermute | solution.py:326
  197.7 4.1 %collective-permute-start.26 = (f32[2,512,384]{2,1,0:T(8,128)}, f32[2,512,384]{2,1,0:T(8,128)}, u32[]{:S(2)}, u32[]{:S(2)}) collective-permute-start(f32[2,512,384]{2,1,0:T(8,128)} %get-tuple-element.100), channel_id=1, source_target_pairs={{0,2},{2,0},{4,6},{6,4},{8,10},{10,8},{12,14},{14,12},{16,18},{18,... | collective-permute-start | bytes 4718600 | tf_op jit(solution)/shard_map/ppermute | solution.py:326

commit v8 on v7

--- a/solution.py
+++ b/solution.py
@@ -131,14 +131,16 @@
         halves = [split_high_low(value) for value in block[:2]]
         high, low = (jnp.concatenate(pieces, axis=0) for pieces in zip(*halves))
         dot = functools.partial(jnp.dot, preferred_element_type=jnp.float32)
-        product = dot(left[0][...], high) + dot(left[0][...], low)
         if tile == 512:
+            product = dot(left[0][...], high) + dot(left[0][...], low)
 
             @pl.when(turn == 0)
             def rest_of_left():
                 left_copies[1].wait()
 
-        product += dot(left[1][...], high)
+            product += dot(left[1][...], high)
+        else:
+            product = dot(left[0][...], high) + dot(left_ref[...], jnp.concatenate([low, high], axis=0))
         if diagonal is not None:
             row_ids = lax.broadcasted_iota(jnp.int32, product.shape, 0) + ids_ref[ids_ref.shape[0] - 1]
             col_ids = lax.broadcasted_iota(jnp.int32, product.shape, 1) + column

time: 205 us -> 205 us (level)
  no operation moved by 1% of the time
where the time goes in v8:
time: 205 us
  Pallas kernels  86.8 us (42%)
  waiting for transfers between devices  79 us (39%)
  starting transfers between devices  32.6 us (16%)
  local copies, waits for them, and re-layouts  4.27 us (2%)
    pallas_call x5, Pallas kernels, panels(): pl.pallas_call(functools.partial(panel_kernel, sizes, diagonal, part or (...  66.6 us
    ppermute x6, waiting for transfers between devices, rounds(): along_x = lambda v: lax.ppermute(v, 'grp', [(0, 1), (1, 0)])  47.5 us
    ppermute x6, waiting for transfers between devices, rounds(): pair_z = lambda v: lax.ppermute(v, 'loop', [(i, i ^ 4) for i in range(16)])  22.5 us
    ppermute x6, starting transfers between devices, rounds(): pair_z = lambda v: lax.ppermute(v, 'loop', [(i, i ^ 4) for i in range(16)])  12.3 us
    pallas_call x3, Pallas kernels, place(): pl.pallas_call(functools.partial(place_kernel, [part for _, part in recei...  10.8 us
    ppermute x6, starting transfers between devices, rounds(): along_y = lambda v: lax.ppermute(v, 'loop', [(i, i ^ 2) for i in range(16)])  9.12 us
    ppermute x6, waiting for transfers between devices, rounds(): along_y = lambda v: lax.ppermute(v, 'loop', [(i, i ^ 2) for i in range(16)])  8.28 us
    ppermute x6, starting transfers between devices, rounds(): along_x = lambda v: lax.ppermute(v, 'grp', [(0, 1), (1, 0)])  6.26 us
  transfers between devices with their start and end apart: 28, of which 12 were waited for; matrix products, arithmetic and copies ran while one was open for 2% of the time, Pallas kernels for 41%

profile of v8, /device:TPU:0, one launch (start us, length us, event | category | flops | bytes accessed | tf_op | source)
XLA Modules:
  0.0 204.7 jit_solution(10784739084382173871)
XLA Ops:
  0.0 1.9 collective-permute-start
  1.9 2.9 %collective-permute-start.2 = (f32[384,1024]{1,0:T(8,128)}, f32[384,1024]{1,0:T(8,128)S(1)}, u32[]{:S(2)}, u32[]{:S(2)}) collective-permute-start(f32[384,1024]{1,0:T(8,128)} %refs_0_.1), channel_id=1, source_target_pairs={{0,1},{1,0},{2,3},{3,2},{4,5},{5,4},{6,7},{7,6},{8,9},{9,8},{10,11... | collective-permute-start | bytes 4718600 | tf_op jit(solution)/shard_map/ppermute | solution.py:322
  4.8 1.5 collective-permute-start.6
  6.3 3.3 %collective-permute-start.4 = (f32[384,1024]{1,0:T(8,128)}, f32[384,1024]{1,0:T(8,128)}, u32[]{:S(2)}, u32[]{:S(2)}) collective-permute-start(f32[384,1024]{1,0:T(8,128)} %refs_0_.1), channel_id=1, source_target_pairs={{0,8},{2,10},{4,12},{6,14},{8,0},{10,2},{12,4},{14,6},{16,24},{18,... | collective-permute-start | bytes 4718600 | tf_op jit(solution)/shard_map/ppermute | solution.py:324
  9.6 1.2 constant_dynamic-slice_fusion.1.refs_0_
  10.8 0.9 copy-done
  11.7 0.6 stack.101.ids_ref
  12.3 0.6 stack.98.ids_ref
  12.9 0.7 pad_add_fusion.ids_ref
  13.6 0.6 pad_add_fusion.3
  14.2 0.7 pad_add_fusion.1
  14.9 24.5 %collective-permute-done.2.refs_1_ = f32[384,1024]{1,0:T(8,128)S(1)} collective-permute-done((f32[384,1024]{1,0:T(8,128)}, f32[384,1024]{1,0:T(8,128)S(1)}, u32[]{:S(2)}, u32[]{:S(2)}) %collective-permute-start.2) | collective-permute-done | bytes 1572896 | tf_op jit(solution)/shard_map/ppermute | solution.py:322
  39.4 1.6 collective-permute-done.6.refs_2_
  41.3 3.2 %collective-permute-start.10 = (f32[384,1024]{1,0:T(8,128)}, f32[384,1024]{1,0:T(8,128)}, u32[]{:S(2)}, u32[]{:S(2)}) collective-permute-start(f32[384,1024]{1,0:T(8,128)} %collective-permute-done.refs_1_), channel_id=1, source_target_pairs={{0,8},{2,10},{4,12},{6,14},{8,0},{10,2},{12,4},{14,6},{16,24},{18,... | collective-permute-start | bytes 4718600 | tf_op jit(solution)/shard_map/ppermute | solution.py:324
  44.5 1.5 collective-permute-start.12
  46.1 0.9 copy-done.1
  47.0 1.8 collective-permute-start.5
  48.8 0.6 collective-permute-done.3.refs_3_
  49.4 4.4 %left_operand.1.left_hbm = bf16[1024,1536]{1,0:T(8,128)(2,1)} custom-call(f32[384,512]{1,0:T(8,128)} %copy-done, f32[384,512]{1,0:T(8,128)} %copy-done.1, f32[384,512]{1,0:T(8,128)} %copy-done.2, f32[384,512]{1,0:T(8,128)} %collective-permute-done.3.refs_3_), custom_call_target="tpu_custom_call" | custom-call | flops 1024 | bytes 1024 | tf_op jit(solution)/shard_map/left_operand/pallas_call | solution.py:35
  53.7 22.5 %collective-permute-done.7.refs_3_ = f32[384,1024]{1,0:T(8,128)} collective-permute-done((f32[384,1024]{1,0:T(8,128)}, f32[384,1024]{1,0:T(8,128)}, u32[]{:S(2)}, u32[]{:S(2)}) %collective-permute-start.7) | collective-permute-done | bytes 1572896 | tf_op jit(solution)/shard_map/ppermute | solution.py:322
  76.2 1.3 collective-permute-done.10.refs_0_
  77.5 1.7 collective-permute-start.13
  79.2 2.2 %choose.2.refs_0_ = f32[384,1024]{1,0:T(8,128)} custom-call(s32[1]{0:T(128)} %bitcast.11.flag_ref, f32[384,1024]{1,0:T(8,128)} %collective-permute-done.10.refs_0_, f32[384,1024]{1,0:T(8,128)} %collective-permute-done.refs_1_), custom_call_target="tpu_custom_call" | custom-call | bytes 1572864 | tf_op jit(solution)/shard_map/choose/pallas_call | solution.py:252
  81.5 1.5 collective-permute-start.11
  83.0 1.5 collective-permute-start.17
  84.5 14.9 %panels.5 = (f32[512,16384]{1,0:T(8,128)}, f32[2,512,1024]{2,1,0:T(8,128)}) custom-call(s32[3]{0:T(128)} %pad_add_fusion.ids_ref, bf16[1024,1536]{1,0:T(8,128)(2,1)} %left_operand.1.left_hbm, f32[384,1024]{1,0:T(8,128)} %refs_0_.1, f32[384,1024]{1,0:T(8,128)} %copy-done.3, f32[384,1024]{1,0:T(8,128)} %collective-permute-done.6.refs_2_, ...), custom_call_target="tpu_custom_call" | custom-call | flops 96636764160 | bytes 14680064 | tf_op jit(solution)/shard_map/panels/pallas_call | solution.py:184
  99.8 15.3 %collective-permute-done.13.refs_3_ = f32[384,1024]{1,0:T(8,128)} collective-permute-done((f32[384,1024]{1,0:T(8,128)}, f32[384,1024]{1,0:T(8,128)}, u32[]{:S(2)}, u32[]{:S(2)}) %collective-permute-start.13) | collective-permute-done | bytes 1572896 | tf_op jit(solution)/shard_map/ppermute | solution.py:324
  115.1 2.4 %collective-permute-done.17.refs_2_ = f32[384,1024]{1,0:T(8,128)} collective-permute-done((f32[384,1024]{1,0:T(8,128)}, f32[384,1024]{1,0:T(8,128)}, u32[]{:S(2)}, u32[]{:S(2)}) %collective-permute-start.17) | collective-permute-done | bytes 1572896 | tf_op jit(solution)/shard_map/ppermute | solution.py:323
  117.5 1.5 collective-permute-start.18
  119.1 0.6 collective-permute-start.15
  119.7 14.8 %panels.6 = (f32[512,16384]{1,0:T(8,128)}, f32[2,512,1024]{2,1,0:T(8,128)}) custom-call(s32[2]{0:T(128)} %get-tuple-element.65.ids_ref, bf16[1024,1536]{1,0:T(8,128)(2,1)} %left_operand.1.left_hbm, f32[384,1024]{1,0:T(8,128)} %choose.2.refs_0_, f32[384,1024]{1,0:T(8,128)} %collective-permute-done.11.refs_1_, ...), custom_call_target="tpu_custom_call", output_to_operand_aliasing={{0}: (6, {})} | custom-call | flops 96636764160 | bytes 14680064 | tf_op jit(solution)/shard_map/panels/pallas_call | solution.py:184
  134.5 0.6 collective-permute-start.24
  135.1 4.3 %place.3.refs_4_ = f32[512,16384]{1,0:T(8,128)} custom-call(s32[2]{0:T(128)} %get-tuple-element.63.ids_ref, f32[2,512,1024]{2,1,0:T(8,128)} %collective-permute-done.9.refs_0_, f32[512,16384]{1,0:T(8,128)} %get-tuple-element.71.refs_1_), custom_call_target="tpu_custom_call", output_to_operand_aliasing={{}: (2, {})} | custom-call | bytes 8388608 | tf_op jit(solution)/shard_map/place/pallas_call | solution.py:286
  139.4 5.9 %collective-permute-done.8.refs_0_ = f32[384,1024]{1,0:T(8,128)} collective-permute-done((f32[384,1024]{1,0:T(8,128)}, f32[384,1024]{1,0:T(8,128)}, u32[]{:S(2)}, u32[]{:S(2)}) %collective-permute-start.8) | collective-permute-done | bytes 1572896 | tf_op jit(solution)/shard_map/ppermute | solution.py:324
  145.3 2.8 %choose.3 = (f32[384,640]{1,0:T(8,128)}, f32[384,640]{1,0:T(8,128)}, f32[384,384]{1,0:T(8,128)}, f32[384,384]{1,0:T(8,128)}) custom-call(s32[1]{0:T(128)} %bitcast.11.flag_ref, f32[384,1024]{1,0:T(8,128)} %collective-permute-done.8.refs_0_, f32[384,1024]{1,0:T(8,128)} %collective-permute-done.5.refs_1_, f32[384,1024]{1,0:T(8,128)} %collective-permute-done.14.refs_2_), custom_call_target="tpu_custom_call" | custom-call | bytes 1572864 | tf_op jit(solution)/shard_map/choose/pallas_call | solution.py:252
  148.1 4.0 %collective-permute-done.18.refs_3_ = f32[384,1024]{1,0:T(8,128)} collective-permute-done((f32[384,1024]{1,0:T(8,128)}, f32[384,1024]{1,0:T(8,128)}, u32[]{:S(2)}, u32[]{:S(2)}) %collective-permute-start.18) | collective-permute-done | bytes 1572896 | tf_op jit(solution)/shard_map/ppermute | solution.py:323
  152.1 1.5 collective-permute-start.19
  153.6 2.2 %collective-permute-start.20 = (f32[384,640]{1,0:T(8,128)}, f32[384,640]{1,0:T(8,128)}, u32[]{:S(2)}, u32[]{:S(2)}) collective-permute-start(f32[384,640]{1,0:T(8,128)} %get-tuple-element.81.refs_4_), channel_id=1, source_target_pairs={{0,8},{2,10},{4,12},{6,14},{8,0},{10,2},{12,4},{14,6},{16,24},{18,... | collective-permute-start | bytes 2949128 | tf_op jit(solution)/shard_map/ppermute | solution.py:324
  155.8 14.8 %panels.7 = (f32[512,16384]{1,0:T(8,128)}, f32[2,512,1024]{2,1,0:T(8,128)}) custom-call(s32[2]{0:T(128)} %get-tuple-element.82.ids_ref, bf16[1024,1536]{1,0:T(8,128)(2,1)} %left_operand.1.left_hbm, f32[384,1024]{1,0:T(8,128)} %collective-permute-done.4.refs_0_, f32[384,1024]{1,0:T(8,128)} %collective-permute-done.15.refs_1_, ...), custom_call_target="tpu_custom_call", output_to_operand_aliasing={{0}: (6, {})} | custom-call | flops 96636764160 | bytes 14680064 | tf_op jit(solution)/shard_map/panels/pallas_call | solution.py:184
  171.0 1.6 collective-permute-start.23
  172.6 1.5 collective-permute-start.22
  174.1 0.9 collective-permute-start.21
  175.0 12.5 %panels.8 = (f32[512,16384]{1,0:T(8,128)}, f32[2,512,640]{2,1,0:T(8,128)}) custom-call(s32[5]{0:T(128)} %stack.98.ids_ref, bf16[1024,1536]{1,0:T(8,128)(2,1)} %left_operand.1.left_hbm, f32[384,640]{1,0:T(8,128)} %get-tuple-element.80.refs_0_, f32[384,640]{1,0:T(8,128)} %collective-permute-done.16.refs_1_, ...), custom_call_target="tpu_custom_call", output_to_operand_aliasing={{0}: (8, {})} | custom-call | flops 60397977600 | bytes 9175040 | tf_op jit(solution)/shard_map/panels/pallas_call | solution.py:184
  187.6 0.5 collective-permute-done.21.refs_1_
  188.1 9.6 %panels.9 = (f32[512,16384]{1,0:T(8,128)}, f32[2,512,384]{2,1,0:T(8,128)}) custom-call(s32[5]{0:T(128)} %stack.101.ids_ref, bf16[1024,1536]{1,0:T(8,128)(2,1)} %left_operand.1.left_hbm, f32[384,384]{1,0:T(8,128)} %get-tuple-element.87.refs_0_, f32[384,384]{1,0:T(8,128)} %collective-permute-done.21.refs_1_, ...), custom_call_target="tpu_custom_call", output_to_operand_aliasing={{0}: (8, {})} | custom-call | flops 36238786560 | bytes 5505024 | tf_op jit(solution)/shard_map/panels/pallas_call | solution.py:184
  197.7 0.6 collective-permute-start.26
  198.3 3.5 %place.4.refs_1_ = f32[512,16384]{1,0:T(8,128)} custom-call(s32[2]{0:T(128)} %get-tuple-element.54.ids_ref, f32[2,512,640]{2,1,0:T(8,128)} %collective-permute-done.27.refs_0_, f32[512,16384]{1,0:T(8,128)} %get-tuple-element.102.refs_1_), custom_call_target="tpu_custom_call", output_to_operand_aliasing={{}: (2, {})} | custom-call | bytes 5242880 | tf_op jit(solution)/shard_map/place/pallas_call | solution.py:286
  201.8 3.0 %place.5 = f32[512,16384]{1,0:T(8,128)} custom-call(s32[2]{0:T(128)} %get-tuple-element.54.ids_ref, f32[2,512,384]{2,1,0:T(8,128)} %collective-permute-done.26.refs_0_, f32[512,16384]{1,0:T(8,128)} %place.4.refs_1_), custom_call_target="tpu_custom_call", output_to_operand_aliasing={{}: (2, {})} | custom-call | bytes 3145728 | tf_op jit(solution)/shard_map/place/pallas_call | solution.py:286
  (34 shorter events, 1.4 us)
Async XLA Ops:
  0.0 14.9 %collective-permute-start = (f32[384,1024]{1,0:T(8,128)}, f32[384,1024]{1,0:T(8,128)}, u32[]{:S(2)}, u32[]{:S(2)}) collective-permute-start(f32[384,1024]{1,0:T(8,128)} %refs_0_.1), channel_id=1, source_target_pairs={{8,16},{10,18},{12,20},{14,22},{16,8},{18,10},{20,12},{22,14},{9,1... | collective-permute-start | bytes 4718600 | tf_op jit(solution)/shard_map/ppermute | solution.py:326
  1.9 37.5 %collective-permute-start.2 = (f32[384,1024]{1,0:T(8,128)}, f32[384,1024]{1,0:T(8,128)S(1)}, u32[]{:S(2)}, u32[]{:S(2)}) collective-permute-start(f32[384,1024]{1,0:T(8,128)} %refs_0_.1), channel_id=1, source_target_pairs={{0,1},{1,0},{2,3},{3,2},{4,5},{5,4},{6,7},{7,6},{8,9},{9,8},{10,11... | collective-permute-start | bytes 4718600 | tf_op jit(solution)/shard_map/ppermute | solution.py:322
  4.8 36.2 %collective-permute-start.6 = (f32[384,1024]{1,0:T(8,128)}, f32[384,1024]{1,0:T(8,128)}, u32[]{:S(2)}, u32[]{:S(2)}) collective-permute-start(f32[384,1024]{1,0:T(8,128)} %refs_0_.1), channel_id=1, source_target_pairs={{0,4},{2,6},{4,0},{6,2},{8,12},{10,14},{12,8},{14,10},{16,20},{18,... | collective-permute-start | bytes 4718600 | tf_op jit(solution)/shard_map/ppermute | solution.py:323
  6.3 38.2 %collective-permute-start.4 = (f32[384,1024]{1,0:T(8,128)}, f32[384,1024]{1,0:T(8,128)}, u32[]{:S(2)}, u32[]{:S(2)}) collective-permute-start(f32[384,1024]{1,0:T(8,128)} %refs_0_.1), channel_id=1, source_target_pairs={{0,8},{2,10},{4,12},{6,14},{8,0},{10,2},{12,4},{14,6},{16,24},{18,... | collective-permute-start | bytes 4718600 | tf_op jit(solution)/shard_map/ppermute | solution.py:324
  10.8 0.9 copy-start
  11.7 3.2 %collective-permute-start.1 = (f32[384,512]{1,0:T(8,128)S(1)}, f32[384,512]{1,0:T(8,128)S(1)}, u32[]{:S(2)}, u32[]{:S(2)}) collective-permute-start(f32[384,512]{1,0:T(8,128)S(1)} %constant_dynamic-slice_fusion.1.refs_0_), channel_id=1, source_target_pairs={{0,2},{2,0},{4,6},{6,4},{8,10},{10,8},{12,14},{14,12},{16,18},{18,... | collective-permute-start | bytes 2359304 | tf_op jit(solution)/shard_map/ppermute | solution.py:328
  14.9 32.1 %copy-start.2 = (f32[384,512]{1,0:T(8,128)}, f32[384,512]{1,0:T(8,128)S(1)}, u32[]{:S(2)}) copy-start(f32[384,512]{1,0:T(8,128)S(1)} %collective-permute-done.1.refs_2_) | copy-start | bytes 2359300
  39.4 9.4 %copy-start.3 = (f32[384,1024]{1,0:T(8,128)}, f32[384,1024]{1,0:T(8,128)S(1)}, u32[]{:S(2)}) copy-start(f32[384,1024]{1,0:T(8,128)S(1)} %collective-permute-done.2.refs_1_) | copy-start | bytes 4718596
  41.0 35.3 %collective-permute-start.7 = (f32[384,1024]{1,0:T(8,128)}, f32[384,1024]{1,0:T(8,128)}, u32[]{:S(2)}, u32[]{:S(2)}) collective-permute-start(f32[384,1024]{1,0:T(8,128)} %collective-permute-done.6.refs_2_), channel_id=1, source_target_pairs={{0,1},{1,0},{2,3},{3,2},{4,5},{5,4},{6,7},{7,6},{8,9},{9,8},{10,11... | collective-permute-start | bytes 4718600 | tf_op jit(solution)/shard_map/ppermute | solution.py:322
  41.3 36.2 %collective-permute-start.10 = (f32[384,1024]{1,0:T(8,128)}, f32[384,1024]{1,0:T(8,128)}, u32[]{:S(2)}, u32[]{:S(2)}) collective-permute-start(f32[384,1024]{1,0:T(8,128)} %collective-permute-done.refs_1_), channel_id=1, source_target_pairs={{0,8},{2,10},{4,12},{6,14},{8,0},{10,2},{12,4},{14,6},{16,24},{18,... | collective-permute-start | bytes 4718600 | tf_op jit(solution)/shard_map/ppermute | solution.py:324
  44.5 38.5 %collective-permute-start.12 = (f32[384,1024]{1,0:T(8,128)}, f32[384,1024]{1,0:T(8,128)}, u32[]{:S(2)}, u32[]{:S(2)}) collective-permute-start(f32[384,1024]{1,0:T(8,128)} %collective-permute-done.4.refs_0_), channel_id=1, source_target_pairs={{0,4},{2,6},{4,0},{6,2},{8,12},{10,14},{12,8},{14,10},{16,20},{18,... | collective-permute-start | bytes 4718600 | tf_op jit(solution)/shard_map/ppermute | solution.py:323
  46.1 0.9 copy-start.1
  47.0 2.4 %collective-permute-start.3 = (f32[384,512]{1,0:T(8,128)S(1)}, f32[384,512]{1,0:T(8,128)}, u32[]{:S(2)}, u32[]{:S(2)}) collective-permute-start(f32[384,512]{1,0:T(8,128)S(1)} %constant_dynamic-slice_fusion.refs_1_), channel_id=1, source_target_pairs={{0,2},{2,0},{4,6},{6,4},{8,10},{10,8},{12,14},{14,12},{16,18},{18,... | collective-permute-start | bytes 2359304 | tf_op jit(solution)/shard_map/ppermute | solution.py:328
  47.0 52.4 %collective-permute-start.5 = (f32[384,1024]{1,0:T(8,128)}, f32[384,1024]{1,0:T(8,128)}, u32[]{:S(2)}, u32[]{:S(2)}) collective-permute-start(f32[384,1024]{1,0:T(8,128)} %collective-permute-done.4.refs_0_), channel_id=1, source_target_pairs={{8,16},{10,18},{12,20},{14,22},{16,8},{18,10},{20,12},{22,14},{9,1... | collective-permute-start | bytes 4718600 | tf_op jit(solution)/shard_map/ppermute | solution.py:326
  77.5 37.6 %collective-permute-start.13 = (f32[384,1024]{1,0:T(8,128)}, f32[384,1024]{1,0:T(8,128)}, u32[]{:S(2)}, u32[]{:S(2)}) collective-permute-start(f32[384,1024]{1,0:T(8,128)} %collective-permute-done.7.refs_3_), channel_id=1, source_target_pairs={{0,8},{2,10},{4,12},{6,14},{8,0},{10,2},{12,4},{14,6},{16,24},{18,... | collective-permute-start | bytes 4718600 | tf_op jit(solution)/shard_map/ppermute | solution.py:324
  81.5 33.7 %collective-permute-start.11 = (f32[384,1024]{1,0:T(8,128)}, f32[384,1024]{1,0:T(8,128)}, u32[]{:S(2)}, u32[]{:S(2)}) collective-permute-start(f32[384,1024]{1,0:T(8,128)} %choose.2.refs_0_), channel_id=1, source_target_pairs={{0,1},{1,0},{2,3},{3,2},{4,5},{5,4},{6,7},{7,6},{8,9},{9,8},{10,11... | collective-permute-start | bytes 4718600 | tf_op jit(solution)/shard_map/ppermute | solution.py:322
  83.0 34.6 %collective-permute-start.17 = (f32[384,1024]{1,0:T(8,128)}, f32[384,1024]{1,0:T(8,128)}, u32[]{:S(2)}, u32[]{:S(2)}) collective-permute-start(f32[384,1024]{1,0:T(8,128)} %choose.2.refs_0_), channel_id=1, source_target_pairs={{0,4},{2,6},{4,0},{6,2},{8,12},{10,14},{12,8},{14,10},{16,20},{18,... | collective-permute-start | bytes 4718600 | tf_op jit(solution)/shard_map/ppermute | solution.py:323
  99.4 35.1 %collective-permute-start.9 = (f32[2,512,1024]{2,1,0:T(8,128)}, f32[2,512,1024]{2,1,0:T(8,128)}, u32[]{:S(2)}, u32[]{:S(2)}) collective-permute-start(f32[2,512,1024]{2,1,0:T(8,128)} %get-tuple-element.64), channel_id=1, source_target_pairs={{0,2},{2,0},{4,6},{6,4},{8,10},{10,8},{12,14},{14,12},{16,18},{18,... | collective-permute-start | bytes 12582920 | tf_op jit(solution)/shard_map/ppermute | solution.py:328
  99.5 45.8 %collective-permute-start.8 = (f32[384,1024]{1,0:T(8,128)}, f32[384,1024]{1,0:T(8,128)}, u32[]{:S(2)}, u32[]{:S(2)}) collective-permute-start(f32[384,1024]{1,0:T(8,128)} %collective-permute-done.5.refs_1_), channel_id=1, source_target_pairs={{0,8},{2,10},{4,12},{6,14},{8,0},{10,2},{12,4},{14,6},{16,24},{18,... | collective-permute-start | bytes 4718600 | tf_op jit(solution)/shard_map/ppermute | solution.py:324
  117.5 34.5 %collective-permute-start.18 = (f32[384,1024]{1,0:T(8,128)}, f32[384,1024]{1,0:T(8,128)}, u32[]{:S(2)}, u32[]{:S(2)}) collective-permute-start(f32[384,1024]{1,0:T(8,128)} %collective-permute-done.11.refs_1_), channel_id=1, source_target_pairs={{0,4},{2,6},{4,0},{6,2},{8,12},{10,14},{12,8},{14,10},{16,20},{18,... | collective-permute-start | bytes 4718600 | tf_op jit(solution)/shard_map/ppermute | solution.py:323
  119.1 34.5 %collective-permute-start.15 = (f32[384,1024]{1,0:T(8,128)}, f32[384,1024]{1,0:T(8,128)}, u32[]{:S(2)}, u32[]{:S(2)}) collective-permute-start(f32[384,1024]{1,0:T(8,128)} %collective-permute-done.4.refs_0_), channel_id=1, source_target_pairs={{0,1},{1,0},{2,3},{3,2},{4,5},{5,4},{6,7},{7,6},{8,9},{9,8},{10,11... | collective-permute-start | bytes 4718600 | tf_op jit(solution)/shard_map/ppermute | solution.py:322
  119.7 25.6 %collective-permute-start.14 = (f32[384,1024]{1,0:T(8,128)}, f32[384,1024]{1,0:T(8,128)}, u32[]{:S(2)}, u32[]{:S(2)}) collective-permute-start(f32[384,1024]{1,0:T(8,128)} %collective-permute-done.13.refs_3_), channel_id=1, source_target_pairs={{8,16},{10,18},{12,20},{14,22},{16,8},{18,10},{20,12},{22,14},{0,2... | collective-permute-start | bytes 4718600 | tf_op jit(solution)/shard_map/ppermute | solution.py:327
  134.5 40.5 %collective-permute-start.24 = (f32[2,512,1024]{2,1,0:T(8,128)}, f32[2,512,1024]{2,1,0:T(8,128)}, u32[]{:S(2)}, u32[]{:S(2)}) collective-permute-start(f32[2,512,1024]{2,1,0:T(8,128)} %get-tuple-element.92), channel_id=1, source_target_pairs={{0,2},{2,0},{4,6},{6,4},{8,10},{10,8},{12,14},{14,12},{16,18},{18,... | collective-permute-start | bytes 12582920 | tf_op jit(solution)/shard_map/ppermute | solution.py:328
  152.1 18.9 %collective-permute-start.19 = (f32[384,640]{1,0:T(8,128)}, f32[384,640]{1,0:T(8,128)}, u32[]{:S(2)}, u32[]{:S(2)}) collective-permute-start(f32[384,640]{1,0:T(8,128)} %get-tuple-element.80.refs_0_), channel_id=1, source_target_pairs={{0,4},{2,6},{4,0},{6,2},{8,12},{10,14},{12,8},{14,10},{16,20},{18,... | collective-permute-start | bytes 2949128 | tf_op jit(solution)/shard_map/ppermute | solution.py:323
  153.6 17.4 %collective-permute-start.16 = (f32[384,640]{1,0:T(8,128)}, f32[384,640]{1,0:T(8,128)}, u32[]{:S(2)}, u32[]{:S(2)}) collective-permute-start(f32[384,640]{1,0:T(8,128)} %get-tuple-element.80.refs_0_), channel_id=1, source_target_pairs={{0,1},{1,0},{2,3},{3,2},{4,5},{5,4},{6,7},{7,6},{8,9},{9,8},{10,11... | collective-permute-start | bytes 2949128 | tf_op jit(solution)/shard_map/ppermute | solution.py:322
  153.6 17.4 %collective-permute-start.20 = (f32[384,640]{1,0:T(8,128)}, f32[384,640]{1,0:T(8,128)}, u32[]{:S(2)}, u32[]{:S(2)}) collective-permute-start(f32[384,640]{1,0:T(8,128)} %get-tuple-element.81.refs_4_), channel_id=1, source_target_pairs={{0,8},{2,10},{4,12},{6,14},{8,0},{10,2},{12,4},{14,6},{16,24},{18,... | collective-permute-start | bytes 2949128 | tf_op jit(solution)/shard_map/ppermute | solution.py:324
  170.6 17.5 %collective-permute-start.25 = (f32[2,512,1024]{2,1,0:T(8,128)}, f32[2,512,1024]{2,1,0:T(8,128)}, u32[]{:S(2)}, u32[]{:S(2)}) collective-permute-start(f32[2,512,1024]{2,1,0:T(8,128)} %get-tuple-element.98), channel_id=1, source_target_pairs={{0,2},{2,0},{4,6},{6,4},{8,10},{10,8},{12,14},{14,12},{16,18},{18,... | collective-permute-start | bytes 12582920 | tf_op jit(solution)/shard_map/ppermute | solution.py:328
  171.0 16.5 %collective-permute-start.23 = (f32[384,384]{1,0:T(8,128)}, f32[384,384]{1,0:T(8,128)}, u32[]{:S(2)}, u32[]{:S(2)}) collective-permute-start(f32[384,384]{1,0:T(8,128)} %get-tuple-element.90.refs_4_), channel_id=1, source_target_pairs={{0,8},{2,10},{4,12},{6,14},{8,0},{10,2},{12,4},{14,6},{16,24},{18,... | collective-permute-start | bytes 1769480 | tf_op jit(solution)/shard_map/ppermute | solution.py:324
  172.6 14.9 %collective-permute-start.22 = (f32[384,384]{1,0:T(8,128)}, f32[384,384]{1,0:T(8,128)}, u32[]{:S(2)}, u32[]{:S(2)}) collective-permute-start(f32[384,384]{1,0:T(8,128)} %get-tuple-element.87.refs_0_), channel_id=1, source_target_pairs={{0,4},{2,6},{4,0},{6,2},{8,12},{10,14},{12,8},{14,10},{16,20},{18,... | collective-permute-start | bytes 1769480 | tf_op jit(solution)/shard_map/ppermute | solution.py:323
  174.1 13.9 %collective-permute-start.21 = (f32[384,384]{1,0:T(8,128)}, f32[384,384]{1,0:T(8,128)}, u32[]{:S(2)}, u32[]{:S(2)}) collective-permute-start(f32[384,384]{1,0:T(8,128)} %get-tuple-element.87.refs_0_), channel_id=1, source_target_pairs={{0,1},{1,0},{2,3},{3,2},{4,5},{5,4},{6,7},{7,6},{8,9},{9,8},{10,11... | collective-permute-start | bytes 1769480 | tf_op jit(solution)/shard_map/ppermute | solution.py:322
  188.1 10.2 %collective-permute-start.27 = (f32[2,512,640]{2,1,0:T(8,128)}, f32[2,512,640]{2,1,0:T(8,128)}, u32[]{:S(2)}, u32[]{:S(2)}) collective-permute-start(f32[2,512,640]{2,1,0:T(8,128)} %get-tuple-element.101), channel_id=1, source_target_pairs={{0,2},{2,0},{4,6},{6,4},{8,10},{10,8},{12,14},{14,12},{16,18},{18,... | collective-permute-start | bytes 7864328 | tf_op jit(solution)/shard_map/ppermute | solution.py:328
  197.7 4.1 %collective-permute-start.26 = (f32[2,512,384]{2,1,0:T(8,128)}, f32[2,512,384]{2,1,0:T(8,128)}, u32[]{:S(2)}, u32[]{:S(2)}) collective-permute-start(f32[2,512,384]{2,1,0:T(8,128)} %get-tuple-element.100), channel_id=1, source_target_pairs={{0,2},{2,0},{4,6},{6,4},{8,10},{10,8},{12,14},{14,12},{16,18},{18,... | collective-permute-start | bytes 4718600 | tf_op jit(solution)/shard_map/ppermute | solution.py:328
